TPU v7x, 512 devices: a whole 4x4x16 slice. The times are simulated.
512 devices in a mesh: node: 8 (over x, core), dev: 64 (over z, y).
Axes of the slice: x: 4, y: 4, z: 16, core: 2. Of those that a mesh axis runs over, the one named last changes fastest.
Arguments:
- element_load: float32 [16, 64, 8, 8, 8, 128], P('node', 'dev'), may hold values from -22 to 22
- orient: int32 [16, 64, 128], P('node', 'dev'), may hold values from 0 to 7
- size_x: float32 [16], P('node'), may hold values from 0.5 to 2
- size_y: float32 [64], P('dev'), may hold values from 0.5 to 2
- size_z: float32 [128], replicated, may hold values from 0.5 to 2
Outputs:
- solution: float32 [16, 64, 8, 8, 8, 128], P('node', 'dev')
- residual: float32 [16, 64, 8, 8, 8, 128], P('node', 'dev')
All inputs are finite; a program needn't handle non-finite values.
Results may differ from a plain program's by a relative error of at most 0.019.
Values sent between devices are 32-bit elements; how exact they have to be, the bound alone decides.
No kernel may reach another device: no remote copies, remote signals or barrier semaphores. Data moves between devices by JAX's collectives and lax.ppermute only.
A program may use at most 64 MiB of HBM per device.

v0:
```python
import math

import jax
import jax.numpy as jnp
from jax import lax
from jax.sharding import PartitionSpec as P

ITERS = 2


precise = lax.Precision.HIGHEST


def passed_along(x, axis, by):
    peers = lax.axis_size(axis)
    pairs = [(i, i + by) for i in range(peers) if 0 <= i + by < peers]
    return lax.ppermute(x, axis, pairs)


def legendre_pair(value):
    prev_val = 1.0
    curr_val = value
    prev_der = 0.0
    curr_der = 1.0
    for order in range(2, 8):
        next_val = ((2 * order - 1) * value * curr_val - (order - 1) * prev_val) / order
        next_der = prev_der + (2 * order - 1) * curr_val
        prev_val, curr_val = (curr_val, next_val)
        prev_der, curr_der = (curr_der, next_der)
    return (curr_val, curr_der)


def second_derivative(value):
    leg_val, leg_der = legendre_pair(value)
    return (2.0 * value * leg_der - 56.0 * leg_val) / (1.0 - value * value)


def basis_tables():
    guesses = [
        -0.8717401485096066,
        -0.5917001814331423,
        -0.2092992179024789,
        0.2092992179024789,
        0.5917001814331423,
        0.8717401485096066,
    ]
    inner_pts = []
    for guess in guesses:
        point = guess
        for newton in range(4):
            point = point - legendre_pair(point)[1] / second_derivative(point)
        inner_pts.append(point)
    gll_points = [-1.0] + inner_pts + [1.0]
    leg_values = [legendre_pair(point)[0] for point in gll_points]
    weights = [2.0 / (56.0 * lv * lv) for lv in leg_values]
    derivative = [[0.0] * 8 for row_at in range(8)]
    for row_at in range(8):
        for col_at in range(8):
            if row_at != col_at:
                derivative[row_at][col_at] = leg_values[row_at] / (
                    leg_values[col_at] * (gll_points[row_at] - gll_points[col_at])
                )
    derivative[0][0] = -14.0
    derivative[7][7] = 14.0
    stiffness = [
        [
            sum(
                (
                    derivative[mid][row_at] * weights[mid] * derivative[mid][col_at]
                    for mid in range(8)
                )
            )
            for col_at in range(8)
        ]
        for row_at in range(8)
    ]
    inv_sqrt = [1.0 / math.sqrt(wt) for wt in weights]
    matrix = [
        [inv_sqrt[row_at] * stiffness[row_at][col_at] * inv_sqrt[col_at] for col_at in range(8)]
        for row_at in range(8)
    ]
    vectors = [[1.0 if row_at == col_at else 0.0 for col_at in range(8)] for row_at in range(8)]
    for sweep in range(14):
        for first in range(8):
            for second in range(first + 1, 8):
                angle = 0.5 * math.atan2(
                    2.0 * matrix[first][second], matrix[second][second] - matrix[first][first]
                )
                cosine = math.cos(angle)
                sine = math.sin(angle)
                for other in range(8):
                    left_val = matrix[other][first]
                    right_val = matrix[other][second]
                    matrix[other][first] = cosine * left_val - sine * right_val
                    matrix[other][second] = sine * left_val + cosine * right_val
                for other in range(8):
                    left_val = matrix[first][other]
                    right_val = matrix[second][other]
                    matrix[first][other] = cosine * left_val - sine * right_val
                    matrix[second][other] = sine * left_val + cosine * right_val
                for other in range(8):
                    left_val = vectors[other][first]
                    right_val = vectors[other][second]
                    vectors[other][first] = cosine * left_val - sine * right_val
                    vectors[other][second] = sine * left_val + cosine * right_val
    eigen_vals = [max(matrix[idx_at][idx_at], 0.0) for idx_at in range(8)]
    eigen_modes = [
        [inv_sqrt[row_at] * vectors[row_at][col_at] for col_at in range(8)] for row_at in range(8)
    ]
    return (
        jnp.asarray(weights, jnp.float32),
        jnp.asarray(stiffness, jnp.float32),
        jnp.asarray(eigen_modes, jnp.float32),
        jnp.asarray(eigen_vals, jnp.float32),
    )


def on_points(cube):
    return cube[None, None, :, :, :, None]


def flip_frame(field_in, orient):
    for bit_at in range(3):
        flipped = (orient // 2**bit_at % 2 == 1)[:, :, None, None, None, :]
        field_in = jnp.where(flipped, jnp.flip(field_in, axis=2 + bit_at), field_in)
    return field_in


def face_weights(global_index, total_count):
    lower_face = jnp.where(global_index == 0, 0.0, 0.5).astype(jnp.float32)
    upper_face = jnp.where(global_index == total_count - 1, 0.0, 0.5).astype(jnp.float32)
    middle = jnp.ones((6, global_index.shape[0]), jnp.float32)
    return jnp.concatenate([lower_face[None], middle, upper_face[None]], axis=0)


def point_weights(weight_x, weight_y, weight_z):
    return (
        weight_x.T[:, None, :, None, None, None]
        * weight_y.T[None, :, None, :, None, None]
        * weight_z[None, None, None, None, :, :]
    )


def coefficients(size_x, size_y, size_z, eigen_vals):
    coef_x = (size_y[None, :, None] * size_z[None, None, :] / (2.0 * size_x[:, None, None]))[
        :, :, None, None, None, :
    ]
    coef_y = (size_x[:, None, None] * size_z[None, None, :] / (2.0 * size_y[None, :, None]))[
        :, :, None, None, None, :
    ]
    coef_z = (size_x[:, None, None] * size_y[None, :, None] / (2.0 * size_z[None, None, :]))[
        :, :, None, None, None, :
    ]
    denominator = (
        on_points(eigen_vals[:, None, None]) * coef_x
        + on_points(eigen_vals[None, :, None]) * coef_y
        + on_points(eigen_vals[None, None, :]) * coef_z
        + (coef_x + coef_y + coef_z) / 3.0
    )
    return (coef_x, coef_y, coef_z, denominator)


def along(matrix, field_in, axis_at):
    einsum_forms = ["ai,xyijkz->xyajkz", "aj,xyijkz->xyiakz", "ak,xyijkz->xyijaz"]
    return jnp.einsum(einsum_forms[axis_at], matrix, field_in, precision=precise)


def laplace(field_in, tables, coefs):
    weights, stiffness = (tables[0], tables[1])
    w_first = weights[:, None, None]
    w_second = weights[None, :, None]
    w_third = weights[None, None, :]
    term_x = along(stiffness, field_in, 0) * on_points(w_second * w_third) * coefs[0]
    term_y = along(stiffness, field_in, 1) * on_points(w_first * w_third) * coefs[1]
    term_z = along(stiffness, field_in, 2) * on_points(w_first * w_second) * coefs[2]
    return term_x + term_y + term_z


def element_solve(field_in, tables, coefs):
    eigen_modes = tables[2]
    spectral = along(eigen_modes.T, along(eigen_modes.T, along(eigen_modes.T, field_in, 0), 1), 2)
    spectral = spectral / coefs[3]
    return along(eigen_modes, along(eigen_modes, along(eigen_modes, spectral, 0), 1), 2)


def face_pair(field_in, dim_at):
    point_dim = 2 + dim_at
    lower_face = lax.index_in_dim(field_in, 0, point_dim, keepdims=False)
    upper_face = lax.index_in_dim(field_in, 7, point_dim, keepdims=False)
    return (lower_face, upper_face)


def assemble(field_in, dim_at, lower_face, upper_face, from_next, from_prev):
    point_dim = 2 + dim_at
    elem_dim = [0, 1, 4][dim_at]
    elements = lower_face.shape[elem_dim]
    after_face = jnp.concatenate(
        [lax.slice_in_dim(lower_face, 1, elements, axis=elem_dim), from_next], axis=elem_dim
    )
    before = jnp.concatenate(
        [from_prev, lax.slice_in_dim(upper_face, 0, elements - 1, axis=elem_dim)], axis=elem_dim
    )
    middle = lax.slice_in_dim(field_in, 1, 7, axis=point_dim)
    return jnp.concatenate(
        [
            jnp.expand_dims(lower_face + before, point_dim),
            middle,
            jnp.expand_dims(upper_face + after_face, point_dim),
        ],
        axis=point_dim,
    )


def remote_x(lower_face, upper_face):
    elements = lower_face.shape[0]
    from_next = passed_along(lax.slice_in_dim(lower_face, 0, 1, axis=0), "node", -1)
    from_prev = passed_along(
        lax.slice_in_dim(upper_face, elements - 1, elements, axis=0), "node", 1
    )
    return (from_next, from_prev)


def remote_y(lower_face, upper_face):
    from_next = passed_along(lower_face, "dev", -1)
    from_prev = passed_along(upper_face, "dev", 1)
    return (from_next, from_prev)


def summed(field_in):
    lower_face, upper_face = face_pair(field_in, 0)
    from_next, from_prev = remote_x(lower_face, upper_face)
    field_in = assemble(field_in, 0, lower_face, upper_face, from_next, from_prev)
    lower_face, upper_face = face_pair(field_in, 1)
    from_next, from_prev = remote_y(lower_face, upper_face)
    field_in = assemble(field_in, 1, lower_face, upper_face, from_next, from_prev)
    lower_face, upper_face = face_pair(field_in, 2)
    zero_slab = jnp.zeros_like(lax.slice_in_dim(lower_face, 0, 1, axis=4))
    return assemble(field_in, 2, lower_face, upper_face, zero_slab, zero_slab)


def shards(element_load, orient, size_x, size_y, size_z):
    tables = basis_tables()
    count_x = element_load.shape[0]
    count_y = element_load.shape[1]
    count_z = element_load.shape[5]
    index_x = lax.axis_index("node") * count_x + jnp.arange(count_x, dtype=jnp.int32)
    index_y = lax.axis_index("dev") * count_y + jnp.arange(count_y, dtype=jnp.int32)
    weight = point_weights(
        face_weights(index_x, count_x * lax.axis_size("node")),
        face_weights(index_y, count_y * lax.axis_size("dev")),
        face_weights(jnp.arange(count_z, dtype=jnp.int32), count_z),
    )
    interior = (weight > 0.0).astype(jnp.float32)
    coefs = coefficients(size_x, size_y, size_z, tables[3])

    def precondition(field_in):
        return interior * summed(element_solve(field_in, tables, coefs))

    right_side = interior * summed(flip_frame(element_load, orient))
    solution = jnp.zeros_like(right_side)
    residual = right_side

    def residual_dot(left_field, right_field):
        return lax.psum(jnp.sum(left_field * right_field * weight), ("node", "dev"))

    precond = precondition(residual)
    direction = precond
    energy_old = residual_dot(residual, precond)
    for step_at in range(ITERS):
        applied = interior * summed(laplace(direction, tables, coefs))
        step_len = energy_old / lax.psum(jnp.sum(direction * applied * weight), ("node", "dev"))
        solution = solution + step_len * direction
        residual = residual - step_len * applied
        if step_at + 1 < ITERS:
            precond = precondition(residual)
            energy_new = residual_dot(residual, precond)
            direction = precond + energy_new / energy_old * direction
            energy_old = energy_new
    return (flip_frame(solution, orient), flip_frame(residual, orient))


def solution(mesh):
    return jax.shard_map(
        shards,
        mesh=mesh,
        in_specs=(
            P("node", "dev", None, None, None, None),
            P("node", "dev", None),
            P("node"),
            P("dev"),
            P(),
        ),
        out_specs=(
            P("node", "dev", None, None, None, None),
            P("node", "dev", None, None, None, None),
        ),
        check_vma=False,
    )
```

profile of v0, /device:TPU:1, one launch (start us, length us, event | category | flops | bytes accessed | tf_op | source)
XLA Modules:
  0.0 467.4 jit_solution(14430508268519169876)
XLA Ops:
  0.6 1.1 copy.13
  2.8 4.5 collective-permute-start
  7.3 5.6 %collective-permute-start.1 = (f32[1,1,8,8,128]{4,2,3,1,0:T(8,128)S(1)}, f32[1,1,8,8,128]{4,2,3,1,0:T(8,128)S(1)}, u32[]{:S(2)}, u32[]{:S(2)}) collective-permute-start(f32[1,1,8,8,128]{4,2,3,1,0:T(8,128)S(1)} %get-tuple-element.67), channel_id=1, source_target_pairs={{64,0},{128,64},{192,128},{256,192},{320,256},{384,320},{448,384},... | collective-permute-start | bytes 98312 | tf_op jit(solution)/shard_map/ppermute | solution.py:17
  13.9 0.7 copy-done.26
  14.5 0.7 copy-done.27
  15.3 0.6 copy-done.31
  16.2 1.3 collective-permute-start.3
  17.5 4.0 collective-permute-start.2
  21.9 1.4 collective-permute-done.2
  24.6 0.9 convolution_bitcast_fusion.10
  25.5 0.9 convolution_bitcast_fusion.9
  26.4 0.6 fusion.1
  27.1 0.9 convolution_bitcast_fusion.7
  28.0 0.9 convolution_bitcast_fusion.6
  29.5 2.4 collective-permute-start.5
  32.0 3.1 collective-permute-start.4
  35.1 1.0 collective-permute-done.4
  36.1 4.1 collective-permute-start.6
  40.3 1.5 collective-permute-done.6
  41.8 1.3 collective-permute-start.7
  43.1 4.6 collective-permute-done.7
  50.1 0.9 fusion.30
  51.7 5.4 %collective-permute-start.8 = (f32[1,1,8,8,128]{4,3,2,1,0:T(8,128)S(1)}, f32[1,1,8,8,128]{4,3,2,1,0:T(8,128)S(1)}, u32[]{:S(2)}, u32[]{:S(2)}) collective-permute-start(f32[1,1,8,8,128]{4,3,2,1,0:T(8,128)S(1)} %get-tuple-element.48), channel_id=1, source_target_pairs={{0,64},{64,128},{128,192},{192,256},{256,320},{320,384},{384,448},... | collective-permute-start | bytes 98312 | tf_op jit(solution)/shard_map/ppermute | solution.py:17
  57.2 1.9 collective-permute-start.9
  59.3 3.1 collective-permute-done.9
  62.4 3.6 collective-permute-start.10
  66.5 0.9 collective-permute-done.10
  67.4 1.5 collective-permute-start.11
  69.0 3.8 collective-permute-done.11
  72.9 0.9 slice_bitcast_fusion.16
  74.0 1.7 multiply_reduce_fusion.2
  75.8 120.0 %all-reduce.10 = (f32[]{:T(128)}, f32[]{:T(128)}) all-reduce(f32[]{:T(128)} %get-tuple-element.5, f32[]{:T(128)} %get-tuple-element.4), channel_id=1, replica_groups=mesh['node'=8,'dev'=64] {'node','dev'}, use_global_device_ids=true, to_apply=%region_1.2 | all-reduce | flops 2 | bytes 16 | tf_op jit(solution)/shard_map/psum | solution.py:264
  197.1 1.5 fusion.14
  198.6 0.9 convolution_bitcast_fusion.5
  199.5 0.9 convolution_bitcast_fusion.4
  200.4 0.6 fusion.3
  201.1 0.9 convolution_bitcast_fusion.2
  201.9 0.9 convolution_bitcast_fusion.1
  202.8 0.6 convolution_bitcast_fusion
  203.5 2.9 collective-permute-start.12
  206.4 1.9 collective-permute-start.13
  208.7 2.9 collective-permute-done.13
  211.8 1.4 collective-permute-start.14
  213.7 0.8 collective-permute-done.14
  214.5 1.3 collective-permute-start.15
  216.2 4.0 collective-permute-done.15
  220.4 0.7 fusion.46
  221.4 0.9 copy-done.1
  222.2 0.9 multiply_reduce_fusion.1
  223.1 0.9 fusion.85
  224.0 106.6 %psum.30 = f32[]{:T(128)} all-reduce(f32[]{:T(128)} %multiply_reduce_fusion.1), channel_id=1, replica_groups=mesh['node'=8,'dev'=64] {'node','dev'}, use_global_device_ids=true, to_apply=%region_5.6 | all-reduce | flops 1 | bytes 8 | tf_op jit(solution)/shard_map/psum | solution.py:264
  332.0 1.0 pad_maximum_fusion
  334.9 0.9 fusion.19
  337.2 2.5 collective-permute-start.16
  339.7 1.9 collective-permute-start.17
  342.0 2.9 collective-permute-done.17
  345.1 1.8 collective-permute-start.18
  346.9 1.3 broadcast_multiply_fusion
  348.2 1.3 collective-permute-start.19
  349.9 3.7 collective-permute-done.19
  353.9 0.9 multiply_reduce_fusion
  354.8 106.2 %psum.31 = f32[]{:T(128)} all-reduce(f32[]{:T(128)} %multiply_reduce_fusion), channel_id=1, replica_groups=mesh['node'=8,'dev'=64] {'node','dev'}, use_global_device_ids=true, to_apply=%region_7.8 | all-reduce | flops 1 | bytes 8 | tf_op jit(solution)/shard_map/psum | solution.py:271
  465.2 1.1 copy.101
  466.3 1.1 copy.102
  (180 shorter events, 16.8 us)
Async XLA Ops:
  0.6 1.2 copy-start.30
  1.9 0.5 copy-start.19
  2.0 0.6 copy-start.23
  2.0 0.7 copy-start.21
  2.8 13.3 %collective-permute-start = (f32[1,1,8,8,128]{4,2,3,1,0:T(8,128)S(1)}, f32[1,1,8,8,128]{4,2,3,1,0:T(8,128)S(1)}, u32[]{:S(2)}, u32[]{:S(2)}) collective-permute-start(f32[1,1,8,8,128]{4,2,3,1,0:T(8,128)S(1)} %get-tuple-element.66), channel_id=1, source_target_pairs={{0,64},{64,128},{128,192},{192,256},{256,320},{320,384},{384,448},... | collective-permute-start | bytes 98312 | tf_op jit(solution)/shard_map/ppermute | solution.py:17
  7.3 8.8 %collective-permute-start.1 = (f32[1,1,8,8,128]{4,2,3,1,0:T(8,128)S(1)}, f32[1,1,8,8,128]{4,2,3,1,0:T(8,128)S(1)}, u32[]{:S(2)}, u32[]{:S(2)}) collective-permute-start(f32[1,1,8,8,128]{4,2,3,1,0:T(8,128)S(1)} %get-tuple-element.67), channel_id=1, source_target_pairs={{64,0},{128,64},{192,128},{256,192},{320,256},{384,320},{448,384},... | collective-permute-start | bytes 98312 | tf_op jit(solution)/shard_map/ppermute | solution.py:17
  13.9 0.7 copy-start.26
  14.5 0.7 copy-start.27
  15.3 11.1 %copy-start.28 = (f32[2,128]{1,0:T(2,128)}, f32[2,128]{1,0:T(2,128)S(1)}, u32[]{:S(2)}) copy-start(f32[2,128]{1,0:T(2,128)S(1)} %get-tuple-element.20) | copy-start | bytes 3076
  15.3 36.0 %copy-start.11 = (f32[2,128]{1,0:T(2,128)}, f32[2,128]{1,0:T(2,128)S(1)}, u32[]{:S(2)}) copy-start(f32[2,128]{1,0:T(2,128)S(1)} %get-tuple-element.21) | copy-start | bytes 3076
  15.3 36.0 %copy-start.13 = (f32[2,128]{1,0:T(2,128)}, f32[2,128]{1,0:T(2,128)S(1)}, u32[]{:S(2)}) copy-start(f32[2,128]{1,0:T(2,128)S(1)} %get-tuple-element.78) | copy-start | bytes 3076
  15.3 36.0 %copy-start.15 = (f32[2,128]{1,0:T(2,128)}, f32[2,128]{1,0:T(2,128)S(1)}, u32[]{:S(2)}) copy-start(f32[2,128]{1,0:T(2,128)S(1)} %get-tuple-element.79) | copy-start | bytes 3076
  15.3 0.7 copy-start.31
  16.0 10.4 %copy-start.17 = (f32[2,8,128]{2,1,0:T(8,128)}, f32[2,8,128]{2,1,0:T(8,128)S(1)}, u32[]{:S(2)}) copy-start(f32[2,8,128]{2,1,0:T(8,128)S(1)} %get-tuple-element.89) | copy-start | bytes 24580
  16.0 10.4 %copy-start.9 = (f32[2,8,8,128]{3,2,1,0:T(8,128)}, f32[2,8,8,128]{3,2,1,0:T(8,128)S(1)}, u32[]{:S(2)}) copy-start(f32[2,8,8,128]{3,2,1,0:T(8,128)S(1)} %broadcast_add_fusion) | copy-start | bytes 196612
  16.2 5.7 %collective-permute-start.3 = (f32[2,1,8,8,128]{4,2,0,3,1:T(8,128)S(1)}, f32[2,1,8,8,128]{4,2,0,3,1:T(8,128)S(1)}, u32[]{:S(2)}, u32[]{:S(2)}) collective-permute-start(f32[2,1,8,8,128]{4,2,0,3,1:T(8,128)S(1)} %bitcast.403), channel_id=1, source_target_pairs={{1,0},{2,1},{3,2},{4,3},{5,4},{6,5},{7,6},{8,7},{9,8},{10,9},{11,1... | collective-permute-start | bytes 196616 | tf_op jit(solution)/shard_map/ppermute | solution.py:17
  17.5 5.8 %collective-permute-start.2 = (f32[2,1,8,8,128]{4,2,0,3,1:T(8,128)S(1)}, f32[2,1,8,8,128]{4,2,0,3,1:T(8,128)S(1)}, u32[]{:S(2)}, u32[]{:S(2)}) collective-permute-start(f32[2,1,8,8,128]{4,2,0,3,1:T(8,128)S(1)} %bitcast.405), channel_id=1, source_target_pairs={{0,1},{1,2},{2,3},{3,4},{4,5},{5,6},{6,7},{7,8},{8,9},{9,10},{10,1... | collective-permute-start | bytes 196616 | tf_op jit(solution)/shard_map/ppermute | solution.py:17
  24.0 0.7 copy-start.3
  29.5 5.6 %collective-permute-start.5 = (f32[1,1,8,8,128]{4,3,2,1,0:T(8,128)S(1)}, f32[1,1,8,8,128]{4,3,2,1,0:T(8,128)S(1)}, u32[]{:S(2)}, u32[]{:S(2)}) collective-permute-start(f32[1,1,8,8,128]{4,3,2,1,0:T(8,128)S(1)} %get-tuple-element.57), channel_id=1, source_target_pairs={{64,0},{128,64},{192,128},{256,192},{320,256},{384,320},{448,384},... | collective-permute-start | bytes 98312 | tf_op jit(solution)/shard_map/ppermute | solution.py:17
  32.0 4.1 collective-permute-start.4
  36.1 5.6 %collective-permute-start.6 = (f32[2,1,8,8,128]{4,3,2,0,1:T(8,128)S(1)}, f32[2,1,8,8,128]{4,3,2,0,1:T(8,128)S(1)}, u32[]{:S(2)}, u32[]{:S(2)}) collective-permute-start(f32[2,1,8,8,128]{4,3,2,0,1:T(8,128)S(1)} %maximum_bitcast_fusion.10), channel_id=1, source_target_pairs={{0,1},{1,2},{2,3},{3,4},{4,5},{5,6},{6,7},{7,8},{8,9},{9,10},{10,1... | collective-permute-start | bytes 196616 | tf_op jit(solution)/shard_map/ppermute | solution.py:17
  41.7 1.3 copy-start.25
  41.8 6.0 %collective-permute-start.7 = (f32[2,1,8,8,128]{4,3,2,0,1:T(8,128)S(1)}, f32[2,1,8,8,128]{4,3,2,0,1:T(8,128)S(1)}, u32[]{:S(2)}, u32[]{:S(2)}) collective-permute-start(f32[2,1,8,8,128]{4,3,2,0,1:T(8,128)S(1)} %get-tuple-element.19), channel_id=1, source_target_pairs={{1,0},{2,1},{3,2},{4,3},{5,4},{6,5},{7,6},{8,7},{9,8},{10,9},{11,1... | collective-permute-start | bytes 196616 | tf_op jit(solution)/shard_map/ppermute | solution.py:17
  43.1 8.2 %copy-start.7 = (f32[8,8]{1,0:T(8,128)}, f32[8,8]{1,0:T(8,128)S(1)}, u32[]{:S(2)}) copy-start(f32[8,8]{1,0:T(8,128)S(1)} %broadcast_multiply_fusion.8) | copy-start | bytes 772
  48.2 0.7 copy-start.5
  51.7 7.5 %collective-permute-start.8 = (f32[1,1,8,8,128]{4,3,2,1,0:T(8,128)S(1)}, f32[1,1,8,8,128]{4,3,2,1,0:T(8,128)S(1)}, u32[]{:S(2)}, u32[]{:S(2)}) collective-permute-start(f32[1,1,8,8,128]{4,3,2,1,0:T(8,128)S(1)} %get-tuple-element.48), channel_id=1, source_target_pairs={{0,64},{64,128},{128,192},{192,256},{256,320},{320,384},{384,448},... | collective-permute-start | bytes 98312 | tf_op jit(solution)/shard_map/ppermute | solution.py:17
  57.2 5.2 %collective-permute-start.9 = (f32[1,1,8,8,128]{4,3,2,1,0:T(8,128)S(1)}, f32[1,1,8,8,128]{4,3,2,1,0:T(8,128)S(1)}, u32[]{:S(2)}, u32[]{:S(2)}) collective-permute-start(f32[1,1,8,8,128]{4,3,2,1,0:T(8,128)S(1)} %get-tuple-element.49), channel_id=1, source_target_pairs={{64,0},{128,64},{192,128},{256,192},{320,256},{384,320},{448,384},... | collective-permute-start | bytes 98312 | tf_op jit(solution)/shard_map/ppermute | solution.py:17
  62.4 5.0 %collective-permute-start.10 = (f32[2,1,8,8,128]{4,3,2,0,1:T(8,128)S(1)}, f32[2,1,8,8,128]{4,3,2,0,1:T(8,128)S(1)}, u32[]{:S(2)}, u32[]{:S(2)}) collective-permute-start(f32[2,1,8,8,128]{4,3,2,0,1:T(8,128)S(1)} %maximum_bitcast_fusion.8), channel_id=1, source_target_pairs={{0,1},{1,2},{2,3},{3,4},{4,5},{5,6},{6,7},{7,8},{8,9},{9,10},{10,1... | collective-permute-start | bytes 196616 | tf_op jit(solution)/shard_map/ppermute | solution.py:17
  66.4 2.4 copy-start
  67.4 5.3 %collective-permute-start.11 = (f32[2,1,8,8,128]{4,3,2,0,1:T(8,128)S(1)}, f32[2,1,8,8,128]{4,3,2,0,1:T(8,128)S(1)}, u32[]{:S(2)}, u32[]{:S(2)}) collective-permute-start(f32[2,1,8,8,128]{4,3,2,0,1:T(8,128)S(1)} %get-tuple-element.17), channel_id=1, source_target_pairs={{1,0},{2,1},{3,2},{4,3},{5,4},{6,5},{7,6},{8,7},{9,8},{10,9},{11,1... | collective-permute-start | bytes 196616 | tf_op jit(solution)/shard_map/ppermute | solution.py:17
  199.5 0.9 copy-start.10
  199.5 0.9 copy-start.18
  199.5 0.9 copy-start.29
  203.5 5.1 %collective-permute-start.12 = (f32[1,1,8,8,128]{4,3,2,1,0:T(8,128)S(1)}, f32[1,1,8,8,128]{4,3,2,1,0:T(8,128)S(1)}, u32[]{:S(2)}, u32[]{:S(2)}) collective-permute-start(f32[1,1,8,8,128]{4,3,2,1,0:T(8,128)S(1)} %get-tuple-element.34), channel_id=1, source_target_pairs={{0,64},{64,128},{128,192},{192,256},{256,320},{320,384},{384,448},... | collective-permute-start | bytes 98312 | tf_op jit(solution)/shard_map/ppermute | solution.py:17
  206.4 5.2 %collective-permute-start.13 = (f32[1,1,8,8,128]{4,3,2,1,0:T(8,128)S(1)}, f32[1,1,8,8,128]{4,3,2,1,0:T(8,128)S(1)}, u32[]{:S(2)}, u32[]{:S(2)}) collective-permute-start(f32[1,1,8,8,128]{4,3,2,1,0:T(8,128)S(1)} %get-tuple-element.35), channel_id=1, source_target_pairs={{64,0},{128,64},{192,128},{256,192},{320,256},{384,320},{448,384},... | collective-permute-start | bytes 98312 | tf_op jit(solution)/shard_map/ppermute | solution.py:17
  211.8 2.7 collective-permute-start.14
  214.5 5.7 %collective-permute-start.15 = (f32[2,1,8,8,128]{4,2,0,3,1:T(8,128)S(1)}, f32[2,1,8,8,128]{4,2,0,3,1:T(8,128)S(1)}, u32[]{:S(2)}, u32[]{:S(2)}) collective-permute-start(f32[2,1,8,8,128]{4,2,0,3,1:T(8,128)S(1)} %get-tuple-element.15), channel_id=1, source_target_pairs={{1,0},{2,1},{3,2},{4,3},{5,4},{6,5},{7,6},{8,7},{9,8},{10,9},{11,1... | collective-permute-start | bytes 196616 | tf_op jit(solution)/shard_map/ppermute | solution.py:17
  221.3 0.9 copy-start.1
  223.1 108.9 %copy-start.4 = (f32[2,8,8,1,128]{4,2,1,0,3:T(8,128)S(1)}, f32[2,8,8,1,128]{4,2,1,0,3:T(8,128)}, u32[]{:S(2)}) copy-start(f32[2,8,8,1,128]{4,2,1,0,3:T(8,128)} %get-tuple-element.12) | copy-start | bytes 196612
  333.0 0.7 copy-start.6
  334.9 0.9 copy-start.8
  335.8 0.7 copy-start.14
  335.8 0.7 copy-start.16
  336.1 0.6 copy-start.12
  337.2 4.7 %collective-permute-start.16 = (f32[1,1,8,8,128]{4,3,2,1,0:T(8,128)S(1)}, f32[1,1,8,8,128]{4,3,2,1,0:T(8,128)S(1)}, u32[]{:S(2)}, u32[]{:S(2)}) collective-permute-start(f32[1,1,8,8,128]{4,3,2,1,0:T(8,128)S(1)} %get-tuple-element.28), channel_id=1, source_target_pairs={{0,64},{64,128},{128,192},{192,256},{256,320},{320,384},{384,448},... | collective-permute-start | bytes 98312 | tf_op jit(solution)/shard_map/ppermute | solution.py:17
  339.7 5.2 %collective-permute-start.17 = (f32[1,1,8,8,128]{4,3,2,1,0:T(8,128)S(1)}, f32[1,1,8,8,128]{4,3,2,1,0:T(8,128)S(1)}, u32[]{:S(2)}, u32[]{:S(2)}) collective-permute-start(f32[1,1,8,8,128]{4,3,2,1,0:T(8,128)S(1)} %get-tuple-element.29), channel_id=1, source_target_pairs={{64,0},{128,64},{192,128},{256,192},{320,256},{384,320},{448,384},... | collective-permute-start | bytes 98312 | tf_op jit(solution)/shard_map/ppermute | solution.py:17
  345.1 3.1 collective-permute-start.18
  348.2 5.4 %collective-permute-start.19 = (f32[2,1,8,8,128]{4,2,0,3,1:T(8,128)S(1)}, f32[2,1,8,8,128]{4,2,0,3,1:T(8,128)S(1)}, u32[]{:S(2)}, u32[]{:S(2)}) collective-permute-start(f32[2,1,8,8,128]{4,2,0,3,1:T(8,128)S(1)} %get-tuple-element.11), channel_id=1, source_target_pairs={{1,0},{2,1},{3,2},{4,3},{5,4},{6,5},{7,6},{8,7},{9,8},{10,9},{11,1... | collective-permute-start | bytes 196616 | tf_op jit(solution)/shard_map/ppermute | solution.py:17
  353.8 108.5 %copy-start.2 = (f32[2,1,8,8,8,128]{5,4,3,2,1,0:T(8,128)S(1)}, f32[2,1,8,8,8,128]{5,4,3,2,1,0:T(8,128)}, u32[]{:S(2)}) copy-start(f32[2,1,8,8,8,128]{5,4,3,2,1,0:T(8,128)} %get-tuple-element.25) | copy-start | bytes 1572868
  462.8 0.6 copy-start.20
  463.7 0.7 copy-start.24
  464.5 0.6 copy-start.22
where the time goes:
time: 469 us; the launch traced here: 467 us
  blocking collectives  333 us (71%)
  starting transfers between devices  53.8 us (11%)
  waiting for transfers between devices  31.1 us (7%)
  other arithmetic  15.7 us (3%)
  local copies, waits for them, and re-layouts  13.8 us (3%)
  matrix products  13.6 us (3%)
  between operations  6.61 us (1%)
    psum x2, blocking collectives, residual_dot(): return lax.psum(jnp.sum(left_field * right_field * weight), ('node', 'dev'))  227 us
    psum x1, blocking collectives, shards(): lax.psum(jnp.sum(direction * applied * weight), ('node', 'dev'))  106 us
    ppermute x20, starting transfers between devices, passed_along(): return lax.ppermute(x, axis, pairs)  53.8 us
    ppermute x20, waiting for transfers between devices, passed_along(): return lax.ppermute(x, axis, pairs)  31.1 us
    dot_general x18, matrix products, along(): jnp.einsum(einsum_forms[axis_at], matrix, field_in, precision=precise)  13.6 us
    unnamed x69, local copies, waits for them, and re-layouts  10.3 us
  transfers between devices with their start and end apart: 20, of which 13 were waited for; matrix products, arithmetic and copies ran while one was open for 1% of the time, Pallas kernels for 0%

commit v1 on v0

--- a/solution.py
+++ b/solution.py
@@ -253,30 +253,40 @@
     interior = (weight > 0.0).astype(jnp.float32)
     coefs = coefficients(size_x, size_y, size_z, tables[3])
 
-    def precondition(field_in):
-        return interior * summed(element_solve(field_in, tables, coefs))
-
-    right_side = interior * summed(flip_frame(element_load, orient))
-    solution = jnp.zeros_like(right_side)
-    residual = right_side
-
-    def residual_dot(left_field, right_field):
-        return lax.psum(jnp.sum(left_field * right_field * weight), ("node", "dev"))
-
-    precond = precondition(residual)
-    direction = precond
-    energy_old = residual_dot(residual, precond)
-    for step_at in range(ITERS):
-        applied = interior * summed(laplace(direction, tables, coefs))
-        step_len = energy_old / lax.psum(jnp.sum(direction * applied * weight), ("node", "dev"))
-        solution = solution + step_len * direction
-        residual = residual - step_len * applied
-        if step_at + 1 < ITERS:
-            precond = precondition(residual)
-            energy_new = residual_dot(residual, precond)
-            direction = precond + energy_new / energy_old * direction
-            energy_old = energy_new
-    return (flip_frame(solution, orient), flip_frame(residual, orient))
+    def apply(local):
+        return interior * summed(local)
+
+    load = apply(flip_frame(element_load, orient))
+    local = element_solve(load, tables, coefs)
+    dot_a = jnp.sum(load * local)
+    first = apply(local)
+    local = laplace(first, tables, coefs)
+    dot_c = jnp.sum(first * local)
+    image = apply(local)
+    local = element_solve(image, tables, coefs)
+    dot_d = jnp.sum(image * local)
+    second = apply(local)
+    local = laplace(second, tables, coefs)
+    dot_e = jnp.sum(second * local)
+    second_image = apply(local)
+    sums = total(jnp.stack([dot_a, dot_c, dot_d, dot_e]))
+    dot_a, dot_c, dot_d, dot_e = sums[0], sums[1], sums[2], sums[3]
+    alpha = dot_a / dot_c
+    energy = dot_a - 2.0 * alpha * dot_c + alpha * alpha * dot_d
+    keep = 1.0 + energy / dot_a
+    curve = keep * keep * dot_c - 2.0 * alpha * keep * dot_d + alpha * alpha * dot_e
+    step = energy / curve
+    answer = (alpha + step * keep) * first - (step * alpha) * second
+    rest = load - (alpha + step * keep) * image + (step * alpha) * second_image
+    return (flip_frame(answer, orient), flip_frame(rest, orient))
+
+
+def total(values):
+    row = jnp.zeros((1, 1, 128), jnp.float32).at[0, 0, :4].set(values)
+    for axis in ("dev", "node"):
+        sent = jnp.broadcast_to(row, (lax.axis_size(axis), 1, 128))
+        row = jnp.sum(lax.all_to_all(sent, axis, 0, 0), axis=0, keepdims=True)
+    return row[0, 0, :4]
 
 
 def solution(mesh):

time: 469 us -> 181 us (0.39)
  blocking collectives: 333 us -> 0 us
  starting transfers between devices: 53.8 us -> 90.5 us
  waiting for transfers between devices: 31.1 us -> 41.6 us
    psum x3 -> x0, blocking collectives: 333 us -> none  [the longest x2 227 us: residual_dot(): return lax.psum(jnp.sum(left_field * right_field * weight), ('node', 'dev'))]
    all_to_all x0 -> x2, starting transfers between devices: none -> 33.6 us  [total(): row = jnp.sum(lax.all_to_all(sent, axis, 0, 0), axis=0, keepdims=True)]
    all_to_all x0 -> x2, waiting for transfers between devices: none -> 12.4 us  [total(): row = jnp.sum(lax.all_to_all(sent, axis, 0, 0), axis=0, keepdims=True)]
    unnamed x69 -> x26, local copies, waits for them, and re-layouts: 10.3 us -> 7.22 us
  transfers between devices with their start and end apart: 20 -> 22, of which waited for: 13 -> 12; matrix products, arithmetic and copies ran while one was open for 1% -> 5% of each run, Pallas kernels for 0% -> 0%
where the time goes in v1:
time: 181 us; the launch traced here: 180 us
  starting transfers between devices  90.5 us (50%)
  waiting for transfers between devices  41.6 us (23%)
  other arithmetic  15.1 us (8%)
  matrix products  13 us (7%)
  local copies, waits for them, and re-layouts  11.7 us (6%)
  between operations  8.2 us (5%)
    ppermute x20, starting transfers between devices, passed_along(): return lax.ppermute(x, axis, pairs)  56.9 us
    all_to_all x2, starting transfers between devices, total(): row = jnp.sum(lax.all_to_all(sent, axis, 0, 0), axis=0, keepdims=True)  33.6 us
    ppermute x20, waiting for transfers between devices, passed_along(): return lax.ppermute(x, axis, pairs)  29.2 us
    dot_general x18, matrix products, along(): jnp.einsum(einsum_forms[axis_at], matrix, field_in, precision=precise)  13 us
    all_to_all x2, waiting for transfers between devices, total(): row = jnp.sum(lax.all_to_all(sent, axis, 0, 0), axis=0, keepdims=True)  12.4 us
    unnamed x26, local copies, waits for them, and re-layouts  7.22 us
  transfers between devices with their start and end apart: 22, of which 12 were waited for; matrix products, arithmetic and copies ran while one was open for 5% of the time, Pallas kernels for 0%

profile of v1, /device:TPU:1, one launch (start us, length us, event | category | flops | bytes accessed | tf_op | source)
XLA Modules:
  0.0 180.1 jit_solution(12963531885561899622)
XLA Ops:
  0.6 0.7 fusion.51
  1.9 1.3 reverse_select_fusion.5
  3.4 4.5 %collective-permute-start = (f32[1,1,8,8,128]{4,3,2,1,0:T(8,128)S(1)}, f32[1,1,8,8,128]{4,3,2,1,0:T(8,128)S(1)}, u32[]{:S(2)}, u32[]{:S(2)}) collective-permute-start(f32[1,1,8,8,128]{4,3,2,1,0:T(8,128)S(1)} %get-tuple-element.80), channel_id=1, source_target_pairs={{0,64},{64,128},{128,192},{192,256},{256,320},{320,384},{384,448},... | collective-permute-start | bytes 98312 | tf_op jit(solution)/shard_map/ppermute | solution.py:17
  8.0 5.6 %collective-permute-start.1 = (f32[1,1,8,8,128]{4,3,2,1,0:T(8,128)S(1)}, f32[1,1,8,8,128]{4,3,2,1,0:T(8,128)S(1)}, u32[]{:S(2)}, u32[]{:S(2)}) collective-permute-start(f32[1,1,8,8,128]{4,3,2,1,0:T(8,128)S(1)} %get-tuple-element.81), channel_id=1, source_target_pairs={{64,0},{128,64},{192,128},{256,192},{320,256},{384,320},{448,384},... | collective-permute-start | bytes 98312 | tf_op jit(solution)/shard_map/ppermute | solution.py:17
  14.4 0.7 copy-done.8
  15.0 0.7 copy-done.9
  15.9 0.7 copy-done.10
  17.2 1.3 collective-permute-start.2
  18.6 1.4 collective-permute-done.2
  20.0 1.3 collective-permute-start.3
  21.7 4.3 %collective-permute-done.3 = f32[2,1,8,8,128]{4,2,0,3,1:T(8,128)S(1)} collective-permute-done((f32[2,1,8,8,128]{4,2,0,3,1:T(8,128)S(1)}, f32[2,1,8,8,128]{4,2,0,3,1:T(8,128)S(1)}, u32[]{:S(2)}, u32[]{:S(2)}) %collective-permute-start.3) | collective-permute-done | bytes 65568 | tf_op jit(solution)/shard_map/ppermute | solution.py:17
  27.2 0.6 convolution_bitcast_fusion.9
  27.8 0.9 convolution_bitcast_fusion.8
  28.7 0.6 fusion.1
  29.3 0.9 convolution_bitcast_fusion.6
  30.2 0.9 convolution_bitcast_fusion.5
  31.1 0.6 fusion.31
  31.7 3.1 %collective-permute-start.4 = (f32[1,1,8,8,128]{4,3,2,1,0:T(8,128)S(1)}, f32[1,1,8,8,128]{4,3,2,1,0:T(8,128)S(1)}, u32[]{:S(2)}, u32[]{:S(2)}) collective-permute-start(f32[1,1,8,8,128]{4,3,2,1,0:T(8,128)S(1)} %get-tuple-element.74), channel_id=1, source_target_pairs={{0,64},{64,128},{128,192},{192,256},{256,320},{320,384},{384,448},... | collective-permute-start | bytes 98312 | tf_op jit(solution)/shard_map/ppermute | solution.py:17
  34.9 1.9 %collective-permute-start.5 = (f32[1,1,8,8,128]{4,3,2,1,0:T(8,128)S(1)}, f32[1,1,8,8,128]{4,3,2,1,0:T(8,128)S(1)}, u32[]{:S(2)}, u32[]{:S(2)}) collective-permute-start(f32[1,1,8,8,128]{4,3,2,1,0:T(8,128)S(1)} %get-tuple-element.77), channel_id=1, source_target_pairs={{64,0},{128,64},{192,128},{256,192},{320,256},{384,320},{448,384},... | collective-permute-start | bytes 98312 | tf_op jit(solution)/shard_map/ppermute | solution.py:17
  36.8 3.3 %collective-permute-done.5 = f32[1,1,8,8,128]{4,3,2,1,0:T(8,128)S(1)} collective-permute-done((f32[1,1,8,8,128]{4,3,2,1,0:T(8,128)S(1)}, f32[1,1,8,8,128]{4,3,2,1,0:T(8,128)S(1)}, u32[]{:S(2)}, u32[]{:S(2)}) %collective-permute-start.5) | collective-permute-done | bytes 32800 | tf_op jit(solution)/shard_map/ppermute | solution.py:17
  40.1 3.6 %collective-permute-start.6 = (f32[2,1,8,8,128]{4,3,2,0,1:T(8,128)S(1)}, f32[2,1,8,8,128]{4,3,2,0,1:T(8,128)S(1)}, u32[]{:S(2)}, u32[]{:S(2)}) collective-permute-start(f32[2,1,8,8,128]{4,3,2,0,1:T(8,128)S(1)} %maximum_bitcast_fusion.6), channel_id=1, source_target_pairs={{0,1},{1,2},{2,3},{3,4},{4,5},{5,6},{6,7},{7,8},{8,9},{9,10},{10,1... | collective-permute-start | bytes 196616 | tf_op jit(solution)/shard_map/ppermute | solution.py:17
  44.0 1.1 collective-permute-done.6
  45.1 1.3 collective-permute-start.7
  46.5 4.0 %collective-permute-done.7 = f32[2,1,8,8,128]{4,3,2,0,1:T(8,128)S(1)} collective-permute-done((f32[2,1,8,8,128]{4,3,2,0,1:T(8,128)S(1)}, f32[2,1,8,8,128]{4,3,2,0,1:T(8,128)S(1)}, u32[]{:S(2)}, u32[]{:S(2)}) %collective-permute-start.7) | collective-permute-done | bytes 65568 | tf_op jit(solution)/shard_map/ppermute | solution.py:17
  52.2 0.6 fusion.26
  52.8 0.9 fusion.28
  53.9 1.2 multiply_reduce_fusion.1
  55.2 4.5 %collective-permute-start.8 = (f32[1,1,8,8,128]{4,3,2,1,0:T(8,128)S(1)}, f32[1,1,8,8,128]{4,3,2,1,0:T(8,128)S(1)}, u32[]{:S(2)}, u32[]{:S(2)}) collective-permute-start(f32[1,1,8,8,128]{4,3,2,1,0:T(8,128)S(1)} %get-tuple-element.66), channel_id=1, source_target_pairs={{0,64},{64,128},{128,192},{192,256},{256,320},{320,384},{384,448},... | collective-permute-start | bytes 98312 | tf_op jit(solution)/shard_map/ppermute | solution.py:17
  59.7 1.9 %collective-permute-start.9 = (f32[1,1,8,8,128]{4,3,2,1,0:T(8,128)S(1)}, f32[1,1,8,8,128]{4,3,2,1,0:T(8,128)S(1)}, u32[]{:S(2)}, u32[]{:S(2)}) collective-permute-start(f32[1,1,8,8,128]{4,3,2,1,0:T(8,128)S(1)} %get-tuple-element.69), channel_id=1, source_target_pairs={{64,0},{128,64},{192,128},{256,192},{320,256},{384,320},{448,384},... | collective-permute-start | bytes 98312 | tf_op jit(solution)/shard_map/ppermute | solution.py:17
  62.0 2.9 %collective-permute-done.9 = f32[1,1,8,8,128]{4,3,2,1,0:T(8,128)S(1)} collective-permute-done((f32[1,1,8,8,128]{4,3,2,1,0:T(8,128)S(1)}, f32[1,1,8,8,128]{4,3,2,1,0:T(8,128)S(1)}, u32[]{:S(2)}, u32[]{:S(2)}) %collective-permute-start.9) | collective-permute-done | bytes 32800 | tf_op jit(solution)/shard_map/ppermute | solution.py:17
  65.1 4.5 %collective-permute-start.10 = (f32[2,1,8,8,128]{4,2,0,3,1:T(8,128)S(1)}, f32[2,1,8,8,128]{4,2,0,3,1:T(8,128)S(1)}, u32[]{:S(2)}, u32[]{:S(2)}) collective-permute-start(f32[2,1,8,8,128]{4,2,0,3,1:T(8,128)S(1)} %maximum_bitcast_fusion.4), channel_id=1, source_target_pairs={{0,1},{1,2},{2,3},{3,4},{4,5},{5,6},{6,7},{7,8},{8,9},{9,10},{10,1... | collective-permute-start | bytes 196616 | tf_op jit(solution)/shard_map/ppermute | solution.py:17
  69.8 0.9 collective-permute-done.10
  70.8 1.3 collective-permute-start.11
  72.4 3.8 %collective-permute-done.11 = f32[2,1,8,8,128]{4,2,0,3,1:T(8,128)S(1)} collective-permute-done((f32[2,1,8,8,128]{4,2,0,3,1:T(8,128)S(1)}, f32[2,1,8,8,128]{4,2,0,3,1:T(8,128)S(1)}, u32[]{:S(2)}, u32[]{:S(2)}) %collective-permute-start.11) | collective-permute-done | bytes 65568 | tf_op jit(solution)/shard_map/ppermute | solution.py:17
  76.9 0.6 convolution_bitcast_fusion.4
  77.5 0.9 convolution_bitcast_fusion.3
  78.4 0.6 fusion.3
  79.0 0.9 convolution_bitcast_fusion.1
  79.9 0.9 convolution_bitcast_fusion
  80.8 0.6 fusion.19
  81.5 4.4 %collective-permute-start.12 = (f32[1,1,8,8,128]{4,2,3,1,0:T(8,128)S(1)}, f32[1,1,8,8,128]{4,2,3,1,0:T(8,128)S(1)}, u32[]{:S(2)}, u32[]{:S(2)}) collective-permute-start(f32[1,1,8,8,128]{4,2,3,1,0:T(8,128)S(1)} %get-tuple-element.60), channel_id=1, source_target_pairs={{0,64},{64,128},{128,192},{192,256},{256,320},{320,384},{384,448},... | collective-permute-start | bytes 98312 | tf_op jit(solution)/shard_map/ppermute | solution.py:17
  86.1 1.9 %collective-permute-start.13 = (f32[1,1,8,8,128]{4,2,3,1,0:T(8,128)S(1)}, f32[1,1,8,8,128]{4,2,3,1,0:T(8,128)S(1)}, u32[]{:S(2)}, u32[]{:S(2)}) collective-permute-start(f32[1,1,8,8,128]{4,2,3,1,0:T(8,128)S(1)} %get-tuple-element.61), channel_id=1, source_target_pairs={{64,0},{128,64},{192,128},{256,192},{320,256},{384,320},{448,384},... | collective-permute-start | bytes 98312 | tf_op jit(solution)/shard_map/ppermute | solution.py:17
  88.1 3.3 %collective-permute-done.13 = f32[1,1,8,8,128]{4,2,3,1,0:T(8,128)S(1)} collective-permute-done((f32[1,1,8,8,128]{4,2,3,1,0:T(8,128)S(1)}, f32[1,1,8,8,128]{4,2,3,1,0:T(8,128)S(1)}, u32[]{:S(2)}, u32[]{:S(2)}) %collective-permute-start.13) | collective-permute-done | bytes 32800 | tf_op jit(solution)/shard_map/ppermute | solution.py:17
  91.4 5.3 %collective-permute-start.14 = (f32[2,1,8,8,128]{4,2,0,3,1:T(8,128)S(1)}, f32[2,1,8,8,128]{4,2,0,3,1:T(8,128)S(1)}, u32[]{:S(2)}, u32[]{:S(2)}) collective-permute-start(f32[2,1,8,8,128]{4,2,0,3,1:T(8,128)S(1)} %bitcast.423), channel_id=1, source_target_pairs={{0,1},{1,2},{2,3},{3,4},{4,5},{5,6},{6,7},{7,8},{8,9},{9,10},{10,1... | collective-permute-start | bytes 196616 | tf_op jit(solution)/shard_map/ppermute | solution.py:17
  96.8 1.3 collective-permute-start.15
  98.2 4.1 %collective-permute-done.15 = f32[2,1,8,8,128]{4,2,0,3,1:T(8,128)S(1)} collective-permute-done((f32[2,1,8,8,128]{4,2,0,3,1:T(8,128)S(1)}, f32[2,1,8,8,128]{4,2,0,3,1:T(8,128)S(1)}, u32[]{:S(2)}, u32[]{:S(2)}) %collective-permute-start.15) | collective-permute-done | bytes 65568 | tf_op jit(solution)/shard_map/ppermute | solution.py:17
  104.0 0.6 fusion.15
  104.6 0.9 fusion.17
  105.8 1.0 fusion.30
  106.7 1.4 fusion.14
  108.2 3.1 %collective-permute-start.16 = (f32[1,1,8,8,128]{4,3,2,1,0:T(8,128)S(1)}, f32[1,1,8,8,128]{4,3,2,1,0:T(8,128)S(1)}, u32[]{:S(2)}, u32[]{:S(2)}) collective-permute-start(f32[1,1,8,8,128]{4,3,2,1,0:T(8,128)S(1)} %get-tuple-element.46), channel_id=1, source_target_pairs={{0,64},{64,128},{128,192},{192,256},{256,320},{320,384},{384,448},... | collective-permute-start | bytes 98312 | tf_op jit(solution)/shard_map/ppermute | solution.py:17
  111.2 1.9 %collective-permute-start.17 = (f32[1,1,8,8,128]{4,3,2,1,0:T(8,128)S(1)}, f32[1,1,8,8,128]{4,3,2,1,0:T(8,128)S(1)}, u32[]{:S(2)}, u32[]{:S(2)}) collective-permute-start(f32[1,1,8,8,128]{4,3,2,1,0:T(8,128)S(1)} %get-tuple-element.49), channel_id=1, source_target_pairs={{64,0},{128,64},{192,128},{256,192},{320,256},{384,320},{448,384},... | collective-permute-start | bytes 98312 | tf_op jit(solution)/shard_map/ppermute | solution.py:17
  113.2 2.6 %select_maximum_fusion.6 = f32[128]{0:T(128)S(1)} fusion(f32[1]{0:T(128)} %bitcast.145, f32[1]{0:T(128)} %bitcast.119, f32[1]{0:T(128)} %bitcast.80, f32[1]{0:T(128)} %bitcast.45), kind=kLoop, calls=%fused_computation.213 | loop fusion | flops 1024 | bytes 528 | tf_op jit(solution)/shard_map/stack | solution.py:272
  115.8 0.6 broadcast_in_dim.202
  116.4 26.9 %all-to-all-start = ((f32[64,1,128]{2,1,0:T(1,128)}), f32[64,1,128]{2,1,0:T(1,128)S(1)}, u32[]{:S(2)}, u32[]{:S(2)}) async-start(f32[64,1,128]{2,1,0:T(1,128)} %broadcast_in_dim.202), calls=%async_computation | async-start | bytes 65536 | tf_op jit(solution)/shard_map/all_to_all | solution.py:288
  143.3 0.6 copy-done.2
  144.0 0.8 slice_add_fusion.1
  144.8 2.9 %collective-permute-start.18 = (f32[2,1,8,8,128]{4,3,2,0,1:T(8,128)S(1)}, f32[2,1,8,8,128]{4,3,2,0,1:T(8,128)S(1)}, u32[]{:S(2)}, u32[]{:S(2)}) collective-permute-start(f32[2,1,8,8,128]{4,3,2,0,1:T(8,128)S(1)} %maximum_bitcast_fusion), channel_id=1, source_target_pairs={{0,1},{1,2},{2,3},{3,4},{4,5},{5,6},{6,7},{7,8},{8,9},{9,10},{10,1... | collective-permute-start | bytes 196616 | tf_op jit(solution)/shard_map/ppermute | solution.py:17
  147.7 9.2 %all-to-all-done = f32[64,1,128]{2,1,0:T(1,128)S(1)} async-done(((f32[64,1,128]{2,1,0:T(1,128)}), f32[64,1,128]{2,1,0:T(1,128)S(1)}, u32[]{:S(2)}, u32[]{:S(2)}) %all-to-all-start) | async-done | bytes 32800 | tf_op jit(solution)/shard_map/all_to_all | solution.py:288
  157.5 6.7 %all-to-all-start.1 = ((f32[8,1,128]{2,1,0:T(1,128)}), f32[8,1,128]{2,1,0:T(1,128)S(1)}, u32[]{:S(2)}, u32[]{:S(2)}) async-start(f32[8,1,128]{2,1,0:T(1,128)} %broadcast_in_dim.203), calls=%async_computation.1 | async-start | bytes 8192 | tf_op jit(solution)/shard_map/all_to_all | solution.py:288
  164.2 1.3 collective-permute-start.19
  165.5 3.2 %all-to-all-done.1 = f32[8,1,128]{2,1,0:T(1,128)S(1)} async-done(((f32[8,1,128]{2,1,0:T(1,128)}), f32[8,1,128]{2,1,0:T(1,128)S(1)}, u32[]{:S(2)}, u32[]{:S(2)}) %all-to-all-start.1) | async-done | bytes 4128 | tf_op jit(solution)/shard_map/all_to_all | solution.py:288
  177.9 1.1 copy.300
  179.0 1.1 copy.299
  (145 shorter events, 13.6 us)
Async XLA Ops:
  1.4 0.6 copy-start.5
  1.4 1.9 %copy-start.3 = (pred[2,128]{1,0:T(4,128)(4,1)}, pred[2,128]{1,0:T(4,128)(4,1)S(1)}, u32[]{:S(2)}) copy-start(pred[2,128]{1,0:T(4,128)(4,1)S(1)} %get-tuple-element.114) | copy-start | bytes 772
  3.4 13.5 %collective-permute-start = (f32[1,1,8,8,128]{4,3,2,1,0:T(8,128)S(1)}, f32[1,1,8,8,128]{4,3,2,1,0:T(8,128)S(1)}, u32[]{:S(2)}, u32[]{:S(2)}) collective-permute-start(f32[1,1,8,8,128]{4,3,2,1,0:T(8,128)S(1)} %get-tuple-element.80), channel_id=1, source_target_pairs={{0,64},{64,128},{128,192},{192,256},{256,320},{320,384},{384,448},... | collective-permute-start | bytes 98312 | tf_op jit(solution)/shard_map/ppermute | solution.py:17
  8.0 9.1 %collective-permute-start.1 = (f32[1,1,8,8,128]{4,3,2,1,0:T(8,128)S(1)}, f32[1,1,8,8,128]{4,3,2,1,0:T(8,128)S(1)}, u32[]{:S(2)}, u32[]{:S(2)}) collective-permute-start(f32[1,1,8,8,128]{4,3,2,1,0:T(8,128)S(1)} %get-tuple-element.81), channel_id=1, source_target_pairs={{64,0},{128,64},{192,128},{256,192},{320,256},{384,320},{448,384},... | collective-permute-start | bytes 98312 | tf_op jit(solution)/shard_map/ppermute | solution.py:17
  14.4 0.7 copy-start.8
  15.0 0.7 copy-start.9
  15.9 0.7 copy-start.10
  17.2 2.8 %collective-permute-start.2 = (f32[2,1,8,8,128]{4,2,0,3,1:T(8,128)S(1)}, f32[2,1,8,8,128]{4,2,0,3,1:T(8,128)S(1)}, u32[]{:S(2)}, u32[]{:S(2)}) collective-permute-start(f32[2,1,8,8,128]{4,2,0,3,1:T(8,128)S(1)} %maximum_bitcast_fusion.10), channel_id=1, source_target_pairs={{0,1},{1,2},{2,3},{3,4},{4,5},{5,6},{6,7},{7,8},{8,9},{9,10},{10,1... | collective-permute-start | bytes 196616 | tf_op jit(solution)/shard_map/ppermute | solution.py:17
  20.0 6.0 %collective-permute-start.3 = (f32[2,1,8,8,128]{4,2,0,3,1:T(8,128)S(1)}, f32[2,1,8,8,128]{4,2,0,3,1:T(8,128)S(1)}, u32[]{:S(2)}, u32[]{:S(2)}) collective-permute-start(f32[2,1,8,8,128]{4,2,0,3,1:T(8,128)S(1)} %get-tuple-element.39), channel_id=1, source_target_pairs={{1,0},{2,1},{3,2},{4,3},{5,4},{6,5},{7,6},{8,7},{9,8},{10,9},{11,1... | collective-permute-start | bytes 196616 | tf_op jit(solution)/shard_map/ppermute | solution.py:17
  26.5 0.7 copy-start
  31.7 5.1 %collective-permute-start.4 = (f32[1,1,8,8,128]{4,3,2,1,0:T(8,128)S(1)}, f32[1,1,8,8,128]{4,3,2,1,0:T(8,128)S(1)}, u32[]{:S(2)}, u32[]{:S(2)}) collective-permute-start(f32[1,1,8,8,128]{4,3,2,1,0:T(8,128)S(1)} %get-tuple-element.74), channel_id=1, source_target_pairs={{0,64},{64,128},{128,192},{192,256},{256,320},{320,384},{384,448},... | collective-permute-start | bytes 98312 | tf_op jit(solution)/shard_map/ppermute | solution.py:17
  34.9 5.2 %collective-permute-start.5 = (f32[1,1,8,8,128]{4,3,2,1,0:T(8,128)S(1)}, f32[1,1,8,8,128]{4,3,2,1,0:T(8,128)S(1)}, u32[]{:S(2)}, u32[]{:S(2)}) collective-permute-start(f32[1,1,8,8,128]{4,3,2,1,0:T(8,128)S(1)} %get-tuple-element.77), channel_id=1, source_target_pairs={{64,0},{128,64},{192,128},{256,192},{320,256},{384,320},{448,384},... | collective-permute-start | bytes 98312 | tf_op jit(solution)/shard_map/ppermute | solution.py:17
  40.1 5.0 %collective-permute-start.6 = (f32[2,1,8,8,128]{4,3,2,0,1:T(8,128)S(1)}, f32[2,1,8,8,128]{4,3,2,0,1:T(8,128)S(1)}, u32[]{:S(2)}, u32[]{:S(2)}) collective-permute-start(f32[2,1,8,8,128]{4,3,2,0,1:T(8,128)S(1)} %maximum_bitcast_fusion.6), channel_id=1, source_target_pairs={{0,1},{1,2},{2,3},{3,4},{4,5},{5,6},{6,7},{7,8},{8,9},{9,10},{10,1... | collective-permute-start | bytes 196616 | tf_op jit(solution)/shard_map/ppermute | solution.py:17
  45.1 1.3 copy-start.7
  45.1 5.3 %collective-permute-start.7 = (f32[2,1,8,8,128]{4,3,2,0,1:T(8,128)S(1)}, f32[2,1,8,8,128]{4,3,2,0,1:T(8,128)S(1)}, u32[]{:S(2)}, u32[]{:S(2)}) collective-permute-start(f32[2,1,8,8,128]{4,3,2,0,1:T(8,128)S(1)} %get-tuple-element.35), channel_id=1, source_target_pairs={{1,0},{2,1},{3,2},{4,3},{5,4},{6,5},{7,6},{8,7},{9,8},{10,9},{11,1... | collective-permute-start | bytes 196616 | tf_op jit(solution)/shard_map/ppermute | solution.py:17
  50.9 0.7 copy-start.1
  55.2 6.7 %collective-permute-start.8 = (f32[1,1,8,8,128]{4,3,2,1,0:T(8,128)S(1)}, f32[1,1,8,8,128]{4,3,2,1,0:T(8,128)S(1)}, u32[]{:S(2)}, u32[]{:S(2)}) collective-permute-start(f32[1,1,8,8,128]{4,3,2,1,0:T(8,128)S(1)} %get-tuple-element.66), channel_id=1, source_target_pairs={{0,64},{64,128},{128,192},{192,256},{256,320},{320,384},{384,448},... | collective-permute-start | bytes 98312 | tf_op jit(solution)/shard_map/ppermute | solution.py:17
  59.7 5.2 %collective-permute-start.9 = (f32[1,1,8,8,128]{4,3,2,1,0:T(8,128)S(1)}, f32[1,1,8,8,128]{4,3,2,1,0:T(8,128)S(1)}, u32[]{:S(2)}, u32[]{:S(2)}) collective-permute-start(f32[1,1,8,8,128]{4,3,2,1,0:T(8,128)S(1)} %get-tuple-element.69), channel_id=1, source_target_pairs={{64,0},{128,64},{192,128},{256,192},{320,256},{384,320},{448,384},... | collective-permute-start | bytes 98312 | tf_op jit(solution)/shard_map/ppermute | solution.py:17
  65.1 5.7 %collective-permute-start.10 = (f32[2,1,8,8,128]{4,2,0,3,1:T(8,128)S(1)}, f32[2,1,8,8,128]{4,2,0,3,1:T(8,128)S(1)}, u32[]{:S(2)}, u32[]{:S(2)}) collective-permute-start(f32[2,1,8,8,128]{4,2,0,3,1:T(8,128)S(1)} %maximum_bitcast_fusion.4), channel_id=1, source_target_pairs={{0,1},{1,2},{2,3},{3,4},{4,5},{5,6},{6,7},{7,8},{8,9},{9,10},{10,1... | collective-permute-start | bytes 196616 | tf_op jit(solution)/shard_map/ppermute | solution.py:17
  70.8 5.5 %collective-permute-start.11 = (f32[2,1,8,8,128]{4,2,0,3,1:T(8,128)S(1)}, f32[2,1,8,8,128]{4,2,0,3,1:T(8,128)S(1)}, u32[]{:S(2)}, u32[]{:S(2)}) collective-permute-start(f32[2,1,8,8,128]{4,2,0,3,1:T(8,128)S(1)} %get-tuple-element.33), channel_id=1, source_target_pairs={{1,0},{2,1},{3,2},{4,3},{5,4},{6,5},{7,6},{8,7},{9,8},{10,9},{11,1... | collective-permute-start | bytes 196616 | tf_op jit(solution)/shard_map/ppermute | solution.py:17
  81.5 6.5 %collective-permute-start.12 = (f32[1,1,8,8,128]{4,2,3,1,0:T(8,128)S(1)}, f32[1,1,8,8,128]{4,2,3,1,0:T(8,128)S(1)}, u32[]{:S(2)}, u32[]{:S(2)}) collective-permute-start(f32[1,1,8,8,128]{4,2,3,1,0:T(8,128)S(1)} %get-tuple-element.60), channel_id=1, source_target_pairs={{0,64},{64,128},{128,192},{192,256},{256,320},{320,384},{384,448},... | collective-permute-start | bytes 98312 | tf_op jit(solution)/shard_map/ppermute | solution.py:17
  86.1 5.2 %collective-permute-start.13 = (f32[1,1,8,8,128]{4,2,3,1,0:T(8,128)S(1)}, f32[1,1,8,8,128]{4,2,3,1,0:T(8,128)S(1)}, u32[]{:S(2)}, u32[]{:S(2)}) collective-permute-start(f32[1,1,8,8,128]{4,2,3,1,0:T(8,128)S(1)} %get-tuple-element.61), channel_id=1, source_target_pairs={{64,0},{128,64},{192,128},{256,192},{320,256},{384,320},{448,384},... | collective-permute-start | bytes 98312 | tf_op jit(solution)/shard_map/ppermute | solution.py:17
  91.4 6.8 %collective-permute-start.14 = (f32[2,1,8,8,128]{4,2,0,3,1:T(8,128)S(1)}, f32[2,1,8,8,128]{4,2,0,3,1:T(8,128)S(1)}, u32[]{:S(2)}, u32[]{:S(2)}) collective-permute-start(f32[2,1,8,8,128]{4,2,0,3,1:T(8,128)S(1)} %bitcast.423), channel_id=1, source_target_pairs={{0,1},{1,2},{2,3},{3,4},{4,5},{5,6},{6,7},{7,8},{8,9},{9,10},{10,1... | collective-permute-start | bytes 196616 | tf_op jit(solution)/shard_map/ppermute | solution.py:17
  96.8 5.6 %collective-permute-start.15 = (f32[2,1,8,8,128]{4,2,0,3,1:T(8,128)S(1)}, f32[2,1,8,8,128]{4,2,0,3,1:T(8,128)S(1)}, u32[]{:S(2)}, u32[]{:S(2)}) collective-permute-start(f32[2,1,8,8,128]{4,2,0,3,1:T(8,128)S(1)} %bitcast.425), channel_id=1, source_target_pairs={{1,0},{2,1},{3,2},{4,3},{5,4},{6,5},{7,6},{8,7},{9,8},{10,9},{11,1... | collective-permute-start | bytes 196616 | tf_op jit(solution)/shard_map/ppermute | solution.py:17
  108.2 35.2 %collective-permute-start.16 = (f32[1,1,8,8,128]{4,3,2,1,0:T(8,128)S(1)}, f32[1,1,8,8,128]{4,3,2,1,0:T(8,128)S(1)}, u32[]{:S(2)}, u32[]{:S(2)}) collective-permute-start(f32[1,1,8,8,128]{4,3,2,1,0:T(8,128)S(1)} %get-tuple-element.46), channel_id=1, source_target_pairs={{0,64},{64,128},{128,192},{192,256},{256,320},{320,384},{384,448},... | collective-permute-start | bytes 98312 | tf_op jit(solution)/shard_map/ppermute | solution.py:17
  111.2 32.1 %collective-permute-start.17 = (f32[1,1,8,8,128]{4,3,2,1,0:T(8,128)S(1)}, f32[1,1,8,8,128]{4,3,2,1,0:T(8,128)S(1)}, u32[]{:S(2)}, u32[]{:S(2)}) collective-permute-start(f32[1,1,8,8,128]{4,3,2,1,0:T(8,128)S(1)} %get-tuple-element.49), channel_id=1, source_target_pairs={{64,0},{128,64},{192,128},{256,192},{320,256},{384,320},{448,384},... | collective-permute-start | bytes 98312 | tf_op jit(solution)/shard_map/ppermute | solution.py:17
  116.4 40.4 %all-to-all-start = ((f32[64,1,128]{2,1,0:T(1,128)}), f32[64,1,128]{2,1,0:T(1,128)S(1)}, u32[]{:S(2)}, u32[]{:S(2)}) async-start(f32[64,1,128]{2,1,0:T(1,128)} %broadcast_in_dim.202), calls=%async_computation | async-start | bytes 65536 | tf_op jit(solution)/shard_map/all_to_all | solution.py:288
  143.3 0.6 copy-start.2
  144.8 19.4 %collective-permute-start.18 = (f32[2,1,8,8,128]{4,3,2,0,1:T(8,128)S(1)}, f32[2,1,8,8,128]{4,3,2,0,1:T(8,128)S(1)}, u32[]{:S(2)}, u32[]{:S(2)}) collective-permute-start(f32[2,1,8,8,128]{4,3,2,0,1:T(8,128)S(1)} %maximum_bitcast_fusion), channel_id=1, source_target_pairs={{0,1},{1,2},{2,3},{3,4},{4,5},{5,6},{6,7},{7,8},{8,9},{9,10},{10,1... | collective-permute-start | bytes 196616 | tf_op jit(solution)/shard_map/ppermute | solution.py:17
  157.5 11.2 %all-to-all-start.1 = ((f32[8,1,128]{2,1,0:T(1,128)}), f32[8,1,128]{2,1,0:T(1,128)S(1)}, u32[]{:S(2)}, u32[]{:S(2)}) async-start(f32[8,1,128]{2,1,0:T(1,128)} %broadcast_in_dim.203), calls=%async_computation.1 | async-start | bytes 8192 | tf_op jit(solution)/shard_map/all_to_all | solution.py:288
  164.2 11.3 %collective-permute-start.19 = (f32[2,1,8,8,128]{4,3,2,0,1:T(8,128)S(1)}, f32[2,1,8,8,128]{4,3,2,0,1:T(8,128)S(1)}, u32[]{:S(2)}, u32[]{:S(2)}) collective-permute-start(f32[2,1,8,8,128]{4,3,2,0,1:T(8,128)S(1)} %get-tuple-element.23), channel_id=1, source_target_pairs={{1,0},{2,1},{3,2},{4,3},{5,4},{6,5},{7,6},{8,7},{9,8},{10,9},{11,1... | collective-permute-start | bytes 196616 | tf_op jit(solution)/shard_map/ppermute | solution.py:17
  176.1 0.7 copy-start.6
  177.2 0.6 copy-start.4

commit v2 on v0

v2 whole, which is shorter than its diff:
```python
import functools
import math

import jax
import jax.numpy as jnp
import ml_dtypes
import numpy as np
from jax import lax
from jax.experimental import pallas as pl
from jax.experimental.pallas import tpu as pltpu
from jax.sharding import PartitionSpec as P

F32 = jnp.float32
BF16 = jnp.bfloat16


def passed_along(x, axis, by):
    peers = lax.axis_size(axis)
    return lax.ppermute(x, axis, [(i, (i + by) % peers) for i in range(peers)])


def legendre_pair(value):
    prev_val = 1.0
    curr_val = value
    prev_der = 0.0
    curr_der = 1.0
    for order in range(2, 8):
        next_val = ((2 * order - 1) * value * curr_val - (order - 1) * prev_val) / order
        next_der = prev_der + (2 * order - 1) * curr_val
        prev_val, curr_val = (curr_val, next_val)
        prev_der, curr_der = (curr_der, next_der)
    return (curr_val, curr_der)


def second_derivative(value):
    leg_val, leg_der = legendre_pair(value)
    return (2.0 * value * leg_der - 56.0 * leg_val) / (1.0 - value * value)


def basis_tables():
    guesses = [
        -0.8717401485096066,
        -0.5917001814331423,
        -0.2092992179024789,
        0.2092992179024789,
        0.5917001814331423,
        0.8717401485096066,
    ]
    inner_pts = []
    for guess in guesses:
        point = guess
        for newton in range(4):
            point = point - legendre_pair(point)[1] / second_derivative(point)
        inner_pts.append(point)
    gll_points = [-1.0] + inner_pts + [1.0]
    leg_values = [legendre_pair(point)[0] for point in gll_points]
    weights = [2.0 / (56.0 * lv * lv) for lv in leg_values]
    derivative = [[0.0] * 8 for row_at in range(8)]
    for row_at in range(8):
        for col_at in range(8):
            if row_at != col_at:
                derivative[row_at][col_at] = leg_values[row_at] / (
                    leg_values[col_at] * (gll_points[row_at] - gll_points[col_at])
                )
    derivative[0][0] = -14.0
    derivative[7][7] = 14.0
    stiffness = [
        [
            sum(
                (
                    derivative[mid][row_at] * weights[mid] * derivative[mid][col_at]
                    for mid in range(8)
                )
            )
            for col_at in range(8)
        ]
        for row_at in range(8)
    ]
    inv_sqrt = [1.0 / math.sqrt(wt) for wt in weights]
    matrix = [
        [inv_sqrt[row_at] * stiffness[row_at][col_at] * inv_sqrt[col_at] for col_at in range(8)]
        for row_at in range(8)
    ]
    vectors = [[1.0 if row_at == col_at else 0.0 for col_at in range(8)] for row_at in range(8)]
    for sweep in range(14):
        for first in range(8):
            for second in range(first + 1, 8):
                angle = 0.5 * math.atan2(
                    2.0 * matrix[first][second], matrix[second][second] - matrix[first][first]
                )
                cosine = math.cos(angle)
                sine = math.sin(angle)
                for other in range(8):
                    left_val = matrix[other][first]
                    right_val = matrix[other][second]
                    matrix[other][first] = cosine * left_val - sine * right_val
                    matrix[other][second] = sine * left_val + cosine * right_val
                for other in range(8):
                    left_val = matrix[first][other]
                    right_val = matrix[second][other]
                    matrix[first][other] = cosine * left_val - sine * right_val
                    matrix[second][other] = sine * left_val + cosine * right_val
                for other in range(8):
                    left_val = vectors[other][first]
                    right_val = vectors[other][second]
                    vectors[other][first] = cosine * left_val - sine * right_val
                    vectors[other][second] = sine * left_val + cosine * right_val
    eigen_vals = [max(matrix[idx_at][idx_at], 0.0) for idx_at in range(8)]
    eigen_modes = [
        [inv_sqrt[row_at] * vectors[row_at][col_at] for col_at in range(8)] for row_at in range(8)
    ]
    return (weights, stiffness, eigen_modes, eigen_vals)


WEIGHTS, STIFF, MODES, LAMS = basis_tables()
EVEN = [MODES[0][m] * MODES[7][m] > 0 for m in range(8)]


def split_table(table):
    high = table.astype(ml_dtypes.bfloat16)
    low = (table - high.astype(np.float64)).astype(ml_dtypes.bfloat16)
    return [high, low]


def plane_tables():
    modes, stiff, weights = np.array(MODES), np.array(STIFF), np.diag(WEIGHTS)
    four = np.eye(4)
    forward = np.kron(four, np.kron(modes.T, modes.T))
    backward = np.kron(four, np.kron(modes, modes))
    along_j = np.kron(four, np.kron(stiff, weights))
    along_k = np.kron(four, np.kron(weights, stiff))
    solve = np.stack(split_table(forward) + split_table(backward))
    local = np.stack(split_table(along_j) + split_table(along_k))
    return solve, local


def rows(i, j):
    return slice((i * 8 + j) * 8, (i * 8 + j) * 8 + 8)


def plane(n):
    return slice(n * 64, n * 64 + 64)


def eight(n):
    return slice(n * 8, n * 8 + 8)


def lanes(x):
    return slice(x * 128, x * 128 + 128)


def weighted(values, factors):
    total = None
    for value, factor in zip(values, factors):
        term = value * factor
        total = term if total is None else total + term
    return total


def halves(v):
    return [v[a] + v[7 - a] for a in range(4)], [v[a] - v[7 - a] for a in range(4)]


def to_modes(v):
    even, odd = halves(v)
    return [weighted(even if EVEN[m] else odd, [MODES[a][m] for a in range(4)]) for m in range(8)]


def from_modes(t):
    out = [None] * 8
    for a in range(4):
        even = weighted([t[m] for m in range(8) if EVEN[m]], [MODES[a][m] for m in range(8) if EVEN[m]])
        odd = weighted([t[m] for m in range(8) if not EVEN[m]], [MODES[a][m] for m in range(8) if not EVEN[m]])
        out[a], out[7 - a] = even + odd, even - odd
    return out


def stiff_line(v):
    even, odd = halves(v)
    out = [None] * 8
    for i in range(4):
        first = weighted(even, [0.5 * (STIFF[i][a] + STIFF[i][7 - a]) for a in range(4)])
        second = weighted(odd, [0.5 * (STIFF[i][a] - STIFF[i][7 - a]) for a in range(4)])
        out[i], out[7 - i] = first + second, first - second
    return out


def store_split(high_ref, low_ref, row, column, parts):
    chunk = jnp.concatenate(parts, axis=0)
    high = chunk.astype(BF16)
    low = (chunk - high.astype(F32)).astype(BF16)
    high_ref[row : row + 16, column] = high
    low_ref[row : row + 16, column] = low


def product(table, at, high, low):
    dot = functools.partial(jnp.dot, preferred_element_type=F32)
    return dot(table[at], high) + dot(table[at], low) + dot(table[at + 1], high)


def z_summed(ref):
    lane = lax.broadcasted_iota(jnp.int32, (8, 128), 1)
    for x in range(2):
        for i in range(8):
            first = ref[x, pl.ds(i * 64, 8, stride=8), :]
            last = ref[x, pl.ds(i * 64 + 7, 8, stride=8), :]
            ref[x, pl.ds(i * 64, 8, stride=8), :] = jnp.where(lane == 0, 0.0, first + pltpu.roll(last, 1, 1))
            ref[x, pl.ds(i * 64 + 7, 8, stride=8), :] = jnp.where(lane == 127, 0.0, last + pltpu.roll(first, 127, 1))


def x_joined(ref):
    both = ref[0, plane(7), :] + ref[1, plane(0), :]
    ref[0, plane(7), :] = both
    ref[1, plane(0), :] = both


def y_faces(ref, low_ref, high_ref):
    for x in range(2):
        for i in range(8):
            low_ref[x, eight(i), :] = ref[x, rows(i, 0), :]
            high_ref[x, eight(i), :] = ref[x, rows(i, 7), :]


def y_joined(value, x, i, j, before, after, coef):
    if j == 0:
        value = (value + before[x, eight(i), :]) * coef[0, 4]
    if j == 7:
        value = (value + after[x, eight(i), :]) * coef[1, 4]
    return value


def sublane_table(values):
    at = lax.broadcasted_iota(jnp.int32, (8, 128), 0)
    out = jnp.full((8, 128), values[7], F32)
    for n in range(7):
        out = jnp.where(at == n, values[n], out)
    return out


def over_sublanes(row):
    return jnp.broadcast_to(row, (8, 128))


def reversed_points(src, mid, out, orient):
    for x in range(2):
        code = over_sublanes(orient[x : x + 1, :])
        flip_i, flip_j, flip_k = (code & 1) != 0, (code & 2) != 0, (code & 4) != 0
        for i in range(4):
            for j in range(4):
                a, b = src[x, rows(i, j), :], src[x, rows(7 - i, j), :]
                c, d = src[x, rows(i, 7 - j), :], src[x, rows(7 - i, 7 - j), :]
                a, b = jnp.where(flip_i, b, a), jnp.where(flip_i, a, b)
                c, d = jnp.where(flip_i, d, c), jnp.where(flip_i, c, d)
                mid[x, rows(i, j), :] = jnp.where(flip_j, c, a)
                mid[x, rows(i, 7 - j), :] = jnp.where(flip_j, a, c)
                mid[x, rows(7 - i, j), :] = jnp.where(flip_j, d, b)
                mid[x, rows(7 - i, 7 - j), :] = jnp.where(flip_j, b, d)
        for i in range(8):
            for k in range(4):
                a = mid[x, pl.ds(i * 64 + k, 8, stride=8), :]
                b = mid[x, pl.ds(i * 64 + 7 - k, 8, stride=8), :]
                out[x, pl.ds(i * 64 + k, 8, stride=8), :] = jnp.where(flip_k, b, a)
                out[x, pl.ds(i * 64 + 7 - k, 8, stride=8), :] = jnp.where(flip_k, a, b)


def start_kernel(numbers, load, orient, size_z, field, y_low, y_high, x_low, x_high, coef, mid):
    reversed_points(load, mid, field, orient)
    z_summed(field)
    x_joined(field)
    y_faces(field, y_low, y_high)
    size_y = numbers[2]
    length = over_sublanes(size_z[...])
    weight_k = sublane_table(WEIGHTS)
    lam_k = sublane_table(LAMS)
    at = lax.broadcasted_iota(jnp.int32, (8, 128), 0)
    for x in range(2):
        size_x = numbers[x]
        coef_x = size_y * length / (2.0 * jnp.full((8, 128), size_x, F32))
        coef_y = size_x * length / (2.0 * jnp.full((8, 128), size_y, F32))
        coef_z = jnp.full((8, 128), size_x * size_y, F32) / (2.0 * length)
        coef[x, 0] = jnp.where(at == 0, coef_x, jnp.where(at == 1, coef_y, coef_z))
        coef[x, 1] = coef_x * weight_k
        coef[x, 2] = lam_k * coef_z + (coef_x + coef_y + coef_z) / 3.0
        coef[x, 3] = jnp.full((8, 128), numbers[3 + x], F32)
        coef[x, 4] = jnp.full((8, 128), numbers[5 + x], F32)
        coef[x, 5] = weight_k
    x_low[0:64, :] = field[0, plane(0), :]
    x_high[0:64, :] = field[1, plane(7), :]
    x_low[64:72, :] = coef[0, 0]
    x_high[64:72, :] = coef[1, 0]


def edge_kernel(x_low, x_high, before, after, low_out, high_out):
    low_out[...] = x_low[...]
    high_out[...] = x_high[...]
    low_out[0:8, :] += before[0, 0:8, :]
    low_out[56:64, :] += after[0, 0:8, :]
    high_out[0:8, :] += before[1, 56:64, :]
    high_out[56:64, :] += after[1, 56:64, :]


def solve_kernel(with_x, *refs):
    coef, table, field, before, after = refs[:5]
    refs = refs[5:]
    if with_x:
        x_before, x_after = refs[:2]
        refs = refs[2:]
    joined, out, y_low, y_high, dot, high, low, mid = refs
    for x in range(2):
        for pair in range(4):
            lines = []
            for j in (2 * pair, 2 * pair + 1):
                line = []
                for i in range(8):
                    value = y_joined(field[x, rows(i, j), :], x, i, j, before, after, coef)
                    if with_x and x == 0 and i == 0:
                        value = (value + x_before[eight(j), :]) * coef[0, 3] * (
                            coef[0, 4] if j == 0 else coef[1, 4] if j == 7 else 1.0
                        )
                    if with_x and x == 1 and i == 7:
                        value = (value + x_after[eight(j), :]) * coef[1, 3] * (
                            coef[0, 4] if j == 0 else coef[1, 4] if j == 7 else 1.0
                        )
                    joined[x, rows(i, j), :] = value
                    line.append(value)
                lines.append(to_modes(line))
            for m in range(8):
                store_split(high, low, m * 64 + pair * 16, lanes(x), [lines[0][m], lines[1][m]])
    for block in range(2):
        part = slice(block * 256, block * 256 + 256)
        mid[part, :] = product(table, 0, high[part, :], low[part, :])
    for x in range(2):
        coef_x, coef_y = over_sublanes(coef[x, 0, 0:1, :]), over_sublanes(coef[x, 0, 1:2, :])
        den_i = [coef_x * LAMS[m] for m in range(8)]
        den_j = [coef_y * LAMS[n] + coef[x, 2] for n in range(8)]
        for m in range(8):
            for pair in range(4):
                parts = [mid[rows(m, n), lanes(x)] / (den_i[m] + den_j[n]) for n in (2 * pair, 2 * pair + 1)]
                store_split(high, low, m * 64 + pair * 16, lanes(x), parts)
    for block in range(2):
        part = slice(block * 256, block * 256 + 256)
        mid[part, :] = product(table, 2, high[part, :], low[part, :])
    total = jnp.zeros((8, 128), F32)
    for x in range(2):
        for j in range(8):
            line = from_modes([mid[rows(m, j), lanes(x)] for m in range(8)])
            for i in range(8):
                out[x, rows(i, j), :] = line[i]
                total = total + line[i] * joined[x, rows(i, j), :]
    dot[...] = total
    z_summed(out)
    x_joined(out)
    y_faces(out, y_low, y_high)


def local_kernel(coef, table, field, before, after, joined, out, x_low, x_high, high, low, first, second):
    for x in range(2):
        for pair in range(4):
            for i in range(8):
                parts = []
                for j in (2 * pair, 2 * pair + 1):
                    value = y_joined(field[x, rows(i, j), :], x, i, j, before, after, coef)
                    if x == 0 and i == 0:
                        value = value * coef[0, 3]
                    if x == 1 and i == 7:
                        value = value * coef[1, 3]
                    joined[x, rows(i, j), :] = value
                    parts.append(value)
                store_split(high, low, i * 64 + pair * 16, lanes(x), parts)
    for block in range(2):
        part = slice(block * 256, block * 256 + 256)
        first[part, :] = product(table, 0, high[part, :], low[part, :])
        second[part, :] = product(table, 2, high[part, :], low[part, :])
    for x in range(2):
        coef_y, coef_z = over_sublanes(coef[x, 0, 1:2, :]), over_sublanes(coef[x, 0, 2:3, :])
        for j in range(8):
            scale = coef[x, 1] * WEIGHTS[j]
            line = stiff_line([joined[x, rows(i, j), :] for i in range(8)])
            for i in range(8):
                flat = coef_y * first[rows(i, j), lanes(x)] + coef_z * second[rows(i, j), lanes(x)]
                out[x, rows(i, j), :] = scale * line[i] + WEIGHTS[i] * flat
    x_low[0:64, :] = joined[0, plane(0), :]
    x_low[64:128, :] = out[0, plane(0), :]
    x_high[0:64, :] = joined[1, plane(7), :]
    x_high[64:128, :] = out[1, plane(7), :]


def cross_kernel(with_row, *refs):
    coef, table, field, local, x_before, x_after, kind_before, kind_after = refs[:8]
    refs = refs[8:]
    if with_row:
        earlier = refs[:3]
        refs = refs[3:]
    joined, out, y_low, y_high, dot, high, low, first, second = refs
    joined[...] = field[...]
    for pair in range(4):
        parts = [[], [], [], []]
        for j in (2 * pair, 2 * pair + 1):
            for side in range(2):
                own = field[side, rows(7 * side, j), :]
                came = (x_after if side else x_before)[eight(j), :] * coef[side, 3]
                joined[side, rows(7 * side, j), :] = own + came
                parts[side].append(came)
                parts[2 + side].append(own)
        for n in range(4):
            store_split(high, low, n * 64 + pair * 16, slice(0, 128), parts[n])
    first[...] = product(table, 0, high[...], low[...])
    second[...] = product(table, 2, high[...], low[...])
    total = jnp.zeros((8, 128), F32)
    for side in range(2):
        end = 7 * side
        coef_y, coef_z = over_sublanes(coef[side, 0, 1:2, :]), over_sublanes(coef[side, 0, 2:3, :])
        kind, sent = (kind_after, x_after) if side else (kind_before, x_before)
        far_x, far_y, far_z = [over_sublanes(kind[64 + n : 65 + n, :]) for n in range(3)]
        for j in range(8):
            came = sent[eight(j), :] * coef[side, 3]
            own = field[side, rows(end, j), :]
            pulled = coef[side, 1] * WEIGHTS[j] * came
            for i in range(8):
                value = local[side, rows(i, j), :] + STIFF[i][end] * pulled
                if i == end:
                    flat = coef_y * first[rows(side, j), :] + coef_z * second[rows(side, j), :]
                    value = value + WEIGHTS[end] * flat
                total = total + value * joined[side, rows(i, j), :]
                if i == end:
                    far = sent[64 + j * 8 : 72 + j * 8, :]
                    far = far + (STIFF[7 - end][7 - end] * WEIGHTS[j]) * (far_x * coef[side, 5]) * own
                    flat = far_y * first[rows(2 + side, j), :] + far_z * second[rows(2 + side, j), :]
                    far = far + WEIGHTS[7 - end] * flat
                    value = (value + far) * coef[side, 3]
                out[side, rows(i, j), :] = value
    z_summed(out)
    x_joined(out)
    y_faces(out, y_low, y_high)
    if with_row:
        lane = lax.broadcasted_iota(jnp.int32, (64, 128), 1)
        row = jnp.zeros((64, 128), F32)
        for n, value in enumerate([ref[...] for ref in earlier] + [total]):
            row = jnp.where(lane == n, jnp.sum(value), row)
        dot[...] = row
    else:
        dot[...] = total


def sum_kernel(parts, out):
    out[...] = over_sublanes(jnp.sum(parts[...], axis=0, keepdims=True))


def end_kernel(coef, orient, sums, last, before, after, load, first, image, second, answer, rest, one, two):
    lane = lax.broadcasted_iota(jnp.int32, (8, 128), 1)
    dots = [jnp.full((8, 128), jnp.sum(jnp.where(lane == n, sums[...], 0.0)), F32) for n in range(4)]
    alpha = dots[0] / dots[1]
    energy = dots[0] - 2.0 * alpha * dots[1] + alpha * alpha * dots[2]
    keep = 1.0 + energy / dots[0]
    curve = keep * keep * dots[1] - 2.0 * alpha * keep * dots[2] + alpha * alpha * dots[3]
    step = energy / curve
    on_first = alpha + step * keep
    on_second = step * alpha
    for x in range(2):
        for i in range(8):
            for j in range(8):
                at = rows(i, j)
                value = y_joined(last[x, at, :], x, i, j, before, after, coef)
                one[x, at, :] = on_first * first[x, at, :] - on_second * second[x, at, :]
                two[x, at, :] = load[x, at, :] - on_first * image[x, at, :] + on_second * value
    reversed_points(one, one, answer, orient)
    reversed_points(two, two, rest, orient)


def f32(*shape):
    return jax.ShapeDtypeStruct(shape, F32)


def call(kernel, outs, scratch, *args, scalars=0):
    return pl.pallas_call(
        kernel,
        out_shape=outs,
        in_specs=[pl.BlockSpec(memory_space=pltpu.SMEM)] * scalars
        + [pl.BlockSpec(memory_space=pltpu.VMEM)] * (len(args) - scalars),
        out_specs=jax.tree.map(lambda _: pl.BlockSpec(memory_space=pltpu.VMEM), outs),
        scratch_shapes=scratch,
        compiler_params=pltpu.CompilerParams(vmem_limit_bytes=24 * 1024 * 1024),
    )(*args)


FIELD = f32(2, 512, 128)
FACES = [f32(2, 64, 128)] * 2
EIGHT = f32(8, 128)


def swap_y(low, high):
    return passed_along(high, "dev", 1), passed_along(low, "dev", -1)


def swap_x(low, high):
    return passed_along(high, "node", 1), passed_along(low, "node", -1)


def shards(element_load, orient, size_x, size_y, size_z):
    solve_np, local_np = plane_tables()
    solve_table, local_table = jnp.asarray(solve_np), jnp.asarray(local_np)
    node, dev = lax.axis_index("node"), lax.axis_index("dev")
    ends = jnp.stack(
        [node > 0, node < lax.axis_size("node") - 1, dev > 0, dev < lax.axis_size("dev") - 1]
    ).astype(F32)
    numbers = jnp.concatenate([size_x, size_y, ends, jnp.zeros((1,), F32)])
    orient = orient.reshape(2, 128)

    field, y_low, y_high, x_low, x_high, coef = call(
        start_kernel,
        [FIELD, *FACES, f32(72, 128), f32(72, 128), f32(2, 8, 8, 128)],
        [pltpu.VMEM((2, 512, 128), F32)],
        numbers, element_load.reshape(2, 512, 128), orient, size_z.reshape(1, 128),
        scalars=1,
    )
    y_came = swap_y(y_low, y_high)
    x_faces = call(edge_kernel, [f32(72, 128)] * 2, [], x_low, x_high, *y_came)
    kinds = swap_x(*x_faces)

    def solved(field, y_came, x_came):
        joined, out, low, high, dot = call(
            functools.partial(solve_kernel, bool(x_came)),
            [FIELD, FIELD, *FACES, EIGHT],
            [pltpu.VMEM((512, 256), BF16)] * 2 + [pltpu.VMEM((512, 256), F32)],
            coef, solve_table, field, *y_came, *x_came,
        )
        return joined, out, swap_y(low, high), dot

    def applied(field, y_came, earlier):
        joined, local, low, high = call(
            local_kernel,
            [FIELD, FIELD, f32(128, 128), f32(128, 128)],
            [pltpu.VMEM((512, 256), BF16)] * 2 + [pltpu.VMEM((512, 256), F32)] * 2,
            coef, local_table, field, *y_came,
        )
        x_came = swap_x(low, high)
        joined, out, low, high, dot = call(
            functools.partial(cross_kernel, bool(earlier)),
            [FIELD, FIELD, *FACES, f32(64, 128) if earlier else EIGHT],
            [pltpu.VMEM((256, 128), BF16)] * 2 + [pltpu.VMEM((256, 128), F32)] * 2,
            coef, local_table, joined, local, *x_came, *kinds, *earlier,
        )
        return joined, out, swap_y(low, high), dot

    load, out, y_came, dot_a = solved(field, y_came, kinds)
    first, out, y_came, dot_c = applied(out, y_came, ())
    image, out, y_came, dot_d = solved(out, y_came, ())
    second, out, y_came, row = applied(out, y_came, (dot_a, dot_c, dot_d))
    row = lax.all_to_all(row.reshape(64, 1, 128), "dev", 0, 0).reshape(64, 128)
    row = call(sum_kernel, EIGHT, [], row)
    row = lax.all_to_all(row.reshape(8, 1, 128), "node", 0, 0).reshape(8, 128)
    answer, rest = call(
        end_kernel,
        [FIELD, FIELD],
        [pltpu.VMEM((2, 512, 128), F32)] * 2,
        coef, orient, row, out, *y_came, load, first, image, second,
    )
    return answer.reshape(element_load.shape), rest.reshape(element_load.shape)


def solution(mesh):
    return jax.shard_map(
        shards,
        mesh=mesh,
        in_specs=(
            P("node", "dev", None, None, None, None),
            P("node", "dev", None),
            P("node"),
            P("dev"),
            P(),
        ),
        out_specs=(
            P("node", "dev", None, None, None, None),
            P("node", "dev", None, None, None, None),
        ),
        check_vma=False,
    )
```

time: 469 us -> 117 us (0.25)
  blocking collectives: 333 us -> 0 us
  starting transfers between devices: 53.8 us -> 78.3 us
  other arithmetic: 15.7 us -> 0.81 us
  matrix products: 13.6 us -> 0 us
  local copies, waits for them, and re-layouts: 13.8 us -> 3.07 us
  Pallas kernels: 0 us -> 8.69 us
  waiting for transfers between devices: 31.1 us -> 24.3 us
  between operations: 6.61 us -> 1.51 us
    psum x3 -> x0, blocking collectives: 333 us -> none  [the longest x2 227 us: residual_dot(): return lax.psum(jnp.sum(left_field * right_field * weight), ('node', 'dev'))]
    all_to_all x0 -> x2, starting transfers between devices: none -> 19.1 us  [the longest x1 12.3 us: shards(): row = lax.all_to_all(row.reshape(64, 1, 128), 'dev', 0, 0).reshape(64, 128)]
    ppermute x20 -> x16, waiting for transfers between devices: 31.1 us -> 15.1 us  [passed_along(): return lax.ppermute(x, axis, [(i, (i + by) % peers) for i in range(peers)])]
    dot_general x18 -> x0, matrix products: 13.6 us -> none  [along(): jnp.einsum(einsum_forms[axis_at], matrix, field_in, precision=precise)]
    all_to_all x0 -> x2, waiting for transfers between devices: none -> 9.27 us  [the longest x1 4.76 us: shards(): row = lax.all_to_all(row.reshape(64, 1, 128), 'dev', 0, 0).reshape(64, 128)]
    pallas_call x0 -> x10, Pallas kernels: none -> 8.69 us  [call(): pl.pallas_call(kernel, out_shape=outs, in_specs=[pl.BlockSpec(memory_spac...]
    unnamed x69 -> x12, local copies, waits for them, and re-layouts: 10.3 us -> 3.07 us
    ppermute x20 -> x16, starting transfers between devices: 53.8 us -> 59.2 us  [passed_along(): return lax.ppermute(x, axis, [(i, (i + by) % peers) for i in range(peers)])]
  transfers between devices with their start and end apart: 20 -> 18, of which waited for: 13 -> 13; matrix products, arithmetic and copies ran while one was open for 1% -> 0% of each run, Pallas kernels for 0% -> 1%
where the time goes in v2:
time: 117 us
  starting transfers between devices  78.3 us (67%)
  waiting for transfers between devices  24.3 us (21%)
  Pallas kernels  8.69 us (7%)
  local copies, waits for them, and re-layouts  3.07 us (3%)
  between operations  1.51 us (1%)
    ppermute x16, starting transfers between devices, passed_along(): return lax.ppermute(x, axis, [(i, (i + by) % peers) for i in range(peers)])  59.2 us
    ppermute x16, waiting for transfers between devices, passed_along(): return lax.ppermute(x, axis, [(i, (i + by) % peers) for i in range(peers)])  15.1 us
    all_to_all x1, starting transfers between devices, shards(): row = lax.all_to_all(row.reshape(64, 1, 128), 'dev', 0, 0).reshape(64, 128)  12.3 us
    pallas_call x10, Pallas kernels, call(): pl.pallas_call(kernel, out_shape=outs, in_specs=[pl.BlockSpec(memory_spac...  8.69 us
    all_to_all x1, starting transfers between devices, shards(): row = lax.all_to_all(row.reshape(8, 1, 128), 'node', 0, 0).reshape(8, 128)  6.77 us
    all_to_all x1, waiting for transfers between devices, shards(): row = lax.all_to_all(row.reshape(64, 1, 128), 'dev', 0, 0).reshape(64, 128)  4.76 us
    all_to_all x1, waiting for transfers between devices, shards(): row = lax.all_to_all(row.reshape(8, 1, 128), 'node', 0, 0).reshape(8, 128)  4.51 us
    unnamed x12, local copies, waits for them, and re-layouts  3.07 us
  transfers between devices with their start and end apart: 18, of which 13 were waited for; matrix products, arithmetic and copies ran while one was open for 0% of the time, Pallas kernels for 1%

profile of v2, /device:TPU:1, one launch (start us, length us, event | category | flops | bytes accessed | tf_op | source)
XLA Modules:
  0.0 116.7 jit_solution(18092360171135227961)
XLA Ops:
  0.6 0.0 copy-start.1
  1.4 0.1 add_convert_fusion
  1.4 0.7 pad_maximum_fusion.numbers
  2.2 0.0 copy-start.2
  2.2 1.0 copy-done.2
  3.2 0.0 copy-start.3
  3.2 0.7 copy-done.3
  3.9 0.0 copy-start.5
  3.9 0.7 copy-done.5
  4.5 0.8 shard_map.86
  5.3 4.0 %collective-permute-start = (f32[2,64,128]{2,1,0:T(8,128)S(1)}, f32[2,64,128]{2,1,0:T(8,128)S(1)}, u32[]{:S(2)}, u32[]{:S(2)}) collective-permute-start(f32[2,64,128]{2,1,0:T(8,128)S(1)} %get-tuple-element.42), channel_id=1, source_target_pairs={{0,1},{1,2},{2,3},{3,4},{4,5},{5,6},{6,7},{7,8},{8,9},{9,10},{10,1... | collective-permute-start | bytes 196616 | tf_op jit(solution)/shard_map/ppermute | solution.py:19
  9.4 12.3 %collective-permute-start.1 = (f32[2,64,128]{2,1,0:T(8,128)S(1)}, f32[2,64,128]{2,1,0:T(8,128)S(1)}, u32[]{:S(2)}, u32[]{:S(2)}) collective-permute-start(f32[2,64,128]{2,1,0:T(8,128)S(1)} %get-tuple-element.43), channel_id=1, source_target_pairs={{0,63},{1,0},{2,1},{3,2},{4,3},{5,4},{6,5},{7,6},{8,7},{9,8},{10,9... | collective-permute-start | bytes 196616 | tf_op jit(solution)/shard_map/ppermute | solution.py:19
  21.7 0.0 collective-permute-done.before.refs_3_
  21.7 1.3 %collective-permute-done.1.after.refs_4_ = f32[2,64,128]{2,1,0:T(8,128)S(1)} collective-permute-done((f32[2,64,128]{2,1,0:T(8,128)S(1)}, f32[2,64,128]{2,1,0:T(8,128)S(1)}, u32[]{:S(2)}, u32[]{:S(2)}) %collective-permute-start.1) | collective-permute-done | bytes 65568 | tf_op jit(solution)/shard_map/ppermute | solution.py:19
  23.0 2.6 %collective-permute-start.2 = (f32[72,128]{1,0:T(8,128)S(1)}, f32[72,128]{1,0:T(8,128)S(1)}, u32[]{:S(2)}, u32[]{:S(2)}) collective-permute-start(f32[72,128]{1,0:T(8,128)S(1)} %get-tuple-element.46), channel_id=1, source_target_pairs={{0,64},{64,128},{128,192},{192,256},{256,320},{320,384},{384,448},... | collective-permute-start | bytes 110600 | tf_op jit(solution)/shard_map/ppermute | solution.py:19
  25.6 0.0 collective-permute-start.3
  25.6 1.1 collective-permute-done.2.refs_5_.refs_6_
  26.7 2.3 %collective-permute-done.3.refs_6_.refs_7_ = f32[72,128]{1,0:T(8,128)S(1)} collective-permute-done((f32[72,128]{1,0:T(8,128)S(1)}, f32[72,128]{1,0:T(8,128)S(1)}, u32[]{:S(2)}, u32[]{:S(2)}) %collective-permute-start.3) | collective-permute-done | bytes 36896 | tf_op jit(solution)/shard_map/ppermute | solution.py:19
  29.0 0.0 copy-done.1
  29.0 0.0 copy-start
  29.0 1.3 %shard_map.88 = (f32[2,512,128]{2,1,0:T(8,128)S(1)}, f32[2,512,128]{2,1,0:T(8,128)S(1)}, f32[2,64,128]{2,1,0:T(8,128)S(1)}, f32[2,64,128]{2,1,0:T(8,128)S(1)}, f32[8,128]{1,0:T(8,128)S(1)}) custom-call(f32[2,8,8,128]{3,2,1,0:T(8,128)S(1)} %get-tuple-element.40.refs_0_.coef, bf16[4,256,256]{2,1,0:T(8,128)(2,1)S(1)} %copy-done.1, ...), custom_call_target="tpu_custom_call" | custom-call | tf_op jit(solution)/shard_map/pallas_call | solution.py:476
  30.3 1.9 %collective-permute-start.4 = (f32[2,64,128]{2,1,0:T(8,128)S(1)}, f32[2,64,128]{2,1,0:T(8,128)S(1)}, u32[]{:S(2)}, u32[]{:S(2)}) collective-permute-start(f32[2,64,128]{2,1,0:T(8,128)S(1)} %get-tuple-element.49), channel_id=1, source_target_pairs={{0,1},{1,2},{2,3},{3,4},{4,5},{5,6},{6,7},{7,8},{8,9},{9,10},{10,1... | collective-permute-start | bytes 196616 | tf_op jit(solution)/shard_map/ppermute | solution.py:19
  32.2 7.3 %collective-permute-start.5 = (f32[2,64,128]{2,1,0:T(8,128)S(1)}, f32[2,64,128]{2,1,0:T(8,128)S(1)}, u32[]{:S(2)}, u32[]{:S(2)}) collective-permute-start(f32[2,64,128]{2,1,0:T(8,128)S(1)} %get-tuple-element.50), channel_id=1, source_target_pairs={{0,63},{1,0},{2,1},{3,2},{4,3},{5,4},{6,5},{7,6},{8,7},{9,8},{10,9... | collective-permute-start | bytes 196616 | tf_op jit(solution)/shard_map/ppermute | solution.py:19
  39.6 0.4 collective-permute-done.4.before
  40.0 0.9 collective-permute-done.5.after
  40.9 0.0 copy-done
  40.9 0.7 shard_map.89
  41.6 0.9 collective-permute-start.6
  42.5 0.2 collective-permute-start.7
  42.6 1.2 collective-permute-done.6.refs_4_
  43.8 2.7 %collective-permute-done.7.refs_5_ = f32[128,128]{1,0:T(8,128)S(1)} collective-permute-done((f32[128,128]{1,0:T(8,128)S(1)}, f32[128,128]{1,0:T(8,128)S(1)}, u32[]{:S(2)}, u32[]{:S(2)}) %collective-permute-start.7) | collective-permute-done | bytes 65568 | tf_op jit(solution)/shard_map/ppermute | solution.py:19
  46.5 0.5 shard_map.90
  47.0 1.9 %collective-permute-start.8 = (f32[2,64,128]{2,1,0:T(8,128)S(1)}, f32[2,64,128]{2,1,0:T(8,128)S(1)}, u32[]{:S(2)}, u32[]{:S(2)}) collective-permute-start(f32[2,64,128]{2,1,0:T(8,128)S(1)} %get-tuple-element.56), channel_id=1, source_target_pairs={{0,1},{1,2},{2,3},{3,4},{4,5},{5,6},{6,7},{7,8},{8,9},{9,10},{10,1... | collective-permute-start | bytes 196616 | tf_op jit(solution)/shard_map/ppermute | solution.py:19
  48.9 7.4 %collective-permute-start.9 = (f32[2,64,128]{2,1,0:T(8,128)S(1)}, f32[2,64,128]{2,1,0:T(8,128)S(1)}, u32[]{:S(2)}, u32[]{:S(2)}) collective-permute-start(f32[2,64,128]{2,1,0:T(8,128)S(1)} %get-tuple-element.57), channel_id=1, source_target_pairs={{0,63},{1,0},{2,1},{3,2},{4,3},{5,4},{6,5},{7,6},{8,7},{9,8},{10,9... | collective-permute-start | bytes 196616 | tf_op jit(solution)/shard_map/ppermute | solution.py:19
  56.3 0.0 collective-permute-done.8.refs_3_
  56.4 1.3 %collective-permute-done.9.refs_4_ = f32[2,64,128]{2,1,0:T(8,128)S(1)} collective-permute-done((f32[2,64,128]{2,1,0:T(8,128)S(1)}, f32[2,64,128]{2,1,0:T(8,128)S(1)}, u32[]{:S(2)}, u32[]{:S(2)}) %collective-permute-start.9) | collective-permute-done | bytes 65568 | tf_op jit(solution)/shard_map/ppermute | solution.py:19
  57.7 1.3 %shard_map.91 = (f32[2,512,128]{2,1,0:T(8,128)S(1)}, f32[2,512,128]{2,1,0:T(8,128)S(1)}, f32[2,64,128]{2,1,0:T(8,128)S(1)}, f32[2,64,128]{2,1,0:T(8,128)S(1)}, f32[8,128]{1,0:T(8,128)S(1)}) custom-call(f32[2,8,8,128]{3,2,1,0:T(8,128)S(1)} %get-tuple-element.40.refs_0_.coef, bf16[4,256,256]{2,1,0:T(8,128)(2,1)S(1)} %copy-done.1, ...), custom_call_target="tpu_custom_call" | custom-call | tf_op jit(solution)/shard_map/pallas_call | solution.py:476
  59.0 1.9 %collective-permute-start.10 = (f32[2,64,128]{2,1,0:T(8,128)S(1)}, f32[2,64,128]{2,1,0:T(8,128)S(1)}, u32[]{:S(2)}, u32[]{:S(2)}) collective-permute-start(f32[2,64,128]{2,1,0:T(8,128)S(1)} %get-tuple-element.59), channel_id=1, source_target_pairs={{0,1},{1,2},{2,3},{3,4},{4,5},{5,6},{6,7},{7,8},{8,9},{9,10},{10,1... | collective-permute-start | bytes 196616 | tf_op jit(solution)/shard_map/ppermute | solution.py:19
  60.9 7.0 %collective-permute-start.11 = (f32[2,64,128]{2,1,0:T(8,128)S(1)}, f32[2,64,128]{2,1,0:T(8,128)S(1)}, u32[]{:S(2)}, u32[]{:S(2)}) collective-permute-start(f32[2,64,128]{2,1,0:T(8,128)S(1)} %get-tuple-element.60), channel_id=1, source_target_pairs={{0,63},{1,0},{2,1},{3,2},{4,3},{5,4},{6,5},{7,6},{8,7},{9,8},{10,9... | collective-permute-start | bytes 196616 | tf_op jit(solution)/shard_map/ppermute | solution.py:19
  67.9 0.0 collective-permute-done.10.before
  67.9 1.3 %collective-permute-done.11.after = f32[2,64,128]{2,1,0:T(8,128)S(1)} collective-permute-done((f32[2,64,128]{2,1,0:T(8,128)S(1)}, f32[2,64,128]{2,1,0:T(8,128)S(1)}, u32[]{:S(2)}, u32[]{:S(2)}) %collective-permute-start.11) | collective-permute-done | bytes 65568 | tf_op jit(solution)/shard_map/ppermute | solution.py:19
  69.2 0.7 shard_map.92
  69.9 2.0 %collective-permute-start.12 = (f32[128,128]{1,0:T(8,128)S(1)}, f32[128,128]{1,0:T(8,128)S(1)}, u32[]{:S(2)}, u32[]{:S(2)}) collective-permute-start(f32[128,128]{1,0:T(8,128)S(1)} %get-tuple-element.63), channel_id=1, source_target_pairs={{0,64},{64,128},{128,192},{192,256},{256,320},{320,384},{384,448},... | collective-permute-start | bytes 196616 | tf_op jit(solution)/shard_map/ppermute | solution.py:19
  72.0 1.0 collective-permute-start.13
  73.0 0.7 collective-permute-done.12.refs_4_
  73.7 1.9 %collective-permute-done.13.refs_5_ = f32[128,128]{1,0:T(8,128)S(1)} collective-permute-done((f32[128,128]{1,0:T(8,128)S(1)}, f32[128,128]{1,0:T(8,128)S(1)}, u32[]{:S(2)}, u32[]{:S(2)}) %collective-permute-start.13) | collective-permute-done | bytes 65568 | tf_op jit(solution)/shard_map/ppermute | solution.py:19
  75.7 1.3 %shard_map.93 = (f32[2,512,128]{2,1,0:T(8,128)S(1)}, f32[2,512,128]{2,1,0:T(8,128)S(1)}, f32[2,64,128]{2,1,0:T(8,128)S(1)}, f32[2,64,128]{2,1,0:T(8,128)S(1)}, f32[64,128]{1,0:T(8,128)}) custom-call(f32[2,8,8,128]{3,2,1,0:T(8,128)S(1)} %get-tuple-element.40.refs_0_.coef, bf16[4,256,256]{2,1,0:T(8,128)(2,1)S(1)} %copy-done, ...), custom_call_target="tpu_custom_call" | custom-call | tf_op jit(solution)/shard_map/pallas_call | solution.py:476
  76.9 12.3 %all-to-all-start = ((f32[64,1,128]{2,1,0:T(1,128)}), f32[64,1,128]{2,1,0:T(1,128)S(1)}, u32[]{:S(2)}, u32[]{:S(2)}) async-start(f32[64,1,128]{2,1,0:T(1,128)} %bitcast.8), calls=%async_computation | async-start | bytes 65536 | tf_op jit(solution)/shard_map/all_to_all | solution.py:550
  89.2 2.9 %collective-permute-start.14 = (f32[2,64,128]{2,1,0:T(8,128)S(1)}, f32[2,64,128]{2,1,0:T(8,128)S(1)}, u32[]{:S(2)}, u32[]{:S(2)}) collective-permute-start(f32[2,64,128]{2,1,0:T(8,128)S(1)} %get-tuple-element.70), channel_id=1, source_target_pairs={{0,1},{1,2},{2,3},{3,4},{4,5},{5,6},{6,7},{7,8},{8,9},{9,10},{10,1... | collective-permute-start | bytes 196616 | tf_op jit(solution)/shard_map/ppermute | solution.py:19
  92.2 5.7 %collective-permute-start.15 = (f32[2,64,128]{2,1,0:T(8,128)S(1)}, f32[2,64,128]{2,1,0:T(8,128)S(1)}, u32[]{:S(2)}, u32[]{:S(2)}) collective-permute-start(f32[2,64,128]{2,1,0:T(8,128)S(1)} %get-tuple-element.71), channel_id=1, source_target_pairs={{0,63},{1,0},{2,1},{3,2},{4,3},{5,4},{6,5},{7,6},{8,7},{9,8},{10,9... | collective-permute-start | bytes 196616 | tf_op jit(solution)/shard_map/ppermute | solution.py:19
  97.9 4.8 %all-to-all-done = f32[64,1,128]{2,1,0:T(1,128)S(1)} async-done(((f32[64,1,128]{2,1,0:T(1,128)}), f32[64,1,128]{2,1,0:T(1,128)S(1)}, u32[]{:S(2)}, u32[]{:S(2)}) %all-to-all-start) | async-done | bytes 32800 | tf_op jit(solution)/shard_map/all_to_all | solution.py:550
  102.6 0.6 shard_map.94
  103.2 6.8 %all-to-all-start.1 = ((f32[8,1,128]{2,1,0:T(1,128)}), f32[8,1,128]{2,1,0:T(1,128)S(1)}, u32[]{:S(2)}, u32[]{:S(2)}) async-start(f32[8,1,128]{2,1,0:T(1,128)} %bitcast.11), calls=%async_computation.1 | async-start | bytes 8192 | tf_op jit(solution)/shard_map/all_to_all | solution.py:552
  110.0 0.0 collective-permute-done.14.before
  110.0 0.0 collective-permute-done.15.after
  110.0 4.5 %all-to-all-done.1 = f32[8,1,128]{2,1,0:T(1,128)S(1)} async-done(((f32[8,1,128]{2,1,0:T(1,128)}), f32[8,1,128]{2,1,0:T(1,128)S(1)}, u32[]{:S(2)}, u32[]{:S(2)}) %all-to-all-start.1) | async-done | bytes 4128 | tf_op jit(solution)/shard_map/all_to_all | solution.py:552
  114.5 0.0 copy-start.4
  114.5 0.7 copy-done.4
  115.2 1.5 %shard_map.95 = (f32[2,512,128]{2,1,0:T(8,128)}, f32[2,512,128]{2,1,0:T(8,128)}) custom-call(f32[2,8,8,128]{3,2,1,0:T(8,128)S(1)} %get-tuple-element.40.refs_0_.coef, s32[2,128]{1,0:T(2,128)S(1)} %bitcast.25, f32[8,128]{1,0:T(8,128)S(1)} %bitcast.23, f32[2,512,128]{2,1,0:T(8,128)S(1)} %get-tuple-element.69.last, ...), custom_call_target="tpu_custom_call" | custom-call | tf_op jit(solution)/shard_map/pallas_call | solution.py:476
  (1 shorter events, 0.0 us)
Async XLA Ops:
  0.6 28.4 %copy-start.1 = (bf16[4,256,256]{2,1,0:T(8,128)(2,1)S(1)}, bf16[4,256,256]{2,1,0:T(8,128)(2,1)}, u32[]{:S(2)}) copy-start(bf16[4,256,256]{2,1,0:T(8,128)(2,1)} %constant.21.clone.refs_1_) | copy-start | bytes 1572868
  2.2 1.0 copy-start.2
  3.2 0.7 copy-start.3
  3.9 0.7 copy-start.5
  5.3 16.3 %collective-permute-start = (f32[2,64,128]{2,1,0:T(8,128)S(1)}, f32[2,64,128]{2,1,0:T(8,128)S(1)}, u32[]{:S(2)}, u32[]{:S(2)}) collective-permute-start(f32[2,64,128]{2,1,0:T(8,128)S(1)} %get-tuple-element.42), channel_id=1, source_target_pairs={{0,1},{1,2},{2,3},{3,4},{4,5},{5,6},{6,7},{7,8},{8,9},{9,10},{10,1... | collective-permute-start | bytes 196616 | tf_op jit(solution)/shard_map/ppermute | solution.py:19
  9.4 13.6 %collective-permute-start.1 = (f32[2,64,128]{2,1,0:T(8,128)S(1)}, f32[2,64,128]{2,1,0:T(8,128)S(1)}, u32[]{:S(2)}, u32[]{:S(2)}) collective-permute-start(f32[2,64,128]{2,1,0:T(8,128)S(1)} %get-tuple-element.43), channel_id=1, source_target_pairs={{0,63},{1,0},{2,1},{3,2},{4,3},{5,4},{6,5},{7,6},{8,7},{9,8},{10,9... | collective-permute-start | bytes 196616 | tf_op jit(solution)/shard_map/ppermute | solution.py:19
  23.0 3.7 %collective-permute-start.2 = (f32[72,128]{1,0:T(8,128)S(1)}, f32[72,128]{1,0:T(8,128)S(1)}, u32[]{:S(2)}, u32[]{:S(2)}) collective-permute-start(f32[72,128]{1,0:T(8,128)S(1)} %get-tuple-element.46), channel_id=1, source_target_pairs={{0,64},{64,128},{128,192},{192,256},{256,320},{320,384},{384,448},... | collective-permute-start | bytes 110600 | tf_op jit(solution)/shard_map/ppermute | solution.py:19
  25.6 3.4 %collective-permute-start.3 = (f32[72,128]{1,0:T(8,128)S(1)}, f32[72,128]{1,0:T(8,128)S(1)}, u32[]{:S(2)}, u32[]{:S(2)}) collective-permute-start(f32[72,128]{1,0:T(8,128)S(1)} %get-tuple-element.47), channel_id=1, source_target_pairs={{0,448},{64,0},{128,64},{192,128},{256,192},{320,256},{384,320},{4... | collective-permute-start | bytes 110600 | tf_op jit(solution)/shard_map/ppermute | solution.py:19
  29.0 11.9 %copy-start = (bf16[4,256,256]{2,1,0:T(8,128)(2,1)S(1)}, bf16[4,256,256]{2,1,0:T(8,128)(2,1)}, u32[]{:S(2)}) copy-start(bf16[4,256,256]{2,1,0:T(8,128)(2,1)} %constant.22.clone.table.refs_1_) | copy-start | bytes 1572868
  30.3 9.7 %collective-permute-start.4 = (f32[2,64,128]{2,1,0:T(8,128)S(1)}, f32[2,64,128]{2,1,0:T(8,128)S(1)}, u32[]{:S(2)}, u32[]{:S(2)}) collective-permute-start(f32[2,64,128]{2,1,0:T(8,128)S(1)} %get-tuple-element.49), channel_id=1, source_target_pairs={{0,1},{1,2},{2,3},{3,4},{4,5},{5,6},{6,7},{7,8},{8,9},{9,10},{10,1... | collective-permute-start | bytes 196616 | tf_op jit(solution)/shard_map/ppermute | solution.py:19
  32.2 8.6 %collective-permute-start.5 = (f32[2,64,128]{2,1,0:T(8,128)S(1)}, f32[2,64,128]{2,1,0:T(8,128)S(1)}, u32[]{:S(2)}, u32[]{:S(2)}) collective-permute-start(f32[2,64,128]{2,1,0:T(8,128)S(1)} %get-tuple-element.50), channel_id=1, source_target_pairs={{0,63},{1,0},{2,1},{3,2},{4,3},{5,4},{6,5},{7,6},{8,7},{9,8},{10,9... | collective-permute-start | bytes 196616 | tf_op jit(solution)/shard_map/ppermute | solution.py:19
  41.6 2.2 %collective-permute-start.6 = (f32[128,128]{1,0:T(8,128)S(1)}, f32[128,128]{1,0:T(8,128)S(1)}, u32[]{:S(2)}, u32[]{:S(2)}) collective-permute-start(f32[128,128]{1,0:T(8,128)S(1)} %get-tuple-element.53), channel_id=1, source_target_pairs={{0,64},{64,128},{128,192},{192,256},{256,320},{320,384},{384,448},... | collective-permute-start | bytes 196616 | tf_op jit(solution)/shard_map/ppermute | solution.py:19
  42.5 4.0 %collective-permute-start.7 = (f32[128,128]{1,0:T(8,128)S(1)}, f32[128,128]{1,0:T(8,128)S(1)}, u32[]{:S(2)}, u32[]{:S(2)}) collective-permute-start(f32[128,128]{1,0:T(8,128)S(1)} %get-tuple-element.54), channel_id=1, source_target_pairs={{0,448},{64,0},{128,64},{192,128},{256,192},{320,256},{384,320},{4... | collective-permute-start | bytes 196616 | tf_op jit(solution)/shard_map/ppermute | solution.py:19
  47.0 9.4 %collective-permute-start.8 = (f32[2,64,128]{2,1,0:T(8,128)S(1)}, f32[2,64,128]{2,1,0:T(8,128)S(1)}, u32[]{:S(2)}, u32[]{:S(2)}) collective-permute-start(f32[2,64,128]{2,1,0:T(8,128)S(1)} %get-tuple-element.56), channel_id=1, source_target_pairs={{0,1},{1,2},{2,3},{3,4},{4,5},{5,6},{6,7},{7,8},{8,9},{9,10},{10,1... | collective-permute-start | bytes 196616 | tf_op jit(solution)/shard_map/ppermute | solution.py:19
  48.9 8.8 %collective-permute-start.9 = (f32[2,64,128]{2,1,0:T(8,128)S(1)}, f32[2,64,128]{2,1,0:T(8,128)S(1)}, u32[]{:S(2)}, u32[]{:S(2)}) collective-permute-start(f32[2,64,128]{2,1,0:T(8,128)S(1)} %get-tuple-element.57), channel_id=1, source_target_pairs={{0,63},{1,0},{2,1},{3,2},{4,3},{5,4},{6,5},{7,6},{8,7},{9,8},{10,9... | collective-permute-start | bytes 196616 | tf_op jit(solution)/shard_map/ppermute | solution.py:19
  59.0 9.0 %collective-permute-start.10 = (f32[2,64,128]{2,1,0:T(8,128)S(1)}, f32[2,64,128]{2,1,0:T(8,128)S(1)}, u32[]{:S(2)}, u32[]{:S(2)}) collective-permute-start(f32[2,64,128]{2,1,0:T(8,128)S(1)} %get-tuple-element.59), channel_id=1, source_target_pairs={{0,1},{1,2},{2,3},{3,4},{4,5},{5,6},{6,7},{7,8},{8,9},{9,10},{10,1... | collective-permute-start | bytes 196616 | tf_op jit(solution)/shard_map/ppermute | solution.py:19
  60.9 8.3 %collective-permute-start.11 = (f32[2,64,128]{2,1,0:T(8,128)S(1)}, f32[2,64,128]{2,1,0:T(8,128)S(1)}, u32[]{:S(2)}, u32[]{:S(2)}) collective-permute-start(f32[2,64,128]{2,1,0:T(8,128)S(1)} %get-tuple-element.60), channel_id=1, source_target_pairs={{0,63},{1,0},{2,1},{3,2},{4,3},{5,4},{6,5},{7,6},{8,7},{9,8},{10,9... | collective-permute-start | bytes 196616 | tf_op jit(solution)/shard_map/ppermute | solution.py:19
  69.9 3.8 %collective-permute-start.12 = (f32[128,128]{1,0:T(8,128)S(1)}, f32[128,128]{1,0:T(8,128)S(1)}, u32[]{:S(2)}, u32[]{:S(2)}) collective-permute-start(f32[128,128]{1,0:T(8,128)S(1)} %get-tuple-element.63), channel_id=1, source_target_pairs={{0,64},{64,128},{128,192},{192,256},{256,320},{320,384},{384,448},... | collective-permute-start | bytes 196616 | tf_op jit(solution)/shard_map/ppermute | solution.py:19
  72.0 3.7 %collective-permute-start.13 = (f32[128,128]{1,0:T(8,128)S(1)}, f32[128,128]{1,0:T(8,128)S(1)}, u32[]{:S(2)}, u32[]{:S(2)}) collective-permute-start(f32[128,128]{1,0:T(8,128)S(1)} %get-tuple-element.64), channel_id=1, source_target_pairs={{0,448},{64,0},{128,64},{192,128},{256,192},{320,256},{384,320},{4... | collective-permute-start | bytes 196616 | tf_op jit(solution)/shard_map/ppermute | solution.py:19
  76.9 25.7 %all-to-all-start = ((f32[64,1,128]{2,1,0:T(1,128)}), f32[64,1,128]{2,1,0:T(1,128)S(1)}, u32[]{:S(2)}, u32[]{:S(2)}) async-start(f32[64,1,128]{2,1,0:T(1,128)} %bitcast.8), calls=%async_computation | async-start | bytes 65536 | tf_op jit(solution)/shard_map/all_to_all | solution.py:550
  89.2 20.8 %collective-permute-start.14 = (f32[2,64,128]{2,1,0:T(8,128)S(1)}, f32[2,64,128]{2,1,0:T(8,128)S(1)}, u32[]{:S(2)}, u32[]{:S(2)}) collective-permute-start(f32[2,64,128]{2,1,0:T(8,128)S(1)} %get-tuple-element.70), channel_id=1, source_target_pairs={{0,1},{1,2},{2,3},{3,4},{4,5},{5,6},{6,7},{7,8},{8,9},{9,10},{10,1... | collective-permute-start | bytes 196616 | tf_op jit(solution)/shard_map/ppermute | solution.py:19
  92.2 17.8 %collective-permute-start.15 = (f32[2,64,128]{2,1,0:T(8,128)S(1)}, f32[2,64,128]{2,1,0:T(8,128)S(1)}, u32[]{:S(2)}, u32[]{:S(2)}) collective-permute-start(f32[2,64,128]{2,1,0:T(8,128)S(1)} %get-tuple-element.71), channel_id=1, source_target_pairs={{0,63},{1,0},{2,1},{3,2},{4,3},{5,4},{6,5},{7,6},{8,7},{9,8},{10,9... | collective-permute-start | bytes 196616 | tf_op jit(solution)/shard_map/ppermute | solution.py:19
  103.2 11.3 %all-to-all-start.1 = ((f32[8,1,128]{2,1,0:T(1,128)}), f32[8,1,128]{2,1,0:T(1,128)S(1)}, u32[]{:S(2)}, u32[]{:S(2)}) async-start(f32[8,1,128]{2,1,0:T(1,128)} %bitcast.11), calls=%async_computation.1 | async-start | bytes 8192 | tf_op jit(solution)/shard_map/all_to_all | solution.py:552
  114.5 0.7 copy-start.4

commit v3 on v2

--- a/solution.py
+++ b/solution.py
@@ -264,27 +264,42 @@
                 out[x, pl.ds(i * 64 + 7 - k, 8, stride=8), :] = jnp.where(flip_k, a, b)
 
 
-def start_kernel(numbers, load, orient, size_z, field, y_low, y_high, x_low, x_high, coef, mid):
-    reversed_points(load, mid, field, orient)
-    z_summed(field)
-    x_joined(field)
-    y_faces(field, y_low, y_high)
-    size_y = numbers[2]
-    length = over_sublanes(size_z[...])
+def start_kernel(ends, size_x_in, size_y_in, load_in, orient_in, size_z_in, *refs):
+    field, y_low, y_high, x_low, x_high, coef, orient, mid, load, length_ref, x_ref, y_ref, ready = refs
+    copies = [
+        pltpu.make_async_copy(load_in, load, ready.at[0]),
+        pltpu.make_async_copy(orient_in, orient, ready.at[1]),
+        pltpu.make_async_copy(size_z_in, length_ref, ready.at[2]),
+        pltpu.make_async_copy(size_x_in, x_ref, ready.at[3]),
+        pltpu.make_async_copy(size_y_in, y_ref, ready.at[4]),
+    ]
+    for copy in copies:
+        copy.start()
+    for copy in copies[1:]:
+        copy.wait()
+    node, dev = lax.axis_index("node"), lax.axis_index("dev")
+    inside = [jnp.where(at_end, 0.0, 1.0).astype(F32) for at_end in (node == 0, node == ends[0], dev == 0, dev == ends[1])]
+    size_y = y_ref[0]
+    length = over_sublanes(length_ref[...])
     weight_k = sublane_table(WEIGHTS)
     lam_k = sublane_table(LAMS)
     at = lax.broadcasted_iota(jnp.int32, (8, 128), 0)
     for x in range(2):
-        size_x = numbers[x]
+        size_x = x_ref[x]
         coef_x = size_y * length / (2.0 * jnp.full((8, 128), size_x, F32))
         coef_y = size_x * length / (2.0 * jnp.full((8, 128), size_y, F32))
         coef_z = jnp.full((8, 128), size_x * size_y, F32) / (2.0 * length)
         coef[x, 0] = jnp.where(at == 0, coef_x, jnp.where(at == 1, coef_y, coef_z))
         coef[x, 1] = coef_x * weight_k
         coef[x, 2] = lam_k * coef_z + (coef_x + coef_y + coef_z) / 3.0
-        coef[x, 3] = jnp.full((8, 128), numbers[3 + x], F32)
-        coef[x, 4] = jnp.full((8, 128), numbers[5 + x], F32)
+        coef[x, 3] = jnp.full((8, 128), inside[x], F32)
+        coef[x, 4] = jnp.full((8, 128), inside[2 + x], F32)
         coef[x, 5] = weight_k
+    copies[0].wait()
+    reversed_points(load, mid, field, orient)
+    z_summed(field)
+    x_joined(field)
+    y_faces(field, y_low, y_high)
     x_low[0:64, :] = field[0, plane(0), :]
     x_high[0:64, :] = field[1, plane(7), :]
     x_low[64:72, :] = coef[0, 0]
@@ -434,22 +449,29 @@
     x_joined(out)
     y_faces(out, y_low, y_high)
     if with_row:
-        lane = lax.broadcasted_iota(jnp.int32, (64, 128), 1)
-        row = jnp.zeros((64, 128), F32)
+        lane = lax.broadcasted_iota(jnp.int32, (8, 128), 1)
+        row = jnp.zeros((8, 128), F32)
         for n, value in enumerate([ref[...] for ref in earlier] + [total]):
-            row = jnp.where(lane == n, jnp.sum(value), row)
-        dot[...] = row
+            value = value + pltpu.roll(value, 64, 1)
+            value = value + pltpu.roll(value, 32, 1)
+            row = jnp.where(lane // 32 == n, value, row)
+        row = over_sublanes(jnp.sum(row, axis=0, keepdims=True))
+        for n in range(dot.shape[0] // 8):
+            dot[eight(n), :] = row
     else:
         dot[...] = total
 
 
 def sum_kernel(parts, out):
-    out[...] = over_sublanes(jnp.sum(parts[...], axis=0, keepdims=True))
+    row = over_sublanes(jnp.sum(parts[...], axis=0, keepdims=True))
+    for n in range(out.shape[0] // 8):
+        out[eight(n), :] = row
 
 
 def end_kernel(coef, orient, sums, last, before, after, load, first, image, second, answer, rest, one, two):
     lane = lax.broadcasted_iota(jnp.int32, (8, 128), 1)
-    dots = [jnp.full((8, 128), jnp.sum(jnp.where(lane == n, sums[...], 0.0)), F32) for n in range(4)]
+    row = jnp.sum(sums[...], axis=0, keepdims=True)
+    dots = [jnp.full((8, 128), jnp.sum(jnp.where(lane[0:1, :] // 32 == n, row, 0.0)), F32) for n in range(4)]
     alpha = dots[0] / dots[1]
     energy = dots[0] - 2.0 * alpha * dots[1] + alpha * alpha * dots[2]
     keep = 1.0 + energy / dots[0]
@@ -472,15 +494,15 @@
     return jax.ShapeDtypeStruct(shape, F32)
 
 
-def call(kernel, outs, scratch, *args, scalars=0):
+def call(kernel, outs, scratch, *args, spaces=(), room=24):
     return pl.pallas_call(
         kernel,
         out_shape=outs,
-        in_specs=[pl.BlockSpec(memory_space=pltpu.SMEM)] * scalars
-        + [pl.BlockSpec(memory_space=pltpu.VMEM)] * (len(args) - scalars),
+        in_specs=[pl.BlockSpec(memory_space=space) for space in spaces]
+        + [pl.BlockSpec(memory_space=pltpu.VMEM)] * (len(args) - len(spaces)),
         out_specs=jax.tree.map(lambda _: pl.BlockSpec(memory_space=pltpu.VMEM), outs),
         scratch_shapes=scratch,
-        compiler_params=pltpu.CompilerParams(vmem_limit_bytes=24 * 1024 * 1024),
+        compiler_params=pltpu.CompilerParams(vmem_limit_bytes=room * 1024 * 1024),
     )(*args)
 
 
@@ -489,30 +511,41 @@
 EIGHT = f32(8, 128)
 
 
+def kept_in_hbm(x):
+    return pltpu.with_memory_space_constraint(x, pltpu.HBM)
+
+
 def swap_y(low, high):
     return passed_along(high, "dev", 1), passed_along(low, "dev", -1)
 
 
 def swap_x(low, high):
     return passed_along(high, "node", 1), passed_along(low, "node", -1)
+
+
+def exchanged(rows_out, axis):
+    came = lax.all_to_all(rows_out.reshape(-1, 1, 128), axis, 0, 0)
+    return came.reshape(rows_out.shape)
 
 
 def shards(element_load, orient, size_x, size_y, size_z):
     solve_np, local_np = plane_tables()
     solve_table, local_table = jnp.asarray(solve_np), jnp.asarray(local_np)
-    node, dev = lax.axis_index("node"), lax.axis_index("dev")
-    ends = jnp.stack(
-        [node > 0, node < lax.axis_size("node") - 1, dev > 0, dev < lax.axis_size("dev") - 1]
-    ).astype(F32)
-    numbers = jnp.concatenate([size_x, size_y, ends, jnp.zeros((1,), F32)])
-    orient = orient.reshape(2, 128)
-
-    field, y_low, y_high, x_low, x_high, coef = call(
-        start_kernel,
-        [FIELD, *FACES, f32(72, 128), f32(72, 128), f32(2, 8, 8, 128)],
-        [pltpu.VMEM((2, 512, 128), F32)],
-        numbers, element_load.reshape(2, 512, 128), orient, size_z.reshape(1, 128),
-        scalars=1,
+    nodes, devs = lax.axis_size("node"), lax.axis_size("dev")
+    field, y_low, y_high, x_low, x_high, coef, orient = call(
+        functools.partial(start_kernel, (nodes - 1, devs - 1)),
+        [FIELD, *FACES, f32(72, 128), f32(72, 128), f32(2, 8, 8, 128), jax.ShapeDtypeStruct((2, 128), jnp.int32)],
+        [
+            pltpu.VMEM((2, 512, 128), F32),
+            pltpu.VMEM((2, 512, 128), F32),
+            pltpu.VMEM((1, 128), F32),
+            pltpu.SMEM((2,), F32),
+            pltpu.SMEM((1,), F32),
+            pltpu.SemaphoreType.DMA((5,)),
+        ],
+        size_x, size_y,
+        *map(kept_in_hbm, (element_load.reshape(2, 512, 128), orient.reshape(2, 128), size_z.reshape(1, 128))),
+        spaces=[pltpu.HBM] * 5,
     )
     y_came = swap_y(y_low, y_high)
     x_faces = call(edge_kernel, [f32(72, 128)] * 2, [], x_low, x_high, *y_came)
@@ -541,20 +574,20 @@
             [pltpu.VMEM((256, 128), BF16)] * 2 + [pltpu.VMEM((256, 128), F32)] * 2,
             coef, local_table, joined, local, *x_came, *kinds, *earlier,
         )
-        return joined, out, swap_y(low, high), dot
+        return joined, out, (low, high), dot
 
     load, out, y_came, dot_a = solved(field, y_came, kinds)
-    first, out, y_came, dot_c = applied(out, y_came, ())
-    image, out, y_came, dot_d = solved(out, y_came, ())
-    second, out, y_came, row = applied(out, y_came, (dot_a, dot_c, dot_d))
-    row = lax.all_to_all(row.reshape(64, 1, 128), "dev", 0, 0).reshape(64, 128)
-    row = call(sum_kernel, EIGHT, [], row)
-    row = lax.all_to_all(row.reshape(8, 1, 128), "node", 0, 0).reshape(8, 128)
+    first, out, faces, dot_c = applied(out, y_came, ())
+    image, out, y_came, dot_d = solved(out, swap_y(*faces), ())
+    second, out, (low, high), row = applied(out, y_came, (dot_a, dot_c, dot_d))
+    before, after = swap_y(low, high)
+    row = call(sum_kernel, f32(8, 128), [], exchanged(row, "dev"))
+    row = exchanged(row, "node")
     answer, rest = call(
         end_kernel,
         [FIELD, FIELD],
         [pltpu.VMEM((2, 512, 128), F32)] * 2,
-        coef, orient, row, out, *y_came, load, first, image, second,
+        coef, orient, row, out, before, after, load, first, image, second,
     )
     return answer.reshape(element_load.shape), rest.reshape(element_load.shape)
 

time: 117 us -> 115 us (0.983)
  local copies, waits for them, and re-layouts: 3.07 us -> 0.66 us
    unnamed x12 -> x6, local copies, waits for them, and re-layouts: 3.07 us -> 0.66 us
where the time goes in v3:
time: 115 us; the launch traced here: 114 us
  starting transfers between devices  78.2 us (68%)
  waiting for transfers between devices  24.4 us (21%)
  Pallas kernels  9.26 us (8%)
  between operations  1.51 us (1%)
    ppermute x16, starting transfers between devices, passed_along(): return lax.ppermute(x, axis, [(i, (i + by) % peers) for i in range(peers)])  59.2 us
    all_to_all x2, starting transfers between devices, exchanged(): came = lax.all_to_all(rows_out.reshape(-1, 1, 128), axis, 0, 0)  19.1 us
    ppermute x16, waiting for transfers between devices, passed_along(): return lax.ppermute(x, axis, [(i, (i + by) % peers) for i in range(peers)])  15.1 us
    all_to_all x2, waiting for transfers between devices, exchanged(): came = lax.all_to_all(rows_out.reshape(-1, 1, 128), axis, 0, 0)  9.27 us
    pallas_call x10, Pallas kernels, call(): pl.pallas_call(kernel, out_shape=outs, in_specs=[pl.BlockSpec(memory_spac...  9.26 us
  transfers between devices with their start and end apart: 18, of which 13 were waited for; matrix products, arithmetic and copies ran while one was open for 0% of the time, Pallas kernels for 1%

profile of v3, /device:TPU:1, one launch (start us, length us, event | category | flops | bytes accessed | tf_op | source)
XLA Modules:
  0.0 114.0 jit_solution(14255334765577805920)
XLA Ops:
  0.6 0.0 copy-start.1
  1.3 0.0 copy-start.2
  1.4 0.6 copy-done.2
  2.0 1.3 %shard_map.86 = (f32[2,512,128]{2,1,0:T(8,128)S(1)}, f32[2,64,128]{2,1,0:T(8,128)S(1)}, f32[2,64,128]{2,1,0:T(8,128)S(1)}, f32[72,128]{1,0:T(8,128)S(1)}, f32[72...) custom-call(f32[2]{0:T(128)S(1)} %copy-done.2, f32[1]{0:T(128)S(6)} %copy.15.size_y_in, ...), custom_call_target="tpu_custom_call" | custom-call | tf_op jit(solution)/shard_map/pallas_call | solution.py:498
  3.3 4.0 %collective-permute-start = (f32[2,64,128]{2,1,0:T(8,128)S(1)}, f32[2,64,128]{2,1,0:T(8,128)S(1)}, u32[]{:S(2)}, u32[]{:S(2)}) collective-permute-start(f32[2,64,128]{2,1,0:T(8,128)S(1)} %get-tuple-element.44), channel_id=1, source_target_pairs={{0,1},{1,2},{2,3},{3,4},{4,5},{5,6},{6,7},{7,8},{8,9},{9,10},{10,1... | collective-permute-start | bytes 196616 | tf_op jit(solution)/shard_map/ppermute | solution.py:19
  7.4 12.3 %collective-permute-start.1 = (f32[2,64,128]{2,1,0:T(8,128)S(1)}, f32[2,64,128]{2,1,0:T(8,128)S(1)}, u32[]{:S(2)}, u32[]{:S(2)}) collective-permute-start(f32[2,64,128]{2,1,0:T(8,128)S(1)} %get-tuple-element.45), channel_id=1, source_target_pairs={{0,63},{1,0},{2,1},{3,2},{4,3},{5,4},{6,5},{7,6},{8,7},{9,8},{10,9... | collective-permute-start | bytes 196616 | tf_op jit(solution)/shard_map/ppermute | solution.py:19
  19.7 0.0 collective-permute-done.before.refs_3_
  19.7 1.3 %collective-permute-done.1.after.refs_4_ = f32[2,64,128]{2,1,0:T(8,128)S(1)} collective-permute-done((f32[2,64,128]{2,1,0:T(8,128)S(1)}, f32[2,64,128]{2,1,0:T(8,128)S(1)}, u32[]{:S(2)}, u32[]{:S(2)}) %collective-permute-start.1) | collective-permute-done | bytes 65568 | tf_op jit(solution)/shard_map/ppermute | solution.py:19
  21.0 2.6 %collective-permute-start.2 = (f32[72,128]{1,0:T(8,128)S(1)}, f32[72,128]{1,0:T(8,128)S(1)}, u32[]{:S(2)}, u32[]{:S(2)}) collective-permute-start(f32[72,128]{1,0:T(8,128)S(1)} %get-tuple-element.48), channel_id=1, source_target_pairs={{0,64},{64,128},{128,192},{192,256},{256,320},{320,384},{384,448},... | collective-permute-start | bytes 110600 | tf_op jit(solution)/shard_map/ppermute | solution.py:19
  23.6 0.0 collective-permute-start.3
  23.6 1.1 collective-permute-done.2.refs_5_.refs_6_
  24.7 2.3 %collective-permute-done.3.refs_6_.refs_7_ = f32[72,128]{1,0:T(8,128)S(1)} collective-permute-done((f32[72,128]{1,0:T(8,128)S(1)}, f32[72,128]{1,0:T(8,128)S(1)}, u32[]{:S(2)}, u32[]{:S(2)}) %collective-permute-start.3) | collective-permute-done | bytes 36896 | tf_op jit(solution)/shard_map/ppermute | solution.py:19
  27.0 0.0 copy-done.1
  27.0 0.0 copy-start
  27.0 1.3 %shard_map.88 = (f32[2,512,128]{2,1,0:T(8,128)S(1)}, f32[2,512,128]{2,1,0:T(8,128)S(1)}, f32[2,64,128]{2,1,0:T(8,128)S(1)}, f32[2,64,128]{2,1,0:T(8,128)S(1)}, f32[8,128]{1,0:T(8,128)S(1)}) custom-call(f32[2,8,8,128]{3,2,1,0:T(8,128)S(1)} %get-tuple-element.41.refs_0_.coef, bf16[4,256,256]{2,1,0:T(8,128)(2,1)S(1)} %copy-done.1, ...), custom_call_target="tpu_custom_call" | custom-call | tf_op jit(solution)/shard_map/pallas_call | solution.py:498
  28.3 1.9 %collective-permute-start.4 = (f32[2,64,128]{2,1,0:T(8,128)S(1)}, f32[2,64,128]{2,1,0:T(8,128)S(1)}, u32[]{:S(2)}, u32[]{:S(2)}) collective-permute-start(f32[2,64,128]{2,1,0:T(8,128)S(1)} %get-tuple-element.51), channel_id=1, source_target_pairs={{0,1},{1,2},{2,3},{3,4},{4,5},{5,6},{6,7},{7,8},{8,9},{9,10},{10,1... | collective-permute-start | bytes 196616 | tf_op jit(solution)/shard_map/ppermute | solution.py:19
  30.3 7.3 %collective-permute-start.5 = (f32[2,64,128]{2,1,0:T(8,128)S(1)}, f32[2,64,128]{2,1,0:T(8,128)S(1)}, u32[]{:S(2)}, u32[]{:S(2)}) collective-permute-start(f32[2,64,128]{2,1,0:T(8,128)S(1)} %get-tuple-element.52), channel_id=1, source_target_pairs={{0,63},{1,0},{2,1},{3,2},{4,3},{5,4},{6,5},{7,6},{8,7},{9,8},{10,9... | collective-permute-start | bytes 196616 | tf_op jit(solution)/shard_map/ppermute | solution.py:19
  37.6 0.4 collective-permute-done.4.before
  38.0 0.9 collective-permute-done.5.after
  38.9 0.0 copy-done
  38.9 0.7 shard_map.89
  39.6 0.9 collective-permute-start.6
  40.5 0.1 collective-permute-start.7
  40.6 1.2 %collective-permute-done.6.refs_4_ = f32[128,128]{1,0:T(8,128)S(1)} collective-permute-done((f32[128,128]{1,0:T(8,128)S(1)}, f32[128,128]{1,0:T(8,128)S(1)}, u32[]{:S(2)}, u32[]{:S(2)}) %collective-permute-start.6) | collective-permute-done | bytes 65568 | tf_op jit(solution)/shard_map/ppermute | solution.py:19
  41.8 2.7 %collective-permute-done.7.refs_5_ = f32[128,128]{1,0:T(8,128)S(1)} collective-permute-done((f32[128,128]{1,0:T(8,128)S(1)}, f32[128,128]{1,0:T(8,128)S(1)}, u32[]{:S(2)}, u32[]{:S(2)}) %collective-permute-start.7) | collective-permute-done | bytes 65568 | tf_op jit(solution)/shard_map/ppermute | solution.py:19
  44.5 0.5 shard_map.90
  45.0 1.9 %collective-permute-start.8 = (f32[2,64,128]{2,1,0:T(8,128)S(1)}, f32[2,64,128]{2,1,0:T(8,128)S(1)}, u32[]{:S(2)}, u32[]{:S(2)}) collective-permute-start(f32[2,64,128]{2,1,0:T(8,128)S(1)} %get-tuple-element.58), channel_id=1, source_target_pairs={{0,1},{1,2},{2,3},{3,4},{4,5},{5,6},{6,7},{7,8},{8,9},{9,10},{10,1... | collective-permute-start | bytes 196616 | tf_op jit(solution)/shard_map/ppermute | solution.py:19
  46.9 7.4 %collective-permute-start.9 = (f32[2,64,128]{2,1,0:T(8,128)S(1)}, f32[2,64,128]{2,1,0:T(8,128)S(1)}, u32[]{:S(2)}, u32[]{:S(2)}) collective-permute-start(f32[2,64,128]{2,1,0:T(8,128)S(1)} %get-tuple-element.59), channel_id=1, source_target_pairs={{0,63},{1,0},{2,1},{3,2},{4,3},{5,4},{6,5},{7,6},{8,7},{9,8},{10,9... | collective-permute-start | bytes 196616 | tf_op jit(solution)/shard_map/ppermute | solution.py:19
  54.4 0.0 collective-permute-done.8.refs_3_
  54.4 1.3 %collective-permute-done.9.refs_4_ = f32[2,64,128]{2,1,0:T(8,128)S(1)} collective-permute-done((f32[2,64,128]{2,1,0:T(8,128)S(1)}, f32[2,64,128]{2,1,0:T(8,128)S(1)}, u32[]{:S(2)}, u32[]{:S(2)}) %collective-permute-start.9) | collective-permute-done | bytes 65568 | tf_op jit(solution)/shard_map/ppermute | solution.py:19
  55.7 1.3 %shard_map.91 = (f32[2,512,128]{2,1,0:T(8,128)S(1)}, f32[2,512,128]{2,1,0:T(8,128)S(1)}, f32[2,64,128]{2,1,0:T(8,128)S(1)}, f32[2,64,128]{2,1,0:T(8,128)S(1)}, f32[8,128]{1,0:T(8,128)S(1)}) custom-call(f32[2,8,8,128]{3,2,1,0:T(8,128)S(1)} %get-tuple-element.41.refs_0_.coef, bf16[4,256,256]{2,1,0:T(8,128)(2,1)S(1)} %copy-done.1, ...), custom_call_target="tpu_custom_call" | custom-call | tf_op jit(solution)/shard_map/pallas_call | solution.py:498
  57.0 1.9 %collective-permute-start.10 = (f32[2,64,128]{2,1,0:T(8,128)S(1)}, f32[2,64,128]{2,1,0:T(8,128)S(1)}, u32[]{:S(2)}, u32[]{:S(2)}) collective-permute-start(f32[2,64,128]{2,1,0:T(8,128)S(1)} %get-tuple-element.61), channel_id=1, source_target_pairs={{0,1},{1,2},{2,3},{3,4},{4,5},{5,6},{6,7},{7,8},{8,9},{9,10},{10,1... | collective-permute-start | bytes 196616 | tf_op jit(solution)/shard_map/ppermute | solution.py:19
  58.9 7.0 %collective-permute-start.11 = (f32[2,64,128]{2,1,0:T(8,128)S(1)}, f32[2,64,128]{2,1,0:T(8,128)S(1)}, u32[]{:S(2)}, u32[]{:S(2)}) collective-permute-start(f32[2,64,128]{2,1,0:T(8,128)S(1)} %get-tuple-element.62), channel_id=1, source_target_pairs={{0,63},{1,0},{2,1},{3,2},{4,3},{5,4},{6,5},{7,6},{8,7},{9,8},{10,9... | collective-permute-start | bytes 196616 | tf_op jit(solution)/shard_map/ppermute | solution.py:19
  65.9 0.0 collective-permute-done.10.before
  66.0 1.3 %collective-permute-done.11.after = f32[2,64,128]{2,1,0:T(8,128)S(1)} collective-permute-done((f32[2,64,128]{2,1,0:T(8,128)S(1)}, f32[2,64,128]{2,1,0:T(8,128)S(1)}, u32[]{:S(2)}, u32[]{:S(2)}) %collective-permute-start.11) | collective-permute-done | bytes 65568 | tf_op jit(solution)/shard_map/ppermute | solution.py:19
  67.3 0.7 shard_map.92
  68.0 2.0 %collective-permute-start.12 = (f32[128,128]{1,0:T(8,128)S(1)}, f32[128,128]{1,0:T(8,128)S(1)}, u32[]{:S(2)}, u32[]{:S(2)}) collective-permute-start(f32[128,128]{1,0:T(8,128)S(1)} %get-tuple-element.65), channel_id=1, source_target_pairs={{0,64},{64,128},{128,192},{192,256},{256,320},{320,384},{384,448},... | collective-permute-start | bytes 196616 | tf_op jit(solution)/shard_map/ppermute | solution.py:19
  70.0 1.0 collective-permute-start.13
  71.0 0.7 collective-permute-done.12.refs_4_
  71.7 2.0 %collective-permute-done.13.refs_5_ = f32[128,128]{1,0:T(8,128)S(1)} collective-permute-done((f32[128,128]{1,0:T(8,128)S(1)}, f32[128,128]{1,0:T(8,128)S(1)}, u32[]{:S(2)}, u32[]{:S(2)}) %collective-permute-start.13) | collective-permute-done | bytes 65568 | tf_op jit(solution)/shard_map/ppermute | solution.py:19
  73.7 1.3 %shard_map.93 = (f32[2,512,128]{2,1,0:T(8,128)S(1)}, f32[2,512,128]{2,1,0:T(8,128)S(1)}, f32[2,64,128]{2,1,0:T(8,128)S(1)}, f32[2,64,128]{2,1,0:T(8,128)S(1)}, f32[64,128]{1,0:T(8,128)}) custom-call(f32[2,8,8,128]{3,2,1,0:T(8,128)S(1)} %get-tuple-element.41.refs_0_.coef, bf16[4,256,256]{2,1,0:T(8,128)(2,1)S(1)} %copy-done, ...), custom_call_target="tpu_custom_call" | custom-call | tf_op jit(solution)/shard_map/pallas_call | solution.py:498
  75.0 12.3 %all-to-all-start = ((f32[64,1,128]{2,1,0:T(1,128)}), f32[64,1,128]{2,1,0:T(1,128)S(1)}, u32[]{:S(2)}, u32[]{:S(2)}) async-start(f32[64,1,128]{2,1,0:T(1,128)} %bitcast.4), calls=%async_computation | async-start | bytes 65536 | tf_op jit(solution)/shard_map/all_to_all | solution.py:527
  87.3 2.9 %collective-permute-start.14 = (f32[2,64,128]{2,1,0:T(8,128)S(1)}, f32[2,64,128]{2,1,0:T(8,128)S(1)}, u32[]{:S(2)}, u32[]{:S(2)}) collective-permute-start(f32[2,64,128]{2,1,0:T(8,128)S(1)} %get-tuple-element.72), channel_id=1, source_target_pairs={{0,1},{1,2},{2,3},{3,4},{4,5},{5,6},{6,7},{7,8},{8,9},{9,10},{10,1... | collective-permute-start | bytes 196616 | tf_op jit(solution)/shard_map/ppermute | solution.py:19
  90.2 5.7 %collective-permute-start.15 = (f32[2,64,128]{2,1,0:T(8,128)S(1)}, f32[2,64,128]{2,1,0:T(8,128)S(1)}, u32[]{:S(2)}, u32[]{:S(2)}) collective-permute-start(f32[2,64,128]{2,1,0:T(8,128)S(1)} %get-tuple-element.73), channel_id=1, source_target_pairs={{0,63},{1,0},{2,1},{3,2},{4,3},{5,4},{6,5},{7,6},{8,7},{9,8},{10,9... | collective-permute-start | bytes 196616 | tf_op jit(solution)/shard_map/ppermute | solution.py:19
  95.9 4.8 %all-to-all-done = f32[64,1,128]{2,1,0:T(1,128)S(1)} async-done(((f32[64,1,128]{2,1,0:T(1,128)}), f32[64,1,128]{2,1,0:T(1,128)S(1)}, u32[]{:S(2)}, u32[]{:S(2)}) %all-to-all-start) | async-done | bytes 32800 | tf_op jit(solution)/shard_map/all_to_all | solution.py:527
  100.7 0.6 shard_map.94
  101.3 6.8 %all-to-all-start.1 = ((f32[8,1,128]{2,1,0:T(1,128)}), f32[8,1,128]{2,1,0:T(1,128)S(1)}, u32[]{:S(2)}, u32[]{:S(2)}) async-start(f32[8,1,128]{2,1,0:T(1,128)} %bitcast.7), calls=%async_computation.1 | async-start | bytes 8192 | tf_op jit(solution)/shard_map/all_to_all | solution.py:527
  108.0 0.0 collective-permute-done.14.before
  108.0 0.0 collective-permute-done.15.after
  108.0 4.5 %all-to-all-done.1 = f32[8,1,128]{2,1,0:T(1,128)S(1)} async-done(((f32[8,1,128]{2,1,0:T(1,128)}), f32[8,1,128]{2,1,0:T(1,128)S(1)}, u32[]{:S(2)}, u32[]{:S(2)}) %all-to-all-start.1) | async-done | bytes 4128 | tf_op jit(solution)/shard_map/all_to_all | solution.py:527
  112.6 1.5 %shard_map.95 = (f32[2,512,128]{2,1,0:T(8,128)}, f32[2,512,128]{2,1,0:T(8,128)}) custom-call(f32[2,8,8,128]{3,2,1,0:T(8,128)S(1)} %get-tuple-element.41.refs_0_.coef, s32[2,128]{1,0:T(2,128)S(1)} %get-tuple-element.42.orient, f32[8,128]{1,0:T(8,128)S(1)} %bitcast.18, f32[2,512,128]{2,1,0:T(8,128)S(1)} %get-tuple-element.71.last, ...), custom_call_target="tpu_custom_call" | custom-call | tf_op jit(solution)/shard_map/pallas_call | solution.py:498
  (1 shorter events, 0.0 us)
Async XLA Ops:
  0.6 26.4 %copy-start.1 = (bf16[4,256,256]{2,1,0:T(8,128)(2,1)S(1)}, bf16[4,256,256]{2,1,0:T(8,128)(2,1)}, u32[]{:S(2)}) copy-start(bf16[4,256,256]{2,1,0:T(8,128)(2,1)} %constant.4.clone.refs_1_) | copy-start | bytes 1572868
  1.3 0.7 copy-start.2
  3.3 16.3 %collective-permute-start = (f32[2,64,128]{2,1,0:T(8,128)S(1)}, f32[2,64,128]{2,1,0:T(8,128)S(1)}, u32[]{:S(2)}, u32[]{:S(2)}) collective-permute-start(f32[2,64,128]{2,1,0:T(8,128)S(1)} %get-tuple-element.44), channel_id=1, source_target_pairs={{0,1},{1,2},{2,3},{3,4},{4,5},{5,6},{6,7},{7,8},{8,9},{9,10},{10,1... | collective-permute-start | bytes 196616 | tf_op jit(solution)/shard_map/ppermute | solution.py:19
  7.4 13.6 %collective-permute-start.1 = (f32[2,64,128]{2,1,0:T(8,128)S(1)}, f32[2,64,128]{2,1,0:T(8,128)S(1)}, u32[]{:S(2)}, u32[]{:S(2)}) collective-permute-start(f32[2,64,128]{2,1,0:T(8,128)S(1)} %get-tuple-element.45), channel_id=1, source_target_pairs={{0,63},{1,0},{2,1},{3,2},{4,3},{5,4},{6,5},{7,6},{8,7},{9,8},{10,9... | collective-permute-start | bytes 196616 | tf_op jit(solution)/shard_map/ppermute | solution.py:19
  21.0 3.7 %collective-permute-start.2 = (f32[72,128]{1,0:T(8,128)S(1)}, f32[72,128]{1,0:T(8,128)S(1)}, u32[]{:S(2)}, u32[]{:S(2)}) collective-permute-start(f32[72,128]{1,0:T(8,128)S(1)} %get-tuple-element.48), channel_id=1, source_target_pairs={{0,64},{64,128},{128,192},{192,256},{256,320},{320,384},{384,448},... | collective-permute-start | bytes 110600 | tf_op jit(solution)/shard_map/ppermute | solution.py:19
  23.6 3.4 %collective-permute-start.3 = (f32[72,128]{1,0:T(8,128)S(1)}, f32[72,128]{1,0:T(8,128)S(1)}, u32[]{:S(2)}, u32[]{:S(2)}) collective-permute-start(f32[72,128]{1,0:T(8,128)S(1)} %get-tuple-element.49), channel_id=1, source_target_pairs={{0,448},{64,0},{128,64},{192,128},{256,192},{320,256},{384,320},{4... | collective-permute-start | bytes 110600 | tf_op jit(solution)/shard_map/ppermute | solution.py:19
  27.0 11.9 %copy-start = (bf16[4,256,256]{2,1,0:T(8,128)(2,1)S(1)}, bf16[4,256,256]{2,1,0:T(8,128)(2,1)}, u32[]{:S(2)}) copy-start(bf16[4,256,256]{2,1,0:T(8,128)(2,1)} %constant.5.clone.table.refs_1_) | copy-start | bytes 1572868
  28.3 9.7 %collective-permute-start.4 = (f32[2,64,128]{2,1,0:T(8,128)S(1)}, f32[2,64,128]{2,1,0:T(8,128)S(1)}, u32[]{:S(2)}, u32[]{:S(2)}) collective-permute-start(f32[2,64,128]{2,1,0:T(8,128)S(1)} %get-tuple-element.51), channel_id=1, source_target_pairs={{0,1},{1,2},{2,3},{3,4},{4,5},{5,6},{6,7},{7,8},{8,9},{9,10},{10,1... | collective-permute-start | bytes 196616 | tf_op jit(solution)/shard_map/ppermute | solution.py:19
  30.3 8.6 %collective-permute-start.5 = (f32[2,64,128]{2,1,0:T(8,128)S(1)}, f32[2,64,128]{2,1,0:T(8,128)S(1)}, u32[]{:S(2)}, u32[]{:S(2)}) collective-permute-start(f32[2,64,128]{2,1,0:T(8,128)S(1)} %get-tuple-element.52), channel_id=1, source_target_pairs={{0,63},{1,0},{2,1},{3,2},{4,3},{5,4},{6,5},{7,6},{8,7},{9,8},{10,9... | collective-permute-start | bytes 196616 | tf_op jit(solution)/shard_map/ppermute | solution.py:19
  39.6 2.2 %collective-permute-start.6 = (f32[128,128]{1,0:T(8,128)S(1)}, f32[128,128]{1,0:T(8,128)S(1)}, u32[]{:S(2)}, u32[]{:S(2)}) collective-permute-start(f32[128,128]{1,0:T(8,128)S(1)} %get-tuple-element.55), channel_id=1, source_target_pairs={{0,64},{64,128},{128,192},{192,256},{256,320},{320,384},{384,448},... | collective-permute-start | bytes 196616 | tf_op jit(solution)/shard_map/ppermute | solution.py:19
  40.5 4.0 %collective-permute-start.7 = (f32[128,128]{1,0:T(8,128)S(1)}, f32[128,128]{1,0:T(8,128)S(1)}, u32[]{:S(2)}, u32[]{:S(2)}) collective-permute-start(f32[128,128]{1,0:T(8,128)S(1)} %get-tuple-element.56), channel_id=1, source_target_pairs={{0,448},{64,0},{128,64},{192,128},{256,192},{320,256},{384,320},{4... | collective-permute-start | bytes 196616 | tf_op jit(solution)/shard_map/ppermute | solution.py:19
  45.0 9.4 %collective-permute-start.8 = (f32[2,64,128]{2,1,0:T(8,128)S(1)}, f32[2,64,128]{2,1,0:T(8,128)S(1)}, u32[]{:S(2)}, u32[]{:S(2)}) collective-permute-start(f32[2,64,128]{2,1,0:T(8,128)S(1)} %get-tuple-element.58), channel_id=1, source_target_pairs={{0,1},{1,2},{2,3},{3,4},{4,5},{5,6},{6,7},{7,8},{8,9},{9,10},{10,1... | collective-permute-start | bytes 196616 | tf_op jit(solution)/shard_map/ppermute | solution.py:19
  46.9 8.8 %collective-permute-start.9 = (f32[2,64,128]{2,1,0:T(8,128)S(1)}, f32[2,64,128]{2,1,0:T(8,128)S(1)}, u32[]{:S(2)}, u32[]{:S(2)}) collective-permute-start(f32[2,64,128]{2,1,0:T(8,128)S(1)} %get-tuple-element.59), channel_id=1, source_target_pairs={{0,63},{1,0},{2,1},{3,2},{4,3},{5,4},{6,5},{7,6},{8,7},{9,8},{10,9... | collective-permute-start | bytes 196616 | tf_op jit(solution)/shard_map/ppermute | solution.py:19
  57.0 9.0 %collective-permute-start.10 = (f32[2,64,128]{2,1,0:T(8,128)S(1)}, f32[2,64,128]{2,1,0:T(8,128)S(1)}, u32[]{:S(2)}, u32[]{:S(2)}) collective-permute-start(f32[2,64,128]{2,1,0:T(8,128)S(1)} %get-tuple-element.61), channel_id=1, source_target_pairs={{0,1},{1,2},{2,3},{3,4},{4,5},{5,6},{6,7},{7,8},{8,9},{9,10},{10,1... | collective-permute-start | bytes 196616 | tf_op jit(solution)/shard_map/ppermute | solution.py:19
  58.9 8.3 %collective-permute-start.11 = (f32[2,64,128]{2,1,0:T(8,128)S(1)}, f32[2,64,128]{2,1,0:T(8,128)S(1)}, u32[]{:S(2)}, u32[]{:S(2)}) collective-permute-start(f32[2,64,128]{2,1,0:T(8,128)S(1)} %get-tuple-element.62), channel_id=1, source_target_pairs={{0,63},{1,0},{2,1},{3,2},{4,3},{5,4},{6,5},{7,6},{8,7},{9,8},{10,9... | collective-permute-start | bytes 196616 | tf_op jit(solution)/shard_map/ppermute | solution.py:19
  68.0 3.8 %collective-permute-start.12 = (f32[128,128]{1,0:T(8,128)S(1)}, f32[128,128]{1,0:T(8,128)S(1)}, u32[]{:S(2)}, u32[]{:S(2)}) collective-permute-start(f32[128,128]{1,0:T(8,128)S(1)} %get-tuple-element.65), channel_id=1, source_target_pairs={{0,64},{64,128},{128,192},{192,256},{256,320},{320,384},{384,448},... | collective-permute-start | bytes 196616 | tf_op jit(solution)/shard_map/ppermute | solution.py:19
  70.0 3.7 %collective-permute-start.13 = (f32[128,128]{1,0:T(8,128)S(1)}, f32[128,128]{1,0:T(8,128)S(1)}, u32[]{:S(2)}, u32[]{:S(2)}) collective-permute-start(f32[128,128]{1,0:T(8,128)S(1)} %get-tuple-element.66), channel_id=1, source_target_pairs={{0,448},{64,0},{128,64},{192,128},{256,192},{320,256},{384,320},{4... | collective-permute-start | bytes 196616 | tf_op jit(solution)/shard_map/ppermute | solution.py:19
  75.0 25.7 %all-to-all-start = ((f32[64,1,128]{2,1,0:T(1,128)}), f32[64,1,128]{2,1,0:T(1,128)S(1)}, u32[]{:S(2)}, u32[]{:S(2)}) async-start(f32[64,1,128]{2,1,0:T(1,128)} %bitcast.4), calls=%async_computation | async-start | bytes 65536 | tf_op jit(solution)/shard_map/all_to_all | solution.py:527
  87.3 20.8 %collective-permute-start.14 = (f32[2,64,128]{2,1,0:T(8,128)S(1)}, f32[2,64,128]{2,1,0:T(8,128)S(1)}, u32[]{:S(2)}, u32[]{:S(2)}) collective-permute-start(f32[2,64,128]{2,1,0:T(8,128)S(1)} %get-tuple-element.72), channel_id=1, source_target_pairs={{0,1},{1,2},{2,3},{3,4},{4,5},{5,6},{6,7},{7,8},{8,9},{9,10},{10,1... | collective-permute-start | bytes 196616 | tf_op jit(solution)/shard_map/ppermute | solution.py:19
  90.2 17.8 %collective-permute-start.15 = (f32[2,64,128]{2,1,0:T(8,128)S(1)}, f32[2,64,128]{2,1,0:T(8,128)S(1)}, u32[]{:S(2)}, u32[]{:S(2)}) collective-permute-start(f32[2,64,128]{2,1,0:T(8,128)S(1)} %get-tuple-element.73), channel_id=1, source_target_pairs={{0,63},{1,0},{2,1},{3,2},{4,3},{5,4},{6,5},{7,6},{8,7},{9,8},{10,9... | collective-permute-start | bytes 196616 | tf_op jit(solution)/shard_map/ppermute | solution.py:19
  101.3 11.3 %all-to-all-start.1 = ((f32[8,1,128]{2,1,0:T(1,128)}), f32[8,1,128]{2,1,0:T(1,128)S(1)}, u32[]{:S(2)}, u32[]{:S(2)}) async-start(f32[8,1,128]{2,1,0:T(1,128)} %bitcast.7), calls=%async_computation.1 | async-start | bytes 8192 | tf_op jit(solution)/shard_map/all_to_all | solution.py:527

commit v4 on v3

--- a/solution.py
+++ b/solution.py
@@ -215,18 +215,30 @@
     ref[1, plane(0), :] = both
 
 
-def y_faces(ref, low_ref, high_ref):
+def is_odd(coef):
+    return coef[0, 6] > 0.5
+
+
+def y_faces(ref, pair_ref, other_ref, coef):
+    odd = is_odd(coef)
     for x in range(2):
         for i in range(8):
-            low_ref[x, eight(i), :] = ref[x, rows(i, 0), :]
-            high_ref[x, eight(i), :] = ref[x, rows(i, 7), :]
-
-
-def y_joined(value, x, i, j, before, after, coef):
+            low, high = ref[x, rows(i, 0), :], ref[x, rows(i, 7), :]
+            pair_ref[x, eight(i), :] = jnp.where(odd, low, high)
+            other_ref[x, eight(i), :] = jnp.where(odd, high, low)
+
+
+def face_came(x, i, end, pair, other, coef):
+    odd = is_odd(coef)
+    first, second = (other, pair) if end == 0 else (pair, other)
+    return jnp.where(odd, second[x, eight(i), :], first[x, eight(i), :])
+
+
+def y_joined(value, x, i, j, other, pair, coef):
     if j == 0:
-        value = (value + before[x, eight(i), :]) * coef[0, 4]
+        value = (value + face_came(x, i, 0, pair, other, coef)) * coef[0, 4]
     if j == 7:
-        value = (value + after[x, eight(i), :]) * coef[1, 4]
+        value = (value + face_came(x, i, 7, pair, other, coef)) * coef[1, 4]
     return value
 
 
@@ -295,24 +307,25 @@
         coef[x, 3] = jnp.full((8, 128), inside[x], F32)
         coef[x, 4] = jnp.full((8, 128), inside[2 + x], F32)
         coef[x, 5] = weight_k
+        coef[x, 6] = jnp.full((8, 128), jnp.where(dev % 2 == 1, 1.0, 0.0), F32)
     copies[0].wait()
     reversed_points(load, mid, field, orient)
     z_summed(field)
     x_joined(field)
-    y_faces(field, y_low, y_high)
+    y_faces(field, y_low, y_high, coef)
     x_low[0:64, :] = field[0, plane(0), :]
     x_high[0:64, :] = field[1, plane(7), :]
     x_low[64:72, :] = coef[0, 0]
     x_high[64:72, :] = coef[1, 0]
 
 
-def edge_kernel(x_low, x_high, before, after, low_out, high_out):
+def edge_kernel(coef, x_low, x_high, other, pair, low_out, high_out):
     low_out[...] = x_low[...]
     high_out[...] = x_high[...]
-    low_out[0:8, :] += before[0, 0:8, :]
-    low_out[56:64, :] += after[0, 0:8, :]
-    high_out[0:8, :] += before[1, 56:64, :]
-    high_out[56:64, :] += after[1, 56:64, :]
+    low_out[0:8, :] += face_came(0, 0, 0, pair, other, coef)
+    low_out[56:64, :] += face_came(0, 0, 7, pair, other, coef)
+    high_out[0:8, :] += face_came(1, 7, 0, pair, other, coef)
+    high_out[56:64, :] += face_came(1, 7, 7, pair, other, coef)
 
 
 def solve_kernel(with_x, *refs):
@@ -366,7 +379,7 @@
     dot[...] = total
     z_summed(out)
     x_joined(out)
-    y_faces(out, y_low, y_high)
+    y_faces(out, y_low, y_high, coef)
 
 
 def local_kernel(coef, table, field, before, after, joined, out, x_low, x_high, high, low, first, second):
@@ -447,7 +460,7 @@
                 out[side, rows(i, j), :] = value
     z_summed(out)
     x_joined(out)
-    y_faces(out, y_low, y_high)
+    y_faces(out, y_low, y_high, coef)
     if with_row:
         lane = lax.broadcasted_iota(jnp.int32, (8, 128), 1)
         row = jnp.zeros((8, 128), F32)
@@ -515,8 +528,11 @@
     return pltpu.with_memory_space_constraint(x, pltpu.HBM)
 
 
-def swap_y(low, high):
-    return passed_along(high, "dev", 1), passed_along(low, "dev", -1)
+def swap_y(pair, other):
+    devs = lax.axis_size("dev")
+    far = lax.ppermute(other, "dev", [(i, i - 1 if i % 2 == 0 else i + 1) for i in range(1, devs - 1)])
+    near = lax.ppermute(pair, "dev", [(i, i + 1 if i % 2 == 0 else i - 1) for i in range(devs)])
+    return far, near
 
 
 def swap_x(low, high):
@@ -543,12 +559,12 @@
             pltpu.SMEM((1,), F32),
             pltpu.SemaphoreType.DMA((5,)),
         ],
-        size_x, size_y,
+        kept_in_hbm(size_x), size_y,
         *map(kept_in_hbm, (element_load.reshape(2, 512, 128), orient.reshape(2, 128), size_z.reshape(1, 128))),
         spaces=[pltpu.HBM] * 5,
     )
     y_came = swap_y(y_low, y_high)
-    x_faces = call(edge_kernel, [f32(72, 128)] * 2, [], x_low, x_high, *y_came)
+    x_faces = call(edge_kernel, [f32(72, 128)] * 2, [], coef, x_low, x_high, *y_came)
     kinds = swap_x(*x_faces)
 
     def solved(field, y_came, x_came):
@@ -570,7 +586,7 @@
         x_came = swap_x(low, high)
         joined, out, low, high, dot = call(
             functools.partial(cross_kernel, bool(earlier)),
-            [FIELD, FIELD, *FACES, f32(64, 128) if earlier else EIGHT],
+            [FIELD, FIELD, *FACES, pltpu.VMEM((64, 128), F32) if earlier else EIGHT],
             [pltpu.VMEM((256, 128), BF16)] * 2 + [pltpu.VMEM((256, 128), F32)] * 2,
             coef, local_table, joined, local, *x_came, *kinds, *earlier,
         )
@@ -581,7 +597,7 @@
     image, out, y_came, dot_d = solved(out, swap_y(*faces), ())
     second, out, (low, high), row = applied(out, y_came, (dot_a, dot_c, dot_d))
     before, after = swap_y(low, high)
-    row = call(sum_kernel, f32(8, 128), [], exchanged(row, "dev"))
+    row = call(sum_kernel, pltpu.VMEM((8, 128), F32), [], exchanged(row, "dev"))
     row = exchanged(row, "node")
     answer, rest = call(
         end_kernel,

time: 115 us -> 110 us (0.957)
  starting transfers between devices: 78.2 us -> 72.6 us
  waiting for transfers between devices: 24.4 us -> 25.8 us
    ppermute x16 -> x6, starting transfers between devices: 59.2 us -> 10 us  [passed_along(): return lax.ppermute(x, axis, [(i, (i + by) % peers) for i in range(peers)])]
    ppermute x0 -> x10, starting transfers between devices: none -> 34.7 us  [the longest x5 31.3 us: swap_y(): lax.ppermute(pair, 'dev', [(i, i + 1 if i % 2 == 0 else i - 1) for i in r...]
    all_to_all x2, starting transfers between devices: 19.1 us -> 27.9 us  [exchanged(): came = lax.all_to_all(rows_out.reshape(-1, 1, 128), axis, 0, 0)]
    ppermute x16 -> x6, waiting for transfers between devices: 15.1 us -> 7.38 us  [passed_along(): return lax.ppermute(x, axis, [(i, (i + by) % peers) for i in range(peers)])]
    ppermute x0 -> x10, waiting for transfers between devices: none -> 6.53 us  [the longest x5 6.52 us: swap_y(): lax.ppermute(pair, 'dev', [(i, i + 1 if i % 2 == 0 else i - 1) for i in r...]
    all_to_all x2, waiting for transfers between devices: 9.27 us -> 11.9 us  [exchanged(): came = lax.all_to_all(rows_out.reshape(-1, 1, 128), axis, 0, 0)]
  transfers between devices with their start and end apart: 18 -> 18, of which waited for: 13 -> 12; matrix products, arithmetic and copies ran while one was open for 0% -> 0% of each run, Pallas kernels for 1% -> 1%
where the time goes in v4:
time: 110 us; the launch traced here: 109 us
  starting transfers between devices  72.6 us (66%)
  waiting for transfers between devices  25.8 us (23%)
  Pallas kernels  9.28 us (8%)
  between operations  1.51 us (1%)
    ppermute x5, starting transfers between devices, swap_y(): lax.ppermute(pair, 'dev', [(i, i + 1 if i % 2 == 0 else i - 1) for i in r...  31.3 us
    all_to_all x2, starting transfers between devices, exchanged(): came = lax.all_to_all(rows_out.reshape(-1, 1, 128), axis, 0, 0)  27.9 us
    all_to_all x2, waiting for transfers between devices, exchanged(): came = lax.all_to_all(rows_out.reshape(-1, 1, 128), axis, 0, 0)  11.9 us
    ppermute x6, starting transfers between devices, passed_along(): return lax.ppermute(x, axis, [(i, (i + by) % peers) for i in range(peers)])  10 us
    pallas_call x10, Pallas kernels, call(): pl.pallas_call(kernel, out_shape=outs, in_specs=[pl.BlockSpec(memory_spac...  9.28 us
    ppermute x6, waiting for transfers between devices, passed_along(): return lax.ppermute(x, axis, [(i, (i + by) % peers) for i in range(peers)])  7.38 us
    ppermute x5, waiting for transfers between devices, swap_y(): lax.ppermute(pair, 'dev', [(i, i + 1 if i % 2 == 0 else i - 1) for i in r...  6.52 us
    ppermute x5, starting transfers between devices, swap_y(): lax.ppermute(other, 'dev', [(i, i - 1 if i % 2 == 0 else i + 1) for i in...  3.32 us
  transfers between devices with their start and end apart: 18, of which 12 were waited for; matrix products, arithmetic and copies ran while one was open for 0% of the time, Pallas kernels for 1%

profile of v4, /device:TPU:1, one launch (start us, length us, event | category | flops | bytes accessed | tf_op | source)
XLA Modules:
  0.0 109.1 jit_solution(14748541368279124614)
XLA Ops:
  0.6 0.0 copy-start.1
  1.3 1.3 %shard_map.86 = (f32[2,512,128]{2,1,0:T(8,128)S(1)}, f32[2,64,128]{2,1,0:T(8,128)S(1)}, f32[2,64,128]{2,1,0:T(8,128)S(1)}, f32[72,128]{1,0:T(8,128)S(1)}, f32[72...) custom-call(f32[2]{0:T(128)} %size_x_in.1, f32[1]{0:T(128)S(6)} %copy.15.size_y_in, ...), custom_call_target="tpu_custom_call" | custom-call | tf_op jit(solution)/shard_map/pallas_call | solution.py:511
  2.7 0.7 collective-permute-start
  3.4 6.6 %collective-permute-start.1 = (f32[2,64,128]{2,1,0:T(8,128)S(1)}, f32[2,64,128]{2,1,0:T(8,128)S(1)}, u32[]{:S(2)}, u32[]{:S(2)}) collective-permute-start(f32[2,64,128]{2,1,0:T(8,128)S(1)} %get-tuple-element.45), channel_id=1, source_target_pairs={{0,1},{1,0},{2,3},{3,2},{4,5},{5,4},{6,7},{7,6},{8,9},{9,8},{10,11... | collective-permute-start | bytes 196616 | tf_op jit(solution)/shard_map/ppermute | solution.py:534
  9.9 0.0 collective-permute-done.other.refs_3_
  9.9 1.6 %collective-permute-done.1.pair.refs_4_ = f32[2,64,128]{2,1,0:T(8,128)S(1)} collective-permute-done((f32[2,64,128]{2,1,0:T(8,128)S(1)}, f32[2,64,128]{2,1,0:T(8,128)S(1)}, u32[]{:S(2)}, u32[]{:S(2)}) %collective-permute-start.1) | collective-permute-done | bytes 65568 | tf_op jit(solution)/shard_map/ppermute | solution.py:534
  11.6 2.9 %collective-permute-start.2 = (f32[72,128]{1,0:T(8,128)S(1)}, f32[72,128]{1,0:T(8,128)S(1)}, u32[]{:S(2)}, u32[]{:S(2)}) collective-permute-start(f32[72,128]{1,0:T(8,128)S(1)} %get-tuple-element.48), channel_id=1, source_target_pairs={{0,64},{64,128},{128,192},{192,256},{256,320},{320,384},{384,448},... | collective-permute-start | bytes 110600 | tf_op jit(solution)/shard_map/ppermute | solution.py:19
  14.5 1.9 %collective-permute-start.3 = (f32[72,128]{1,0:T(8,128)S(1)}, f32[72,128]{1,0:T(8,128)S(1)}, u32[]{:S(2)}, u32[]{:S(2)}) collective-permute-start(f32[72,128]{1,0:T(8,128)S(1)} %get-tuple-element.49), channel_id=1, source_target_pairs={{0,448},{64,0},{128,64},{192,128},{256,192},{320,256},{384,320},{4... | collective-permute-start | bytes 110600 | tf_op jit(solution)/shard_map/ppermute | solution.py:19
  16.4 0.7 collective-permute-done.2.refs_5_.refs_6_
  17.1 0.8 collective-permute-done.3.refs_6_.refs_7_
  17.9 0.0 copy-done.1
  17.9 0.0 copy-start
  17.9 1.3 %shard_map.88 = (f32[2,512,128]{2,1,0:T(8,128)S(1)}, f32[2,512,128]{2,1,0:T(8,128)S(1)}, f32[2,64,128]{2,1,0:T(8,128)S(1)}, f32[2,64,128]{2,1,0:T(8,128)S(1)}, f32[8,128]{1,0:T(8,128)S(1)}) custom-call(f32[2,8,8,128]{3,2,1,0:T(8,128)S(1)} %get-tuple-element.41.coef.refs_0_, bf16[4,256,256]{2,1,0:T(8,128)(2,1)S(1)} %copy-done.1, ...), custom_call_target="tpu_custom_call" | custom-call | tf_op jit(solution)/shard_map/pallas_call | solution.py:511
  19.2 0.7 collective-permute-start.4
  19.9 5.4 %collective-permute-start.5 = (f32[2,64,128]{2,1,0:T(8,128)S(1)}, f32[2,64,128]{2,1,0:T(8,128)S(1)}, u32[]{:S(2)}, u32[]{:S(2)}) collective-permute-start(f32[2,64,128]{2,1,0:T(8,128)S(1)} %get-tuple-element.52), channel_id=1, source_target_pairs={{0,1},{1,0},{2,3},{3,2},{4,5},{5,4},{6,7},{7,6},{8,9},{9,8},{10,11... | collective-permute-start | bytes 196616 | tf_op jit(solution)/shard_map/ppermute | solution.py:534
  25.4 0.0 collective-permute-done.4.before
  25.4 1.6 %collective-permute-done.5.after = f32[2,64,128]{2,1,0:T(8,128)S(1)} collective-permute-done((f32[2,64,128]{2,1,0:T(8,128)S(1)}, f32[2,64,128]{2,1,0:T(8,128)S(1)}, u32[]{:S(2)}, u32[]{:S(2)}) %collective-permute-start.5) | collective-permute-done | bytes 65568 | tf_op jit(solution)/shard_map/ppermute | solution.py:534
  27.0 0.0 copy-done
  27.0 0.7 shard_map.89
  27.7 1.3 %collective-permute-start.6 = (f32[128,128]{1,0:T(8,128)S(1)}, f32[128,128]{1,0:T(8,128)S(1)}, u32[]{:S(2)}, u32[]{:S(2)}) collective-permute-start(f32[128,128]{1,0:T(8,128)S(1)} %get-tuple-element.55), channel_id=1, source_target_pairs={{0,64},{64,128},{128,192},{192,256},{256,320},{320,384},{384,448},... | collective-permute-start | bytes 196616 | tf_op jit(solution)/shard_map/ppermute | solution.py:19
  29.0 0.9 collective-permute-start.7
  29.9 0.7 collective-permute-done.6.refs_4_
  30.7 2.0 %collective-permute-done.7.refs_5_ = f32[128,128]{1,0:T(8,128)S(1)} collective-permute-done((f32[128,128]{1,0:T(8,128)S(1)}, f32[128,128]{1,0:T(8,128)S(1)}, u32[]{:S(2)}, u32[]{:S(2)}) %collective-permute-start.7) | collective-permute-done | bytes 65568 | tf_op jit(solution)/shard_map/ppermute | solution.py:19
  32.7 0.5 shard_map.90
  33.2 0.7 collective-permute-start.8
  33.9 7.5 %collective-permute-start.9 = (f32[2,64,128]{2,1,0:T(8,128)S(1)}, f32[2,64,128]{2,1,0:T(8,128)S(1)}, u32[]{:S(2)}, u32[]{:S(2)}) collective-permute-start(f32[2,64,128]{2,1,0:T(8,128)S(1)} %get-tuple-element.59), channel_id=1, source_target_pairs={{0,1},{1,0},{2,3},{3,2},{4,5},{5,4},{6,7},{7,6},{8,9},{9,8},{10,11... | collective-permute-start | bytes 196616 | tf_op jit(solution)/shard_map/ppermute | solution.py:534
  41.4 0.0 collective-permute-done.8.refs_3_
  41.4 1.6 %collective-permute-done.9.refs_4_ = f32[2,64,128]{2,1,0:T(8,128)S(1)} collective-permute-done((f32[2,64,128]{2,1,0:T(8,128)S(1)}, f32[2,64,128]{2,1,0:T(8,128)S(1)}, u32[]{:S(2)}, u32[]{:S(2)}) %collective-permute-start.9) | collective-permute-done | bytes 65568 | tf_op jit(solution)/shard_map/ppermute | solution.py:534
  43.0 1.3 %shard_map.91 = (f32[2,512,128]{2,1,0:T(8,128)S(1)}, f32[2,512,128]{2,1,0:T(8,128)S(1)}, f32[2,64,128]{2,1,0:T(8,128)S(1)}, f32[2,64,128]{2,1,0:T(8,128)S(1)}, f32[8,128]{1,0:T(8,128)S(1)}) custom-call(f32[2,8,8,128]{3,2,1,0:T(8,128)S(1)} %get-tuple-element.41.coef.refs_0_, bf16[4,256,256]{2,1,0:T(8,128)(2,1)S(1)} %copy-done.1, ...), custom_call_target="tpu_custom_call" | custom-call | tf_op jit(solution)/shard_map/pallas_call | solution.py:511
  44.3 0.7 collective-permute-start.10
  45.0 6.5 %collective-permute-start.11 = (f32[2,64,128]{2,1,0:T(8,128)S(1)}, f32[2,64,128]{2,1,0:T(8,128)S(1)}, u32[]{:S(2)}, u32[]{:S(2)}) collective-permute-start(f32[2,64,128]{2,1,0:T(8,128)S(1)} %get-tuple-element.62), channel_id=1, source_target_pairs={{0,1},{1,0},{2,3},{3,2},{4,5},{5,4},{6,7},{7,6},{8,9},{9,8},{10,11... | collective-permute-start | bytes 196616 | tf_op jit(solution)/shard_map/ppermute | solution.py:534
  51.5 0.0 collective-permute-done.10.before
  51.5 1.6 %collective-permute-done.11.after = f32[2,64,128]{2,1,0:T(8,128)S(1)} collective-permute-done((f32[2,64,128]{2,1,0:T(8,128)S(1)}, f32[2,64,128]{2,1,0:T(8,128)S(1)}, u32[]{:S(2)}, u32[]{:S(2)}) %collective-permute-start.11) | collective-permute-done | bytes 65568 | tf_op jit(solution)/shard_map/ppermute | solution.py:534
  53.2 0.7 shard_map.92
  53.9 2.4 %collective-permute-start.12 = (f32[128,128]{1,0:T(8,128)S(1)}, f32[128,128]{1,0:T(8,128)S(1)}, u32[]{:S(2)}, u32[]{:S(2)}) collective-permute-start(f32[128,128]{1,0:T(8,128)S(1)} %get-tuple-element.65), channel_id=1, source_target_pairs={{0,64},{64,128},{128,192},{192,256},{256,320},{320,384},{384,448},... | collective-permute-start | bytes 196616 | tf_op jit(solution)/shard_map/ppermute | solution.py:19
  56.3 0.5 collective-permute-start.13
  56.8 0.8 collective-permute-done.12.refs_4_
  57.6 2.4 %collective-permute-done.13.refs_5_ = f32[128,128]{1,0:T(8,128)S(1)} collective-permute-done((f32[128,128]{1,0:T(8,128)S(1)}, f32[128,128]{1,0:T(8,128)S(1)}, u32[]{:S(2)}, u32[]{:S(2)}) %collective-permute-start.13) | collective-permute-done | bytes 65568 | tf_op jit(solution)/shard_map/ppermute | solution.py:19
  60.0 1.3 %shard_map.93 = (f32[2,512,128]{2,1,0:T(8,128)S(1)}, f32[2,512,128]{2,1,0:T(8,128)S(1)}, f32[2,64,128]{2,1,0:T(8,128)S(1)}, f32[2,64,128]{2,1,0:T(8,128)S(1)}, f32[64,128]{1,0:T(8,128)}) custom-call(f32[2,8,8,128]{3,2,1,0:T(8,128)S(1)} %get-tuple-element.41.coef.refs_0_, bf16[4,256,256]{2,1,0:T(8,128)(2,1)S(1)} %copy-done, ...), custom_call_target="tpu_custom_call" | custom-call | tf_op jit(solution)/shard_map/pallas_call | solution.py:511
  61.2 21.2 %all-to-all-start = ((f32[64,1,128]{2,1,0:T(1,128)}), f32[64,1,128]{2,1,0:T(1,128)S(1)}, u32[]{:S(2)}, u32[]{:S(2)}) async-start(f32[64,1,128]{2,1,0:T(1,128)} %bitcast.4), calls=%async_computation | async-start | bytes 65536 | tf_op jit(solution)/shard_map/all_to_all | solution.py:543
  82.4 0.7 collective-permute-start.14
  83.1 5.3 %collective-permute-start.15 = (f32[2,64,128]{2,1,0:T(8,128)S(1)}, f32[2,64,128]{2,1,0:T(8,128)S(1)}, u32[]{:S(2)}, u32[]{:S(2)}) collective-permute-start(f32[2,64,128]{2,1,0:T(8,128)S(1)} %get-tuple-element.73), channel_id=1, source_target_pairs={{0,1},{1,0},{2,3},{3,2},{4,5},{5,4},{6,7},{7,6},{8,9},{9,8},{10,11... | collective-permute-start | bytes 196616 | tf_op jit(solution)/shard_map/ppermute | solution.py:534
  88.4 7.4 %all-to-all-done = f32[64,1,128]{2,1,0:T(1,128)S(1)} async-done(((f32[64,1,128]{2,1,0:T(1,128)}), f32[64,1,128]{2,1,0:T(1,128)S(1)}, u32[]{:S(2)}, u32[]{:S(2)}) %all-to-all-start) | async-done | bytes 32800 | tf_op jit(solution)/shard_map/all_to_all | solution.py:543
  95.8 0.6 shard_map.94
  96.4 6.7 %all-to-all-start.1 = ((f32[8,1,128]{2,1,0:T(1,128)}), f32[8,1,128]{2,1,0:T(1,128)S(1)}, u32[]{:S(2)}, u32[]{:S(2)}) async-start(f32[8,1,128]{2,1,0:T(1,128)} %bitcast.7), calls=%async_computation.1 | async-start | bytes 8192 | tf_op jit(solution)/shard_map/all_to_all | solution.py:543
  103.1 0.0 collective-permute-done.14.before
  103.1 0.0 collective-permute-done.15.after
  103.1 4.5 %all-to-all-done.1 = f32[8,1,128]{2,1,0:T(1,128)S(1)} async-done(((f32[8,1,128]{2,1,0:T(1,128)}), f32[8,1,128]{2,1,0:T(1,128)S(1)}, u32[]{:S(2)}, u32[]{:S(2)}) %all-to-all-start.1) | async-done | bytes 4128 | tf_op jit(solution)/shard_map/all_to_all | solution.py:543
  107.6 1.5 %shard_map.95 = (f32[2,512,128]{2,1,0:T(8,128)}, f32[2,512,128]{2,1,0:T(8,128)}) custom-call(f32[2,8,8,128]{3,2,1,0:T(8,128)S(1)} %get-tuple-element.41.coef.refs_0_, s32[2,128]{1,0:T(2,128)S(1)} %get-tuple-element.42.orient, f32[8,128]{1,0:T(8,128)S(1)} %bitcast.18, f32[2,512,128]{2,1,0:T(8,128)S(1)} %get-tuple-element.71.last, ...), custom_call_target="tpu_custom_call" | custom-call | tf_op jit(solution)/shard_map/pallas_call | solution.py:511
  (1 shorter events, 0.0 us)
Async XLA Ops:
  0.6 17.3 %copy-start.1 = (bf16[4,256,256]{2,1,0:T(8,128)(2,1)S(1)}, bf16[4,256,256]{2,1,0:T(8,128)(2,1)}, u32[]{:S(2)}) copy-start(bf16[4,256,256]{2,1,0:T(8,128)(2,1)} %constant.4.clone.refs_1_) | copy-start | bytes 1572868
  2.7 7.3 %collective-permute-start = (f32[2,64,128]{2,1,0:T(8,128)S(1)}, f32[2,64,128]{2,1,0:T(8,128)S(1)}, u32[]{:S(2)}, u32[]{:S(2)}) collective-permute-start(f32[2,64,128]{2,1,0:T(8,128)S(1)} %get-tuple-element.44), channel_id=1, source_target_pairs={{1,2},{2,1},{3,4},{4,3},{5,6},{6,5},{7,8},{8,7},{9,10},{10,9},{11,... | collective-permute-start | bytes 196616 | tf_op jit(solution)/shard_map/ppermute | solution.py:533
  3.4 8.2 %collective-permute-start.1 = (f32[2,64,128]{2,1,0:T(8,128)S(1)}, f32[2,64,128]{2,1,0:T(8,128)S(1)}, u32[]{:S(2)}, u32[]{:S(2)}) collective-permute-start(f32[2,64,128]{2,1,0:T(8,128)S(1)} %get-tuple-element.45), channel_id=1, source_target_pairs={{0,1},{1,0},{2,3},{3,2},{4,5},{5,4},{6,7},{7,6},{8,9},{9,8},{10,11... | collective-permute-start | bytes 196616 | tf_op jit(solution)/shard_map/ppermute | solution.py:534
  11.6 5.5 %collective-permute-start.2 = (f32[72,128]{1,0:T(8,128)S(1)}, f32[72,128]{1,0:T(8,128)S(1)}, u32[]{:S(2)}, u32[]{:S(2)}) collective-permute-start(f32[72,128]{1,0:T(8,128)S(1)} %get-tuple-element.48), channel_id=1, source_target_pairs={{0,64},{64,128},{128,192},{192,256},{256,320},{320,384},{384,448},... | collective-permute-start | bytes 110600 | tf_op jit(solution)/shard_map/ppermute | solution.py:19
  14.5 3.4 %collective-permute-start.3 = (f32[72,128]{1,0:T(8,128)S(1)}, f32[72,128]{1,0:T(8,128)S(1)}, u32[]{:S(2)}, u32[]{:S(2)}) collective-permute-start(f32[72,128]{1,0:T(8,128)S(1)} %get-tuple-element.49), channel_id=1, source_target_pairs={{0,448},{64,0},{128,64},{192,128},{256,192},{320,256},{384,320},{4... | collective-permute-start | bytes 110600 | tf_op jit(solution)/shard_map/ppermute | solution.py:19
  17.9 9.1 %copy-start = (bf16[4,256,256]{2,1,0:T(8,128)(2,1)S(1)}, bf16[4,256,256]{2,1,0:T(8,128)(2,1)}, u32[]{:S(2)}) copy-start(bf16[4,256,256]{2,1,0:T(8,128)(2,1)} %constant.5.clone.table.refs_1_) | copy-start | bytes 1572868
  19.2 6.1 %collective-permute-start.4 = (f32[2,64,128]{2,1,0:T(8,128)S(1)}, f32[2,64,128]{2,1,0:T(8,128)S(1)}, u32[]{:S(2)}, u32[]{:S(2)}) collective-permute-start(f32[2,64,128]{2,1,0:T(8,128)S(1)} %get-tuple-element.51), channel_id=1, source_target_pairs={{1,2},{2,1},{3,4},{4,3},{5,6},{6,5},{7,8},{8,7},{9,10},{10,9},{11,... | collective-permute-start | bytes 196616 | tf_op jit(solution)/shard_map/ppermute | solution.py:533
  19.9 7.1 %collective-permute-start.5 = (f32[2,64,128]{2,1,0:T(8,128)S(1)}, f32[2,64,128]{2,1,0:T(8,128)S(1)}, u32[]{:S(2)}, u32[]{:S(2)}) collective-permute-start(f32[2,64,128]{2,1,0:T(8,128)S(1)} %get-tuple-element.52), channel_id=1, source_target_pairs={{0,1},{1,0},{2,3},{3,2},{4,5},{5,4},{6,7},{7,6},{8,9},{9,8},{10,11... | collective-permute-start | bytes 196616 | tf_op jit(solution)/shard_map/ppermute | solution.py:534
  27.7 2.9 %collective-permute-start.6 = (f32[128,128]{1,0:T(8,128)S(1)}, f32[128,128]{1,0:T(8,128)S(1)}, u32[]{:S(2)}, u32[]{:S(2)}) collective-permute-start(f32[128,128]{1,0:T(8,128)S(1)} %get-tuple-element.55), channel_id=1, source_target_pairs={{0,64},{64,128},{128,192},{192,256},{256,320},{320,384},{384,448},... | collective-permute-start | bytes 196616 | tf_op jit(solution)/shard_map/ppermute | solution.py:19
  29.0 3.7 %collective-permute-start.7 = (f32[128,128]{1,0:T(8,128)S(1)}, f32[128,128]{1,0:T(8,128)S(1)}, u32[]{:S(2)}, u32[]{:S(2)}) collective-permute-start(f32[128,128]{1,0:T(8,128)S(1)} %get-tuple-element.56), channel_id=1, source_target_pairs={{0,448},{64,0},{128,64},{192,128},{256,192},{320,256},{384,320},{4... | collective-permute-start | bytes 196616 | tf_op jit(solution)/shard_map/ppermute | solution.py:19
  33.2 8.1 %collective-permute-start.8 = (f32[2,64,128]{2,1,0:T(8,128)S(1)}, f32[2,64,128]{2,1,0:T(8,128)S(1)}, u32[]{:S(2)}, u32[]{:S(2)}) collective-permute-start(f32[2,64,128]{2,1,0:T(8,128)S(1)} %get-tuple-element.58), channel_id=1, source_target_pairs={{1,2},{2,1},{3,4},{4,3},{5,6},{6,5},{7,8},{8,7},{9,10},{10,9},{11,... | collective-permute-start | bytes 196616 | tf_op jit(solution)/shard_map/ppermute | solution.py:533
  33.9 9.1 %collective-permute-start.9 = (f32[2,64,128]{2,1,0:T(8,128)S(1)}, f32[2,64,128]{2,1,0:T(8,128)S(1)}, u32[]{:S(2)}, u32[]{:S(2)}) collective-permute-start(f32[2,64,128]{2,1,0:T(8,128)S(1)} %get-tuple-element.59), channel_id=1, source_target_pairs={{0,1},{1,0},{2,3},{3,2},{4,5},{5,4},{6,7},{7,6},{8,9},{9,8},{10,11... | collective-permute-start | bytes 196616 | tf_op jit(solution)/shard_map/ppermute | solution.py:534
  44.3 7.2 %collective-permute-start.10 = (f32[2,64,128]{2,1,0:T(8,128)S(1)}, f32[2,64,128]{2,1,0:T(8,128)S(1)}, u32[]{:S(2)}, u32[]{:S(2)}) collective-permute-start(f32[2,64,128]{2,1,0:T(8,128)S(1)} %get-tuple-element.61), channel_id=1, source_target_pairs={{1,2},{2,1},{3,4},{4,3},{5,6},{6,5},{7,8},{8,7},{9,10},{10,9},{11,... | collective-permute-start | bytes 196616 | tf_op jit(solution)/shard_map/ppermute | solution.py:533
  45.0 8.1 %collective-permute-start.11 = (f32[2,64,128]{2,1,0:T(8,128)S(1)}, f32[2,64,128]{2,1,0:T(8,128)S(1)}, u32[]{:S(2)}, u32[]{:S(2)}) collective-permute-start(f32[2,64,128]{2,1,0:T(8,128)S(1)} %get-tuple-element.62), channel_id=1, source_target_pairs={{0,1},{1,0},{2,3},{3,2},{4,5},{5,4},{6,7},{7,6},{8,9},{9,8},{10,11... | collective-permute-start | bytes 196616 | tf_op jit(solution)/shard_map/ppermute | solution.py:534
  53.9 3.7 %collective-permute-start.12 = (f32[128,128]{1,0:T(8,128)S(1)}, f32[128,128]{1,0:T(8,128)S(1)}, u32[]{:S(2)}, u32[]{:S(2)}) collective-permute-start(f32[128,128]{1,0:T(8,128)S(1)} %get-tuple-element.65), channel_id=1, source_target_pairs={{0,64},{64,128},{128,192},{192,256},{256,320},{320,384},{384,448},... | collective-permute-start | bytes 196616 | tf_op jit(solution)/shard_map/ppermute | solution.py:19
  56.3 3.7 %collective-permute-start.13 = (f32[128,128]{1,0:T(8,128)S(1)}, f32[128,128]{1,0:T(8,128)S(1)}, u32[]{:S(2)}, u32[]{:S(2)}) collective-permute-start(f32[128,128]{1,0:T(8,128)S(1)} %get-tuple-element.66), channel_id=1, source_target_pairs={{0,448},{64,0},{128,64},{192,128},{256,192},{320,256},{384,320},{4... | collective-permute-start | bytes 196616 | tf_op jit(solution)/shard_map/ppermute | solution.py:19
  61.2 34.5 %all-to-all-start = ((f32[64,1,128]{2,1,0:T(1,128)}), f32[64,1,128]{2,1,0:T(1,128)S(1)}, u32[]{:S(2)}, u32[]{:S(2)}) async-start(f32[64,1,128]{2,1,0:T(1,128)} %bitcast.4), calls=%async_computation | async-start | bytes 65536 | tf_op jit(solution)/shard_map/all_to_all | solution.py:543
  82.4 20.7 %collective-permute-start.14 = (f32[2,64,128]{2,1,0:T(8,128)S(1)}, f32[2,64,128]{2,1,0:T(8,128)S(1)}, u32[]{:S(2)}, u32[]{:S(2)}) collective-permute-start(f32[2,64,128]{2,1,0:T(8,128)S(1)} %get-tuple-element.72), channel_id=1, source_target_pairs={{1,2},{2,1},{3,4},{4,3},{5,6},{6,5},{7,8},{8,7},{9,10},{10,9},{11,... | collective-permute-start | bytes 196616 | tf_op jit(solution)/shard_map/ppermute | solution.py:533
  83.1 20.1 %collective-permute-start.15 = (f32[2,64,128]{2,1,0:T(8,128)S(1)}, f32[2,64,128]{2,1,0:T(8,128)S(1)}, u32[]{:S(2)}, u32[]{:S(2)}) collective-permute-start(f32[2,64,128]{2,1,0:T(8,128)S(1)} %get-tuple-element.73), channel_id=1, source_target_pairs={{0,1},{1,0},{2,3},{3,2},{4,5},{5,4},{6,7},{7,6},{8,9},{9,8},{10,11... | collective-permute-start | bytes 196616 | tf_op jit(solution)/shard_map/ppermute | solution.py:534
  96.4 11.3 %all-to-all-start.1 = ((f32[8,1,128]{2,1,0:T(1,128)}), f32[8,1,128]{2,1,0:T(1,128)S(1)}, u32[]{:S(2)}, u32[]{:S(2)}) async-start(f32[8,1,128]{2,1,0:T(1,128)} %bitcast.7), calls=%async_computation.1 | async-start | bytes 8192 | tf_op jit(solution)/shard_map/all_to_all | solution.py:543

commit v5 on v4

--- a/solution.py
+++ b/solution.py
@@ -254,8 +254,8 @@
     return jnp.broadcast_to(row, (8, 128))
 
 
-def reversed_points(src, mid, out, orient):
-    for x in range(2):
+def reversed_points(src, mid, out, orient, columns=(0, 1)):
+    for x in columns:
         code = over_sublanes(orient[x : x + 1, :])
         flip_i, flip_j, flip_k = (code & 1) != 0, (code & 2) != 0, (code & 4) != 0
         for i in range(4):
@@ -279,15 +279,16 @@
 def start_kernel(ends, size_x_in, size_y_in, load_in, orient_in, size_z_in, *refs):
     field, y_low, y_high, x_low, x_high, coef, orient, mid, load, length_ref, x_ref, y_ref, ready = refs
     copies = [
-        pltpu.make_async_copy(load_in, load, ready.at[0]),
+        pltpu.make_async_copy(load_in.at[0], load.at[0], ready.at[0]),
         pltpu.make_async_copy(orient_in, orient, ready.at[1]),
         pltpu.make_async_copy(size_z_in, length_ref, ready.at[2]),
         pltpu.make_async_copy(size_x_in, x_ref, ready.at[3]),
         pltpu.make_async_copy(size_y_in, y_ref, ready.at[4]),
+        pltpu.make_async_copy(load_in.at[1], load.at[1], ready.at[5]),
     ]
     for copy in copies:
         copy.start()
-    for copy in copies[1:]:
+    for copy in copies[1:5]:
         copy.wait()
     node, dev = lax.axis_index("node"), lax.axis_index("dev")
     inside = [jnp.where(at_end, 0.0, 1.0).astype(F32) for at_end in (node == 0, node == ends[0], dev == 0, dev == ends[1])]
@@ -309,7 +310,9 @@
         coef[x, 5] = weight_k
         coef[x, 6] = jnp.full((8, 128), jnp.where(dev % 2 == 1, 1.0, 0.0), F32)
     copies[0].wait()
-    reversed_points(load, mid, field, orient)
+    reversed_points(load, mid, field, orient, (0,))
+    copies[5].wait()
+    reversed_points(load, mid, field, orient, (1,))
     z_summed(field)
     x_joined(field)
     y_faces(field, y_low, y_high, coef)
@@ -481,7 +484,7 @@
         out[eight(n), :] = row
 
 
-def end_kernel(coef, orient, sums, last, before, after, load, first, image, second, answer, rest, one, two):
+def end_kernel(coef, orient, sums, last, before, after, load, first, image, second, answer, rest, one, two, sent):
     lane = lax.broadcasted_iota(jnp.int32, (8, 128), 1)
     row = jnp.sum(sums[...], axis=0, keepdims=True)
     dots = [jnp.full((8, 128), jnp.sum(jnp.where(lane[0:1, :] // 32 == n, row, 0.0)), F32) for n in range(4)]
@@ -492,28 +495,38 @@
     step = energy / curve
     on_first = alpha + step * keep
     on_second = step * alpha
-    for x in range(2):
+    copies = []
+    for x in range(2):
+        for i in range(8):
+            for j in range(8):
+                at = rows(i, j)
+                one[x, at, :] = on_first * first[x, at, :] - on_second * second[x, at, :]
+        reversed_points(one, one, one, orient, (x,))
+        copies.append(pltpu.make_async_copy(one.at[x], answer.at[x], sent.at[x, 0]))
+        copies[-1].start()
         for i in range(8):
             for j in range(8):
                 at = rows(i, j)
                 value = y_joined(last[x, at, :], x, i, j, before, after, coef)
-                one[x, at, :] = on_first * first[x, at, :] - on_second * second[x, at, :]
                 two[x, at, :] = load[x, at, :] - on_first * image[x, at, :] + on_second * value
-    reversed_points(one, one, answer, orient)
-    reversed_points(two, two, rest, orient)
+        reversed_points(two, two, two, orient, (x,))
+        copies.append(pltpu.make_async_copy(two.at[x], rest.at[x], sent.at[x, 1]))
+        copies[-1].start()
+    for copy in copies:
+        copy.wait()
 
 
 def f32(*shape):
     return jax.ShapeDtypeStruct(shape, F32)
 
 
-def call(kernel, outs, scratch, *args, spaces=(), room=24):
+def call(kernel, outs, scratch, *args, spaces=(), room=24, out_space=pltpu.VMEM):
     return pl.pallas_call(
         kernel,
         out_shape=outs,
         in_specs=[pl.BlockSpec(memory_space=space) for space in spaces]
         + [pl.BlockSpec(memory_space=pltpu.VMEM)] * (len(args) - len(spaces)),
-        out_specs=jax.tree.map(lambda _: pl.BlockSpec(memory_space=pltpu.VMEM), outs),
+        out_specs=jax.tree.map(lambda _: pl.BlockSpec(memory_space=out_space), outs),
         scratch_shapes=scratch,
         compiler_params=pltpu.CompilerParams(vmem_limit_bytes=room * 1024 * 1024),
     )(*args)
@@ -557,7 +570,7 @@
             pltpu.VMEM((1, 128), F32),
             pltpu.SMEM((2,), F32),
             pltpu.SMEM((1,), F32),
-            pltpu.SemaphoreType.DMA((5,)),
+            pltpu.SemaphoreType.DMA((6,)),
         ],
         kept_in_hbm(size_x), size_y,
         *map(kept_in_hbm, (element_load.reshape(2, 512, 128), orient.reshape(2, 128), size_z.reshape(1, 128))),
@@ -602,8 +615,9 @@
     answer, rest = call(
         end_kernel,
         [FIELD, FIELD],
-        [pltpu.VMEM((2, 512, 128), F32)] * 2,
+        [pltpu.VMEM((2, 512, 128), F32)] * 2 + [pltpu.SemaphoreType.DMA((2, 2))],
         coef, orient, row, out, before, after, load, first, image, second,
+        out_space=pltpu.HBM,
     )
     return answer.reshape(element_load.shape), rest.reshape(element_load.shape)
 

time: 110 us -> 109 us (level)
  no operation moved by 1% of the time
where the time goes in v5:
time: 109 us
  starting transfers between devices  72.6 us (67%)
  waiting for transfers between devices  25.8 us (24%)
  Pallas kernels  9.09 us (8%)
  between operations  1.51 us (1%)
    ppermute x5, starting transfers between devices, swap_y(): lax.ppermute(pair, 'dev', [(i, i + 1 if i % 2 == 0 else i - 1) for i in r...  31.3 us
    all_to_all x2, starting transfers between devices, exchanged(): came = lax.all_to_all(rows_out.reshape(-1, 1, 128), axis, 0, 0)  27.9 us
    all_to_all x2, waiting for transfers between devices, exchanged(): came = lax.all_to_all(rows_out.reshape(-1, 1, 128), axis, 0, 0)  11.9 us
    ppermute x6, starting transfers between devices, passed_along(): return lax.ppermute(x, axis, [(i, (i + by) % peers) for i in range(peers)])  10 us
    pallas_call x10, Pallas kernels, call(): pl.pallas_call(kernel, out_shape=outs, in_specs=[pl.BlockSpec(memory_spac...  9.09 us
    ppermute x6, waiting for transfers between devices, passed_along(): return lax.ppermute(x, axis, [(i, (i + by) % peers) for i in range(peers)])  7.38 us
    ppermute x5, waiting for transfers between devices, swap_y(): lax.ppermute(pair, 'dev', [(i, i + 1 if i % 2 == 0 else i - 1) for i in r...  6.52 us
    ppermute x5, starting transfers between devices, swap_y(): lax.ppermute(other, 'dev', [(i, i - 1 if i % 2 == 0 else i + 1) for i in...  3.32 us
  transfers between devices with their start and end apart: 18, of which 12 were waited for; matrix products, arithmetic and copies ran while one was open for 0% of the time, Pallas kernels for 1%

profile of v5, /device:TPU:1, one launch (start us, length us, event | category | flops | bytes accessed | tf_op | source)
XLA Modules:
  0.0 108.9 jit_solution(14548825702207926519)
XLA Ops:
  0.6 0.0 copy-start.1
  1.3 1.3 %shard_map.86 = (f32[2,512,128]{2,1,0:T(8,128)S(1)}, f32[2,64,128]{2,1,0:T(8,128)S(1)}, f32[2,64,128]{2,1,0:T(8,128)S(1)}, f32[72,128]{1,0:T(8,128)S(1)}, f32[72...) custom-call(f32[2]{0:T(128)} %size_x_in.1, f32[1]{0:T(128)S(6)} %copy.15.size_y_in, ...), custom_call_target="tpu_custom_call" | custom-call | tf_op jit(solution)/shard_map/pallas_call | solution.py:524
  2.6 0.7 collective-permute-start
  3.3 6.6 %collective-permute-start.1 = (f32[2,64,128]{2,1,0:T(8,128)S(1)}, f32[2,64,128]{2,1,0:T(8,128)S(1)}, u32[]{:S(2)}, u32[]{:S(2)}) collective-permute-start(f32[2,64,128]{2,1,0:T(8,128)S(1)} %get-tuple-element.45), channel_id=1, source_target_pairs={{0,1},{1,0},{2,3},{3,2},{4,5},{5,4},{6,7},{7,6},{8,9},{9,8},{10,11... | collective-permute-start | bytes 196616 | tf_op jit(solution)/shard_map/ppermute | solution.py:547
  9.9 0.0 collective-permute-done.other.refs_3_
  9.9 1.6 %collective-permute-done.1.pair.refs_4_ = f32[2,64,128]{2,1,0:T(8,128)S(1)} collective-permute-done((f32[2,64,128]{2,1,0:T(8,128)S(1)}, f32[2,64,128]{2,1,0:T(8,128)S(1)}, u32[]{:S(2)}, u32[]{:S(2)}) %collective-permute-start.1) | collective-permute-done | bytes 65568 | tf_op jit(solution)/shard_map/ppermute | solution.py:547
  11.5 2.9 %collective-permute-start.2 = (f32[72,128]{1,0:T(8,128)S(1)}, f32[72,128]{1,0:T(8,128)S(1)}, u32[]{:S(2)}, u32[]{:S(2)}) collective-permute-start(f32[72,128]{1,0:T(8,128)S(1)} %get-tuple-element.48), channel_id=1, source_target_pairs={{0,64},{64,128},{128,192},{192,256},{256,320},{320,384},{384,448},... | collective-permute-start | bytes 110600 | tf_op jit(solution)/shard_map/ppermute | solution.py:19
  14.5 1.9 %collective-permute-start.3 = (f32[72,128]{1,0:T(8,128)S(1)}, f32[72,128]{1,0:T(8,128)S(1)}, u32[]{:S(2)}, u32[]{:S(2)}) collective-permute-start(f32[72,128]{1,0:T(8,128)S(1)} %get-tuple-element.49), channel_id=1, source_target_pairs={{0,448},{64,0},{128,64},{192,128},{256,192},{320,256},{384,320},{4... | collective-permute-start | bytes 110600 | tf_op jit(solution)/shard_map/ppermute | solution.py:19
  16.4 0.7 collective-permute-done.2.refs_5_.refs_6_
  17.1 0.8 collective-permute-done.3.refs_6_.refs_7_
  17.9 0.0 copy-done.1
  17.9 0.0 copy-start
  17.9 1.3 %shard_map.88 = (f32[2,512,128]{2,1,0:T(8,128)S(1)}, f32[2,512,128]{2,1,0:T(8,128)S(1)}, f32[2,64,128]{2,1,0:T(8,128)S(1)}, f32[2,64,128]{2,1,0:T(8,128)S(1)}, f32[8,128]{1,0:T(8,128)S(1)}) custom-call(f32[2,8,8,128]{3,2,1,0:T(8,128)S(1)} %get-tuple-element.41.coef.refs_0_, bf16[4,256,256]{2,1,0:T(8,128)(2,1)S(1)} %copy-done.1, ...), custom_call_target="tpu_custom_call" | custom-call | tf_op jit(solution)/shard_map/pallas_call | solution.py:524
  19.2 0.7 collective-permute-start.4
  19.9 5.5 %collective-permute-start.5 = (f32[2,64,128]{2,1,0:T(8,128)S(1)}, f32[2,64,128]{2,1,0:T(8,128)S(1)}, u32[]{:S(2)}, u32[]{:S(2)}) collective-permute-start(f32[2,64,128]{2,1,0:T(8,128)S(1)} %get-tuple-element.52), channel_id=1, source_target_pairs={{0,1},{1,0},{2,3},{3,2},{4,5},{5,4},{6,7},{7,6},{8,9},{9,8},{10,11... | collective-permute-start | bytes 196616 | tf_op jit(solution)/shard_map/ppermute | solution.py:547
  25.3 0.0 collective-permute-done.4.before
  25.3 1.6 %collective-permute-done.5.after = f32[2,64,128]{2,1,0:T(8,128)S(1)} collective-permute-done((f32[2,64,128]{2,1,0:T(8,128)S(1)}, f32[2,64,128]{2,1,0:T(8,128)S(1)}, u32[]{:S(2)}, u32[]{:S(2)}) %collective-permute-start.5) | collective-permute-done | bytes 65568 | tf_op jit(solution)/shard_map/ppermute | solution.py:547
  27.0 0.0 copy-done
  27.0 0.7 shard_map.89
  27.7 1.3 %collective-permute-start.6 = (f32[128,128]{1,0:T(8,128)S(1)}, f32[128,128]{1,0:T(8,128)S(1)}, u32[]{:S(2)}, u32[]{:S(2)}) collective-permute-start(f32[128,128]{1,0:T(8,128)S(1)} %get-tuple-element.55), channel_id=1, source_target_pairs={{0,64},{64,128},{128,192},{192,256},{256,320},{320,384},{384,448},... | collective-permute-start | bytes 196616 | tf_op jit(solution)/shard_map/ppermute | solution.py:19
  29.0 0.9 collective-permute-start.7
  29.9 0.7 collective-permute-done.6.refs_4_
  30.6 2.1 %collective-permute-done.7.refs_5_ = f32[128,128]{1,0:T(8,128)S(1)} collective-permute-done((f32[128,128]{1,0:T(8,128)S(1)}, f32[128,128]{1,0:T(8,128)S(1)}, u32[]{:S(2)}, u32[]{:S(2)}) %collective-permute-start.7) | collective-permute-done | bytes 65568 | tf_op jit(solution)/shard_map/ppermute | solution.py:19
  32.7 0.5 shard_map.90
  33.2 0.7 collective-permute-start.8
  33.9 7.5 %collective-permute-start.9 = (f32[2,64,128]{2,1,0:T(8,128)S(1)}, f32[2,64,128]{2,1,0:T(8,128)S(1)}, u32[]{:S(2)}, u32[]{:S(2)}) collective-permute-start(f32[2,64,128]{2,1,0:T(8,128)S(1)} %get-tuple-element.59), channel_id=1, source_target_pairs={{0,1},{1,0},{2,3},{3,2},{4,5},{5,4},{6,7},{7,6},{8,9},{9,8},{10,11... | collective-permute-start | bytes 196616 | tf_op jit(solution)/shard_map/ppermute | solution.py:547
  41.3 0.0 collective-permute-done.8.refs_3_
  41.3 1.6 %collective-permute-done.9.refs_4_ = f32[2,64,128]{2,1,0:T(8,128)S(1)} collective-permute-done((f32[2,64,128]{2,1,0:T(8,128)S(1)}, f32[2,64,128]{2,1,0:T(8,128)S(1)}, u32[]{:S(2)}, u32[]{:S(2)}) %collective-permute-start.9) | collective-permute-done | bytes 65568 | tf_op jit(solution)/shard_map/ppermute | solution.py:547
  43.0 1.3 %shard_map.91 = (f32[2,512,128]{2,1,0:T(8,128)S(1)}, f32[2,512,128]{2,1,0:T(8,128)S(1)}, f32[2,64,128]{2,1,0:T(8,128)S(1)}, f32[2,64,128]{2,1,0:T(8,128)S(1)}, f32[8,128]{1,0:T(8,128)S(1)}) custom-call(f32[2,8,8,128]{3,2,1,0:T(8,128)S(1)} %get-tuple-element.41.coef.refs_0_, bf16[4,256,256]{2,1,0:T(8,128)(2,1)S(1)} %copy-done.1, ...), custom_call_target="tpu_custom_call" | custom-call | tf_op jit(solution)/shard_map/pallas_call | solution.py:524
  44.3 0.7 collective-permute-start.10
  45.0 6.5 %collective-permute-start.11 = (f32[2,64,128]{2,1,0:T(8,128)S(1)}, f32[2,64,128]{2,1,0:T(8,128)S(1)}, u32[]{:S(2)}, u32[]{:S(2)}) collective-permute-start(f32[2,64,128]{2,1,0:T(8,128)S(1)} %get-tuple-element.62), channel_id=1, source_target_pairs={{0,1},{1,0},{2,3},{3,2},{4,5},{5,4},{6,7},{7,6},{8,9},{9,8},{10,11... | collective-permute-start | bytes 196616 | tf_op jit(solution)/shard_map/ppermute | solution.py:547
  51.5 0.0 collective-permute-done.10.before
  51.5 1.6 %collective-permute-done.11.after = f32[2,64,128]{2,1,0:T(8,128)S(1)} collective-permute-done((f32[2,64,128]{2,1,0:T(8,128)S(1)}, f32[2,64,128]{2,1,0:T(8,128)S(1)}, u32[]{:S(2)}, u32[]{:S(2)}) %collective-permute-start.11) | collective-permute-done | bytes 65568 | tf_op jit(solution)/shard_map/ppermute | solution.py:547
  53.1 0.7 shard_map.92
  53.8 2.4 %collective-permute-start.12 = (f32[128,128]{1,0:T(8,128)S(1)}, f32[128,128]{1,0:T(8,128)S(1)}, u32[]{:S(2)}, u32[]{:S(2)}) collective-permute-start(f32[128,128]{1,0:T(8,128)S(1)} %get-tuple-element.65), channel_id=1, source_target_pairs={{0,64},{64,128},{128,192},{192,256},{256,320},{320,384},{384,448},... | collective-permute-start | bytes 196616 | tf_op jit(solution)/shard_map/ppermute | solution.py:19
  56.2 0.6 collective-permute-start.13
  56.8 0.8 collective-permute-done.12.refs_4_
  57.6 2.4 %collective-permute-done.13.refs_5_ = f32[128,128]{1,0:T(8,128)S(1)} collective-permute-done((f32[128,128]{1,0:T(8,128)S(1)}, f32[128,128]{1,0:T(8,128)S(1)}, u32[]{:S(2)}, u32[]{:S(2)}) %collective-permute-start.13) | collective-permute-done | bytes 65568 | tf_op jit(solution)/shard_map/ppermute | solution.py:19
  59.9 1.3 %shard_map.93 = (f32[2,512,128]{2,1,0:T(8,128)S(1)}, f32[2,512,128]{2,1,0:T(8,128)S(1)}, f32[2,64,128]{2,1,0:T(8,128)S(1)}, f32[2,64,128]{2,1,0:T(8,128)S(1)}, f32[64,128]{1,0:T(8,128)}) custom-call(f32[2,8,8,128]{3,2,1,0:T(8,128)S(1)} %get-tuple-element.41.coef.refs_0_, bf16[4,256,256]{2,1,0:T(8,128)(2,1)S(1)} %copy-done, ...), custom_call_target="tpu_custom_call" | custom-call | tf_op jit(solution)/shard_map/pallas_call | solution.py:524
  61.2 21.3 %all-to-all-start = ((f32[64,1,128]{2,1,0:T(1,128)}), f32[64,1,128]{2,1,0:T(1,128)S(1)}, u32[]{:S(2)}, u32[]{:S(2)}) async-start(f32[64,1,128]{2,1,0:T(1,128)} %bitcast.4), calls=%async_computation | async-start | bytes 65536 | tf_op jit(solution)/shard_map/all_to_all | solution.py:556
  82.5 0.7 collective-permute-start.14
  83.2 5.3 %collective-permute-start.15 = (f32[2,64,128]{2,1,0:T(8,128)S(1)}, f32[2,64,128]{2,1,0:T(8,128)S(1)}, u32[]{:S(2)}, u32[]{:S(2)}) collective-permute-start(f32[2,64,128]{2,1,0:T(8,128)S(1)} %get-tuple-element.73), channel_id=1, source_target_pairs={{0,1},{1,0},{2,3},{3,2},{4,5},{5,4},{6,7},{7,6},{8,9},{9,8},{10,11... | collective-permute-start | bytes 196616 | tf_op jit(solution)/shard_map/ppermute | solution.py:547
  88.6 7.4 %all-to-all-done = f32[64,1,128]{2,1,0:T(1,128)S(1)} async-done(((f32[64,1,128]{2,1,0:T(1,128)}), f32[64,1,128]{2,1,0:T(1,128)S(1)}, u32[]{:S(2)}, u32[]{:S(2)}) %all-to-all-start) | async-done | bytes 32800 | tf_op jit(solution)/shard_map/all_to_all | solution.py:556
  95.9 0.6 shard_map.94
  96.5 6.6 %all-to-all-start.1 = ((f32[8,1,128]{2,1,0:T(1,128)}), f32[8,1,128]{2,1,0:T(1,128)S(1)}, u32[]{:S(2)}, u32[]{:S(2)}) async-start(f32[8,1,128]{2,1,0:T(1,128)} %bitcast.7), calls=%async_computation.1 | async-start | bytes 8192 | tf_op jit(solution)/shard_map/all_to_all | solution.py:556
  103.1 0.0 collective-permute-done.14.before
  103.1 0.0 collective-permute-done.15.after
  103.1 4.5 %all-to-all-done.1 = f32[8,1,128]{2,1,0:T(1,128)S(1)} async-done(((f32[8,1,128]{2,1,0:T(1,128)}), f32[8,1,128]{2,1,0:T(1,128)S(1)}, u32[]{:S(2)}, u32[]{:S(2)}) %all-to-all-start.1) | async-done | bytes 4128 | tf_op jit(solution)/shard_map/all_to_all | solution.py:556
  107.6 1.3 %shard_map.95 = (f32[2,512,128]{2,1,0:T(8,128)}, f32[2,512,128]{2,1,0:T(8,128)}) custom-call(f32[2,8,8,128]{3,2,1,0:T(8,128)S(1)} %get-tuple-element.41.coef.refs_0_, s32[2,128]{1,0:T(2,128)S(1)} %get-tuple-element.42.orient, f32[8,128]{1,0:T(8,128)S(1)} %bitcast.18, f32[2,512,128]{2,1,0:T(8,128)S(1)} %get-tuple-element.71.last, ...), custom_call_target="tpu_custom_call" | custom-call | tf_op jit(solution)/shard_map/pallas_call | solution.py:524
  (1 shorter events, 0.0 us)
Async XLA Ops:
  0.6 17.2 %copy-start.1 = (bf16[4,256,256]{2,1,0:T(8,128)(2,1)S(1)}, bf16[4,256,256]{2,1,0:T(8,128)(2,1)}, u32[]{:S(2)}) copy-start(bf16[4,256,256]{2,1,0:T(8,128)(2,1)} %constant.4.clone.refs_1_) | copy-start | bytes 1572868
  2.6 7.3 %collective-permute-start = (f32[2,64,128]{2,1,0:T(8,128)S(1)}, f32[2,64,128]{2,1,0:T(8,128)S(1)}, u32[]{:S(2)}, u32[]{:S(2)}) collective-permute-start(f32[2,64,128]{2,1,0:T(8,128)S(1)} %get-tuple-element.44), channel_id=1, source_target_pairs={{1,2},{2,1},{3,4},{4,3},{5,6},{6,5},{7,8},{8,7},{9,10},{10,9},{11,... | collective-permute-start | bytes 196616 | tf_op jit(solution)/shard_map/ppermute | solution.py:546
  3.3 8.2 %collective-permute-start.1 = (f32[2,64,128]{2,1,0:T(8,128)S(1)}, f32[2,64,128]{2,1,0:T(8,128)S(1)}, u32[]{:S(2)}, u32[]{:S(2)}) collective-permute-start(f32[2,64,128]{2,1,0:T(8,128)S(1)} %get-tuple-element.45), channel_id=1, source_target_pairs={{0,1},{1,0},{2,3},{3,2},{4,5},{5,4},{6,7},{7,6},{8,9},{9,8},{10,11... | collective-permute-start | bytes 196616 | tf_op jit(solution)/shard_map/ppermute | solution.py:547
  11.5 5.5 %collective-permute-start.2 = (f32[72,128]{1,0:T(8,128)S(1)}, f32[72,128]{1,0:T(8,128)S(1)}, u32[]{:S(2)}, u32[]{:S(2)}) collective-permute-start(f32[72,128]{1,0:T(8,128)S(1)} %get-tuple-element.48), channel_id=1, source_target_pairs={{0,64},{64,128},{128,192},{192,256},{256,320},{320,384},{384,448},... | collective-permute-start | bytes 110600 | tf_op jit(solution)/shard_map/ppermute | solution.py:19
  14.5 3.4 %collective-permute-start.3 = (f32[72,128]{1,0:T(8,128)S(1)}, f32[72,128]{1,0:T(8,128)S(1)}, u32[]{:S(2)}, u32[]{:S(2)}) collective-permute-start(f32[72,128]{1,0:T(8,128)S(1)} %get-tuple-element.49), channel_id=1, source_target_pairs={{0,448},{64,0},{128,64},{192,128},{256,192},{320,256},{384,320},{4... | collective-permute-start | bytes 110600 | tf_op jit(solution)/shard_map/ppermute | solution.py:19
  17.9 9.1 %copy-start = (bf16[4,256,256]{2,1,0:T(8,128)(2,1)S(1)}, bf16[4,256,256]{2,1,0:T(8,128)(2,1)}, u32[]{:S(2)}) copy-start(bf16[4,256,256]{2,1,0:T(8,128)(2,1)} %constant.5.clone.table.refs_1_) | copy-start | bytes 1572868
  19.2 6.1 %collective-permute-start.4 = (f32[2,64,128]{2,1,0:T(8,128)S(1)}, f32[2,64,128]{2,1,0:T(8,128)S(1)}, u32[]{:S(2)}, u32[]{:S(2)}) collective-permute-start(f32[2,64,128]{2,1,0:T(8,128)S(1)} %get-tuple-element.51), channel_id=1, source_target_pairs={{1,2},{2,1},{3,4},{4,3},{5,6},{6,5},{7,8},{8,7},{9,10},{10,9},{11,... | collective-permute-start | bytes 196616 | tf_op jit(solution)/shard_map/ppermute | solution.py:546
  19.9 7.1 %collective-permute-start.5 = (f32[2,64,128]{2,1,0:T(8,128)S(1)}, f32[2,64,128]{2,1,0:T(8,128)S(1)}, u32[]{:S(2)}, u32[]{:S(2)}) collective-permute-start(f32[2,64,128]{2,1,0:T(8,128)S(1)} %get-tuple-element.52), channel_id=1, source_target_pairs={{0,1},{1,0},{2,3},{3,2},{4,5},{5,4},{6,7},{7,6},{8,9},{9,8},{10,11... | collective-permute-start | bytes 196616 | tf_op jit(solution)/shard_map/ppermute | solution.py:547
  27.7 2.9 %collective-permute-start.6 = (f32[128,128]{1,0:T(8,128)S(1)}, f32[128,128]{1,0:T(8,128)S(1)}, u32[]{:S(2)}, u32[]{:S(2)}) collective-permute-start(f32[128,128]{1,0:T(8,128)S(1)} %get-tuple-element.55), channel_id=1, source_target_pairs={{0,64},{64,128},{128,192},{192,256},{256,320},{320,384},{384,448},... | collective-permute-start | bytes 196616 | tf_op jit(solution)/shard_map/ppermute | solution.py:19
  29.0 3.7 %collective-permute-start.7 = (f32[128,128]{1,0:T(8,128)S(1)}, f32[128,128]{1,0:T(8,128)S(1)}, u32[]{:S(2)}, u32[]{:S(2)}) collective-permute-start(f32[128,128]{1,0:T(8,128)S(1)} %get-tuple-element.56), channel_id=1, source_target_pairs={{0,448},{64,0},{128,64},{192,128},{256,192},{320,256},{384,320},{4... | collective-permute-start | bytes 196616 | tf_op jit(solution)/shard_map/ppermute | solution.py:19
  33.2 8.1 %collective-permute-start.8 = (f32[2,64,128]{2,1,0:T(8,128)S(1)}, f32[2,64,128]{2,1,0:T(8,128)S(1)}, u32[]{:S(2)}, u32[]{:S(2)}) collective-permute-start(f32[2,64,128]{2,1,0:T(8,128)S(1)} %get-tuple-element.58), channel_id=1, source_target_pairs={{1,2},{2,1},{3,4},{4,3},{5,6},{6,5},{7,8},{8,7},{9,10},{10,9},{11,... | collective-permute-start | bytes 196616 | tf_op jit(solution)/shard_map/ppermute | solution.py:546
  33.9 9.1 %collective-permute-start.9 = (f32[2,64,128]{2,1,0:T(8,128)S(1)}, f32[2,64,128]{2,1,0:T(8,128)S(1)}, u32[]{:S(2)}, u32[]{:S(2)}) collective-permute-start(f32[2,64,128]{2,1,0:T(8,128)S(1)} %get-tuple-element.59), channel_id=1, source_target_pairs={{0,1},{1,0},{2,3},{3,2},{4,5},{5,4},{6,7},{7,6},{8,9},{9,8},{10,11... | collective-permute-start | bytes 196616 | tf_op jit(solution)/shard_map/ppermute | solution.py:547
  44.3 7.2 %collective-permute-start.10 = (f32[2,64,128]{2,1,0:T(8,128)S(1)}, f32[2,64,128]{2,1,0:T(8,128)S(1)}, u32[]{:S(2)}, u32[]{:S(2)}) collective-permute-start(f32[2,64,128]{2,1,0:T(8,128)S(1)} %get-tuple-element.61), channel_id=1, source_target_pairs={{1,2},{2,1},{3,4},{4,3},{5,6},{6,5},{7,8},{8,7},{9,10},{10,9},{11,... | collective-permute-start | bytes 196616 | tf_op jit(solution)/shard_map/ppermute | solution.py:546
  45.0 8.2 %collective-permute-start.11 = (f32[2,64,128]{2,1,0:T(8,128)S(1)}, f32[2,64,128]{2,1,0:T(8,128)S(1)}, u32[]{:S(2)}, u32[]{:S(2)}) collective-permute-start(f32[2,64,128]{2,1,0:T(8,128)S(1)} %get-tuple-element.62), channel_id=1, source_target_pairs={{0,1},{1,0},{2,3},{3,2},{4,5},{5,4},{6,7},{7,6},{8,9},{9,8},{10,11... | collective-permute-start | bytes 196616 | tf_op jit(solution)/shard_map/ppermute | solution.py:547
  53.8 3.7 %collective-permute-start.12 = (f32[128,128]{1,0:T(8,128)S(1)}, f32[128,128]{1,0:T(8,128)S(1)}, u32[]{:S(2)}, u32[]{:S(2)}) collective-permute-start(f32[128,128]{1,0:T(8,128)S(1)} %get-tuple-element.65), channel_id=1, source_target_pairs={{0,64},{64,128},{128,192},{192,256},{256,320},{320,384},{384,448},... | collective-permute-start | bytes 196616 | tf_op jit(solution)/shard_map/ppermute | solution.py:19
  56.2 3.7 %collective-permute-start.13 = (f32[128,128]{1,0:T(8,128)S(1)}, f32[128,128]{1,0:T(8,128)S(1)}, u32[]{:S(2)}, u32[]{:S(2)}) collective-permute-start(f32[128,128]{1,0:T(8,128)S(1)} %get-tuple-element.66), channel_id=1, source_target_pairs={{0,448},{64,0},{128,64},{192,128},{256,192},{320,256},{384,320},{4... | collective-permute-start | bytes 196616 | tf_op jit(solution)/shard_map/ppermute | solution.py:19
  61.2 34.7 %all-to-all-start = ((f32[64,1,128]{2,1,0:T(1,128)}), f32[64,1,128]{2,1,0:T(1,128)S(1)}, u32[]{:S(2)}, u32[]{:S(2)}) async-start(f32[64,1,128]{2,1,0:T(1,128)} %bitcast.4), calls=%async_computation | async-start | bytes 65536 | tf_op jit(solution)/shard_map/all_to_all | solution.py:556
  82.5 20.5 %collective-permute-start.14 = (f32[2,64,128]{2,1,0:T(8,128)S(1)}, f32[2,64,128]{2,1,0:T(8,128)S(1)}, u32[]{:S(2)}, u32[]{:S(2)}) collective-permute-start(f32[2,64,128]{2,1,0:T(8,128)S(1)} %get-tuple-element.72), channel_id=1, source_target_pairs={{1,2},{2,1},{3,4},{4,3},{5,6},{6,5},{7,8},{8,7},{9,10},{10,9},{11,... | collective-permute-start | bytes 196616 | tf_op jit(solution)/shard_map/ppermute | solution.py:546
  83.2 19.9 %collective-permute-start.15 = (f32[2,64,128]{2,1,0:T(8,128)S(1)}, f32[2,64,128]{2,1,0:T(8,128)S(1)}, u32[]{:S(2)}, u32[]{:S(2)}) collective-permute-start(f32[2,64,128]{2,1,0:T(8,128)S(1)} %get-tuple-element.73), channel_id=1, source_target_pairs={{0,1},{1,0},{2,3},{3,2},{4,5},{5,4},{6,7},{7,6},{8,9},{9,8},{10,11... | collective-permute-start | bytes 196616 | tf_op jit(solution)/shard_map/ppermute | solution.py:547
  96.5 11.1 %all-to-all-start.1 = ((f32[8,1,128]{2,1,0:T(1,128)}), f32[8,1,128]{2,1,0:T(1,128)S(1)}, u32[]{:S(2)}, u32[]{:S(2)}) async-start(f32[8,1,128]{2,1,0:T(1,128)} %bitcast.7), calls=%async_computation.1 | async-start | bytes 8192 | tf_op jit(solution)/shard_map/all_to_all | solution.py:556

commit v6 on v5

--- a/solution.py
+++ b/solution.py
@@ -599,7 +599,7 @@
         x_came = swap_x(low, high)
         joined, out, low, high, dot = call(
             functools.partial(cross_kernel, bool(earlier)),
-            [FIELD, FIELD, *FACES, pltpu.VMEM((64, 128), F32) if earlier else EIGHT],
+            [FIELD, FIELD, *FACES, pltpu.VMEM((8, 128), F32) if earlier else EIGHT],
             [pltpu.VMEM((256, 128), BF16)] * 2 + [pltpu.VMEM((256, 128), F32)] * 2,
             coef, local_table, joined, local, *x_came, *kinds, *earlier,
         )
@@ -610,8 +610,8 @@
     image, out, y_came, dot_d = solved(out, swap_y(*faces), ())
     second, out, (low, high), row = applied(out, y_came, (dot_a, dot_c, dot_d))
     before, after = swap_y(low, high)
-    row = call(sum_kernel, pltpu.VMEM((8, 128), F32), [], exchanged(row, "dev"))
-    row = exchanged(row, "node")
+    row = call(sum_kernel, pltpu.VMEM((64, 128), F32), [], exchanged(row, "node"))
+    row = exchanged(row, "dev")
     answer, rest = call(
         end_kernel,
         [FIELD, FIELD],

time: 109 us -> 108 us (level)
  blocking collectives: 0 us -> 10.3 us
  starting transfers between devices: 72.6 us -> 66.2 us
  waiting for transfers between devices: 25.8 us -> 21.2 us
    all_to_all x0 -> x1, blocking collectives: none -> 10.3 us  [exchanged(): came = lax.all_to_all(rows_out.reshape(-1, 1, 128), axis, 0, 0)]
    all_to_all x2 -> x1, waiting for transfers between devices: 11.9 us -> 5.39 us  [exchanged(): came = lax.all_to_all(rows_out.reshape(-1, 1, 128), axis, 0, 0)]
    all_to_all x2 -> x1, starting transfers between devices: 27.9 us -> 21.5 us  [exchanged(): came = lax.all_to_all(rows_out.reshape(-1, 1, 128), axis, 0, 0)]
    ppermute x5, waiting for transfers between devices: 6.52 us -> 8.46 us  [swap_y(): lax.ppermute(pair, 'dev', [(i, i + 1 if i % 2 == 0 else i - 1) for i in r...]
  transfers between devices with their start and end apart: 18 -> 17, of which waited for: 12 -> 12; matrix products, arithmetic and copies ran while one was open for 0% -> 0% of each run, Pallas kernels for 1% -> 0%
where the time goes in v6:
time: 108 us
  starting transfers between devices  66.2 us (61%)
  waiting for transfers between devices  21.2 us (20%)
  blocking collectives  10.3 us (10%)
  Pallas kernels  8.52 us (8%)
  between operations  1.52 us (1%)
    ppermute x5, starting transfers between devices, swap_y(): lax.ppermute(pair, 'dev', [(i, i + 1 if i % 2 == 0 else i - 1) for i in r...  31.3 us
    all_to_all x1, starting transfers between devices, exchanged(): came = lax.all_to_all(rows_out.reshape(-1, 1, 128), axis, 0, 0)  21.5 us
    all_to_all x1, blocking collectives, exchanged(): came = lax.all_to_all(rows_out.reshape(-1, 1, 128), axis, 0, 0)  10.3 us
    ppermute x6, starting transfers between devices, passed_along(): return lax.ppermute(x, axis, [(i, (i + by) % peers) for i in range(peers)])  10 us
    pallas_call x10, Pallas kernels, call(): pl.pallas_call(kernel, out_shape=outs, in_specs=[pl.BlockSpec(memory_spac...  8.52 us
    ppermute x5, waiting for transfers between devices, swap_y(): lax.ppermute(pair, 'dev', [(i, i + 1 if i % 2 == 0 else i - 1) for i in r...  8.46 us
    ppermute x6, waiting for transfers between devices, passed_along(): return lax.ppermute(x, axis, [(i, (i + by) % peers) for i in range(peers)])  7.38 us
    all_to_all x1, waiting for transfers between devices, exchanged(): came = lax.all_to_all(rows_out.reshape(-1, 1, 128), axis, 0, 0)  5.39 us
  transfers between devices with their start and end apart: 17, of which 12 were waited for; matrix products, arithmetic and copies ran while one was open for 0% of the time, Pallas kernels for 0%

profile of v6, /device:TPU:1, one launch (start us, length us, event | category | flops | bytes accessed | tf_op | source)
XLA Modules:
  0.0 107.8 jit_solution(3053865962006139816)
XLA Ops:
  0.6 0.0 copy-start.1
  1.3 1.3 %shard_map.86 = (f32[2,512,128]{2,1,0:T(8,128)S(1)}, f32[2,64,128]{2,1,0:T(8,128)S(1)}, f32[2,64,128]{2,1,0:T(8,128)S(1)}, f32[72,128]{1,0:T(8,128)S(1)}, f32[72...) custom-call(f32[2]{0:T(128)} %size_x_in.1, f32[1]{0:T(128)S(6)} %copy.15.size_y_in, ...), custom_call_target="tpu_custom_call" | custom-call | tf_op jit(solution)/shard_map/pallas_call | solution.py:524
  2.6 0.7 collective-permute-start
  3.3 6.6 %collective-permute-start.1 = (f32[2,64,128]{2,1,0:T(8,128)S(1)}, f32[2,64,128]{2,1,0:T(8,128)S(1)}, u32[]{:S(2)}, u32[]{:S(2)}) collective-permute-start(f32[2,64,128]{2,1,0:T(8,128)S(1)} %get-tuple-element.45), channel_id=1, source_target_pairs={{0,1},{1,0},{2,3},{3,2},{4,5},{5,4},{6,7},{7,6},{8,9},{9,8},{10,11... | collective-permute-start | bytes 196616 | tf_op jit(solution)/shard_map/ppermute | solution.py:547
  9.9 0.0 collective-permute-done.other.refs_3_
  9.9 1.6 %collective-permute-done.1.pair.refs_4_ = f32[2,64,128]{2,1,0:T(8,128)S(1)} collective-permute-done((f32[2,64,128]{2,1,0:T(8,128)S(1)}, f32[2,64,128]{2,1,0:T(8,128)S(1)}, u32[]{:S(2)}, u32[]{:S(2)}) %collective-permute-start.1) | collective-permute-done | bytes 65568 | tf_op jit(solution)/shard_map/ppermute | solution.py:547
  11.5 2.9 %collective-permute-start.2 = (f32[72,128]{1,0:T(8,128)S(1)}, f32[72,128]{1,0:T(8,128)S(1)}, u32[]{:S(2)}, u32[]{:S(2)}) collective-permute-start(f32[72,128]{1,0:T(8,128)S(1)} %get-tuple-element.48), channel_id=1, source_target_pairs={{0,64},{64,128},{128,192},{192,256},{256,320},{320,384},{384,448},... | collective-permute-start | bytes 110600 | tf_op jit(solution)/shard_map/ppermute | solution.py:19
  14.5 1.9 %collective-permute-start.3 = (f32[72,128]{1,0:T(8,128)S(1)}, f32[72,128]{1,0:T(8,128)S(1)}, u32[]{:S(2)}, u32[]{:S(2)}) collective-permute-start(f32[72,128]{1,0:T(8,128)S(1)} %get-tuple-element.49), channel_id=1, source_target_pairs={{0,448},{64,0},{128,64},{192,128},{256,192},{320,256},{384,320},{4... | collective-permute-start | bytes 110600 | tf_op jit(solution)/shard_map/ppermute | solution.py:19
  16.4 0.7 collective-permute-done.2.refs_5_.refs_6_
  17.1 0.8 collective-permute-done.3.refs_6_.refs_7_
  17.9 0.0 copy-done.1
  17.9 0.0 copy-start
  17.9 1.3 %shard_map.88 = (f32[2,512,128]{2,1,0:T(8,128)S(1)}, f32[2,512,128]{2,1,0:T(8,128)S(1)}, f32[2,64,128]{2,1,0:T(8,128)S(1)}, f32[2,64,128]{2,1,0:T(8,128)S(1)}, f32[8,128]{1,0:T(8,128)S(1)}) custom-call(f32[2,8,8,128]{3,2,1,0:T(8,128)S(1)} %get-tuple-element.41.coef.refs_0_, bf16[4,256,256]{2,1,0:T(8,128)(2,1)S(1)} %copy-done.1, ...), custom_call_target="tpu_custom_call" | custom-call | tf_op jit(solution)/shard_map/pallas_call | solution.py:524
  19.2 0.7 collective-permute-start.4
  19.9 5.5 %collective-permute-start.5 = (f32[2,64,128]{2,1,0:T(8,128)S(1)}, f32[2,64,128]{2,1,0:T(8,128)S(1)}, u32[]{:S(2)}, u32[]{:S(2)}) collective-permute-start(f32[2,64,128]{2,1,0:T(8,128)S(1)} %get-tuple-element.52), channel_id=1, source_target_pairs={{0,1},{1,0},{2,3},{3,2},{4,5},{5,4},{6,7},{7,6},{8,9},{9,8},{10,11... | collective-permute-start | bytes 196616 | tf_op jit(solution)/shard_map/ppermute | solution.py:547
  25.3 0.0 collective-permute-done.4.before
  25.3 1.6 %collective-permute-done.5.after = f32[2,64,128]{2,1,0:T(8,128)S(1)} collective-permute-done((f32[2,64,128]{2,1,0:T(8,128)S(1)}, f32[2,64,128]{2,1,0:T(8,128)S(1)}, u32[]{:S(2)}, u32[]{:S(2)}) %collective-permute-start.5) | collective-permute-done | bytes 65568 | tf_op jit(solution)/shard_map/ppermute | solution.py:547
  27.0 0.0 copy-done
  27.0 0.7 shard_map.89
  27.7 1.3 %collective-permute-start.6 = (f32[128,128]{1,0:T(8,128)S(1)}, f32[128,128]{1,0:T(8,128)S(1)}, u32[]{:S(2)}, u32[]{:S(2)}) collective-permute-start(f32[128,128]{1,0:T(8,128)S(1)} %get-tuple-element.55), channel_id=1, source_target_pairs={{0,64},{64,128},{128,192},{192,256},{256,320},{320,384},{384,448},... | collective-permute-start | bytes 196616 | tf_op jit(solution)/shard_map/ppermute | solution.py:19
  29.0 0.9 collective-permute-start.7
  29.9 0.7 collective-permute-done.6.refs_4_
  30.6 2.0 %collective-permute-done.7.refs_5_ = f32[128,128]{1,0:T(8,128)S(1)} collective-permute-done((f32[128,128]{1,0:T(8,128)S(1)}, f32[128,128]{1,0:T(8,128)S(1)}, u32[]{:S(2)}, u32[]{:S(2)}) %collective-permute-start.7) | collective-permute-done | bytes 65568 | tf_op jit(solution)/shard_map/ppermute | solution.py:19
  32.7 0.5 shard_map.90
  33.2 0.7 collective-permute-start.8
  33.9 7.5 %collective-permute-start.9 = (f32[2,64,128]{2,1,0:T(8,128)S(1)}, f32[2,64,128]{2,1,0:T(8,128)S(1)}, u32[]{:S(2)}, u32[]{:S(2)}) collective-permute-start(f32[2,64,128]{2,1,0:T(8,128)S(1)} %get-tuple-element.59), channel_id=1, source_target_pairs={{0,1},{1,0},{2,3},{3,2},{4,5},{5,4},{6,7},{7,6},{8,9},{9,8},{10,11... | collective-permute-start | bytes 196616 | tf_op jit(solution)/shard_map/ppermute | solution.py:547
  41.3 0.0 collective-permute-done.8.refs_3_
  41.4 1.6 %collective-permute-done.9.refs_4_ = f32[2,64,128]{2,1,0:T(8,128)S(1)} collective-permute-done((f32[2,64,128]{2,1,0:T(8,128)S(1)}, f32[2,64,128]{2,1,0:T(8,128)S(1)}, u32[]{:S(2)}, u32[]{:S(2)}) %collective-permute-start.9) | collective-permute-done | bytes 65568 | tf_op jit(solution)/shard_map/ppermute | solution.py:547
  43.0 1.3 %shard_map.91 = (f32[2,512,128]{2,1,0:T(8,128)S(1)}, f32[2,512,128]{2,1,0:T(8,128)S(1)}, f32[2,64,128]{2,1,0:T(8,128)S(1)}, f32[2,64,128]{2,1,0:T(8,128)S(1)}, f32[8,128]{1,0:T(8,128)S(1)}) custom-call(f32[2,8,8,128]{3,2,1,0:T(8,128)S(1)} %get-tuple-element.41.coef.refs_0_, bf16[4,256,256]{2,1,0:T(8,128)(2,1)S(1)} %copy-done.1, ...), custom_call_target="tpu_custom_call" | custom-call | tf_op jit(solution)/shard_map/pallas_call | solution.py:524
  44.3 0.7 collective-permute-start.10
  45.0 6.5 %collective-permute-start.11 = (f32[2,64,128]{2,1,0:T(8,128)S(1)}, f32[2,64,128]{2,1,0:T(8,128)S(1)}, u32[]{:S(2)}, u32[]{:S(2)}) collective-permute-start(f32[2,64,128]{2,1,0:T(8,128)S(1)} %get-tuple-element.62), channel_id=1, source_target_pairs={{0,1},{1,0},{2,3},{3,2},{4,5},{5,4},{6,7},{7,6},{8,9},{9,8},{10,11... | collective-permute-start | bytes 196616 | tf_op jit(solution)/shard_map/ppermute | solution.py:547
  51.5 0.0 collective-permute-done.10.before
  51.5 1.6 %collective-permute-done.11.after = f32[2,64,128]{2,1,0:T(8,128)S(1)} collective-permute-done((f32[2,64,128]{2,1,0:T(8,128)S(1)}, f32[2,64,128]{2,1,0:T(8,128)S(1)}, u32[]{:S(2)}, u32[]{:S(2)}) %collective-permute-start.11) | collective-permute-done | bytes 65568 | tf_op jit(solution)/shard_map/ppermute | solution.py:547
  53.1 0.7 shard_map.92
  53.9 2.4 %collective-permute-start.12 = (f32[128,128]{1,0:T(8,128)S(1)}, f32[128,128]{1,0:T(8,128)S(1)}, u32[]{:S(2)}, u32[]{:S(2)}) collective-permute-start(f32[128,128]{1,0:T(8,128)S(1)} %get-tuple-element.65), channel_id=1, source_target_pairs={{0,64},{64,128},{128,192},{192,256},{256,320},{320,384},{384,448},... | collective-permute-start | bytes 196616 | tf_op jit(solution)/shard_map/ppermute | solution.py:19
  56.3 0.5 collective-permute-start.13
  56.8 0.8 collective-permute-done.12.refs_4_
  57.6 2.4 %collective-permute-done.13.refs_5_ = f32[128,128]{1,0:T(8,128)S(1)} collective-permute-done((f32[128,128]{1,0:T(8,128)S(1)}, f32[128,128]{1,0:T(8,128)S(1)}, u32[]{:S(2)}, u32[]{:S(2)}) %collective-permute-start.13) | collective-permute-done | bytes 65568 | tf_op jit(solution)/shard_map/ppermute | solution.py:19
  60.0 0.6 shard_map.93
  60.6 10.3 %all_to_all.10 = f32[8,1,128]{2,1,0:T(1,128)S(1)} all-to-all(f32[8,1,128]{2,1,0:T(1,128)S(1)} %bitcast.19), channel_id=1, replica_groups=mesh['node'=8,'dev'=64] {'node'}, dimensions={0} | all-to-all | bytes 8192 | tf_op jit(solution)/shard_map/all_to_all | solution.py:556
  70.9 0.6 shard_map.94
  71.6 21.5 %all-to-all-start.1 = ((f32[64,1,128]{2,1,0:T(1,128)}), f32[64,1,128]{2,1,0:T(1,128)S(1)}, u32[]{:S(2)}, u32[]{:S(2)}) async-start(f32[64,1,128]{2,1,0:T(1,128)} %bitcast.7), calls=%async_computation.1 | async-start | bytes 65536 | tf_op jit(solution)/shard_map/all_to_all | solution.py:556
  93.1 0.7 collective-permute-start.14
  93.7 5.3 %collective-permute-start.15 = (f32[2,64,128]{2,1,0:T(8,128)S(1)}, f32[2,64,128]{2,1,0:T(8,128)S(1)}, u32[]{:S(2)}, u32[]{:S(2)}) collective-permute-start(f32[2,64,128]{2,1,0:T(8,128)S(1)} %get-tuple-element.73), channel_id=1, source_target_pairs={{0,1},{1,0},{2,3},{3,2},{4,5},{5,4},{6,7},{7,6},{8,9},{9,8},{10,11... | collective-permute-start | bytes 196616 | tf_op jit(solution)/shard_map/ppermute | solution.py:547
  99.1 0.0 collective-permute-done.14.before
  99.1 1.9 %collective-permute-done.15.after = f32[2,64,128]{2,1,0:T(8,128)S(1)} collective-permute-done((f32[2,64,128]{2,1,0:T(8,128)S(1)}, f32[2,64,128]{2,1,0:T(8,128)S(1)}, u32[]{:S(2)}, u32[]{:S(2)}) %collective-permute-start.15) | collective-permute-done | bytes 65568 | tf_op jit(solution)/shard_map/ppermute | solution.py:547
  101.1 5.4 %all-to-all-done.1 = f32[64,1,128]{2,1,0:T(1,128)S(1)} async-done(((f32[64,1,128]{2,1,0:T(1,128)}), f32[64,1,128]{2,1,0:T(1,128)S(1)}, u32[]{:S(2)}, u32[]{:S(2)}) %all-to-all-start.1) | async-done | bytes 32800 | tf_op jit(solution)/shard_map/all_to_all | solution.py:556
  106.5 1.4 %shard_map.95 = (f32[2,512,128]{2,1,0:T(8,128)}, f32[2,512,128]{2,1,0:T(8,128)}) custom-call(f32[2,8,8,128]{3,2,1,0:T(8,128)S(1)} %get-tuple-element.41.coef.refs_0_, s32[2,128]{1,0:T(2,128)S(1)} %get-tuple-element.42.orient, f32[64,128]{1,0:T(8,128)S(1)} %bitcast.17, f32[2,512,128]{2,1,0:T(8,128)S(1)} %get-tuple-element.71.last, ...), custom_call_target="tpu_custom_call" | custom-call | tf_op jit(solution)/shard_map/pallas_call | solution.py:524
  (1 shorter events, 0.0 us)
Async XLA Ops:
  0.6 17.2 %copy-start.1 = (bf16[4,256,256]{2,1,0:T(8,128)(2,1)S(1)}, bf16[4,256,256]{2,1,0:T(8,128)(2,1)}, u32[]{:S(2)}) copy-start(bf16[4,256,256]{2,1,0:T(8,128)(2,1)} %constant.4.clone.refs_1_) | copy-start | bytes 1572868
  2.6 7.3 %collective-permute-start = (f32[2,64,128]{2,1,0:T(8,128)S(1)}, f32[2,64,128]{2,1,0:T(8,128)S(1)}, u32[]{:S(2)}, u32[]{:S(2)}) collective-permute-start(f32[2,64,128]{2,1,0:T(8,128)S(1)} %get-tuple-element.44), channel_id=1, source_target_pairs={{1,2},{2,1},{3,4},{4,3},{5,6},{6,5},{7,8},{8,7},{9,10},{10,9},{11,... | collective-permute-start | bytes 196616 | tf_op jit(solution)/shard_map/ppermute | solution.py:546
  3.3 8.2 %collective-permute-start.1 = (f32[2,64,128]{2,1,0:T(8,128)S(1)}, f32[2,64,128]{2,1,0:T(8,128)S(1)}, u32[]{:S(2)}, u32[]{:S(2)}) collective-permute-start(f32[2,64,128]{2,1,0:T(8,128)S(1)} %get-tuple-element.45), channel_id=1, source_target_pairs={{0,1},{1,0},{2,3},{3,2},{4,5},{5,4},{6,7},{7,6},{8,9},{9,8},{10,11... | collective-permute-start | bytes 196616 | tf_op jit(solution)/shard_map/ppermute | solution.py:547
  11.5 5.5 %collective-permute-start.2 = (f32[72,128]{1,0:T(8,128)S(1)}, f32[72,128]{1,0:T(8,128)S(1)}, u32[]{:S(2)}, u32[]{:S(2)}) collective-permute-start(f32[72,128]{1,0:T(8,128)S(1)} %get-tuple-element.48), channel_id=1, source_target_pairs={{0,64},{64,128},{128,192},{192,256},{256,320},{320,384},{384,448},... | collective-permute-start | bytes 110600 | tf_op jit(solution)/shard_map/ppermute | solution.py:19
  14.5 3.4 %collective-permute-start.3 = (f32[72,128]{1,0:T(8,128)S(1)}, f32[72,128]{1,0:T(8,128)S(1)}, u32[]{:S(2)}, u32[]{:S(2)}) collective-permute-start(f32[72,128]{1,0:T(8,128)S(1)} %get-tuple-element.49), channel_id=1, source_target_pairs={{0,448},{64,0},{128,64},{192,128},{256,192},{320,256},{384,320},{4... | collective-permute-start | bytes 110600 | tf_op jit(solution)/shard_map/ppermute | solution.py:19
  17.9 9.1 %copy-start = (bf16[4,256,256]{2,1,0:T(8,128)(2,1)S(1)}, bf16[4,256,256]{2,1,0:T(8,128)(2,1)}, u32[]{:S(2)}) copy-start(bf16[4,256,256]{2,1,0:T(8,128)(2,1)} %constant.5.clone.table.refs_1_) | copy-start | bytes 1572868
  19.2 6.1 %collective-permute-start.4 = (f32[2,64,128]{2,1,0:T(8,128)S(1)}, f32[2,64,128]{2,1,0:T(8,128)S(1)}, u32[]{:S(2)}, u32[]{:S(2)}) collective-permute-start(f32[2,64,128]{2,1,0:T(8,128)S(1)} %get-tuple-element.51), channel_id=1, source_target_pairs={{1,2},{2,1},{3,4},{4,3},{5,6},{6,5},{7,8},{8,7},{9,10},{10,9},{11,... | collective-permute-start | bytes 196616 | tf_op jit(solution)/shard_map/ppermute | solution.py:546
  19.9 7.1 %collective-permute-start.5 = (f32[2,64,128]{2,1,0:T(8,128)S(1)}, f32[2,64,128]{2,1,0:T(8,128)S(1)}, u32[]{:S(2)}, u32[]{:S(2)}) collective-permute-start(f32[2,64,128]{2,1,0:T(8,128)S(1)} %get-tuple-element.52), channel_id=1, source_target_pairs={{0,1},{1,0},{2,3},{3,2},{4,5},{5,4},{6,7},{7,6},{8,9},{9,8},{10,11... | collective-permute-start | bytes 196616 | tf_op jit(solution)/shard_map/ppermute | solution.py:547
  27.7 2.9 %collective-permute-start.6 = (f32[128,128]{1,0:T(8,128)S(1)}, f32[128,128]{1,0:T(8,128)S(1)}, u32[]{:S(2)}, u32[]{:S(2)}) collective-permute-start(f32[128,128]{1,0:T(8,128)S(1)} %get-tuple-element.55), channel_id=1, source_target_pairs={{0,64},{64,128},{128,192},{192,256},{256,320},{320,384},{384,448},... | collective-permute-start | bytes 196616 | tf_op jit(solution)/shard_map/ppermute | solution.py:19
  29.0 3.7 %collective-permute-start.7 = (f32[128,128]{1,0:T(8,128)S(1)}, f32[128,128]{1,0:T(8,128)S(1)}, u32[]{:S(2)}, u32[]{:S(2)}) collective-permute-start(f32[128,128]{1,0:T(8,128)S(1)} %get-tuple-element.56), channel_id=1, source_target_pairs={{0,448},{64,0},{128,64},{192,128},{256,192},{320,256},{384,320},{4... | collective-permute-start | bytes 196616 | tf_op jit(solution)/shard_map/ppermute | solution.py:19
  33.2 8.1 %collective-permute-start.8 = (f32[2,64,128]{2,1,0:T(8,128)S(1)}, f32[2,64,128]{2,1,0:T(8,128)S(1)}, u32[]{:S(2)}, u32[]{:S(2)}) collective-permute-start(f32[2,64,128]{2,1,0:T(8,128)S(1)} %get-tuple-element.58), channel_id=1, source_target_pairs={{1,2},{2,1},{3,4},{4,3},{5,6},{6,5},{7,8},{8,7},{9,10},{10,9},{11,... | collective-permute-start | bytes 196616 | tf_op jit(solution)/shard_map/ppermute | solution.py:546
  33.9 9.1 %collective-permute-start.9 = (f32[2,64,128]{2,1,0:T(8,128)S(1)}, f32[2,64,128]{2,1,0:T(8,128)S(1)}, u32[]{:S(2)}, u32[]{:S(2)}) collective-permute-start(f32[2,64,128]{2,1,0:T(8,128)S(1)} %get-tuple-element.59), channel_id=1, source_target_pairs={{0,1},{1,0},{2,3},{3,2},{4,5},{5,4},{6,7},{7,6},{8,9},{9,8},{10,11... | collective-permute-start | bytes 196616 | tf_op jit(solution)/shard_map/ppermute | solution.py:547
  44.3 7.2 %collective-permute-start.10 = (f32[2,64,128]{2,1,0:T(8,128)S(1)}, f32[2,64,128]{2,1,0:T(8,128)S(1)}, u32[]{:S(2)}, u32[]{:S(2)}) collective-permute-start(f32[2,64,128]{2,1,0:T(8,128)S(1)} %get-tuple-element.61), channel_id=1, source_target_pairs={{1,2},{2,1},{3,4},{4,3},{5,6},{6,5},{7,8},{8,7},{9,10},{10,9},{11,... | collective-permute-start | bytes 196616 | tf_op jit(solution)/shard_map/ppermute | solution.py:546
  45.0 8.2 %collective-permute-start.11 = (f32[2,64,128]{2,1,0:T(8,128)S(1)}, f32[2,64,128]{2,1,0:T(8,128)S(1)}, u32[]{:S(2)}, u32[]{:S(2)}) collective-permute-start(f32[2,64,128]{2,1,0:T(8,128)S(1)} %get-tuple-element.62), channel_id=1, source_target_pairs={{0,1},{1,0},{2,3},{3,2},{4,5},{5,4},{6,7},{7,6},{8,9},{9,8},{10,11... | collective-permute-start | bytes 196616 | tf_op jit(solution)/shard_map/ppermute | solution.py:547
  53.9 3.7 %collective-permute-start.12 = (f32[128,128]{1,0:T(8,128)S(1)}, f32[128,128]{1,0:T(8,128)S(1)}, u32[]{:S(2)}, u32[]{:S(2)}) collective-permute-start(f32[128,128]{1,0:T(8,128)S(1)} %get-tuple-element.65), channel_id=1, source_target_pairs={{0,64},{64,128},{128,192},{192,256},{256,320},{320,384},{384,448},... | collective-permute-start | bytes 196616 | tf_op jit(solution)/shard_map/ppermute | solution.py:19
  56.3 3.7 %collective-permute-start.13 = (f32[128,128]{1,0:T(8,128)S(1)}, f32[128,128]{1,0:T(8,128)S(1)}, u32[]{:S(2)}, u32[]{:S(2)}) collective-permute-start(f32[128,128]{1,0:T(8,128)S(1)} %get-tuple-element.66), channel_id=1, source_target_pairs={{0,448},{64,0},{128,64},{192,128},{256,192},{320,256},{384,320},{4... | collective-permute-start | bytes 196616 | tf_op jit(solution)/shard_map/ppermute | solution.py:19
  71.6 34.9 %all-to-all-start.1 = ((f32[64,1,128]{2,1,0:T(1,128)}), f32[64,1,128]{2,1,0:T(1,128)S(1)}, u32[]{:S(2)}, u32[]{:S(2)}) async-start(f32[64,1,128]{2,1,0:T(1,128)} %bitcast.7), calls=%async_computation.1 | async-start | bytes 65536 | tf_op jit(solution)/shard_map/all_to_all | solution.py:556
  93.1 6.0 %collective-permute-start.14 = (f32[2,64,128]{2,1,0:T(8,128)S(1)}, f32[2,64,128]{2,1,0:T(8,128)S(1)}, u32[]{:S(2)}, u32[]{:S(2)}) collective-permute-start(f32[2,64,128]{2,1,0:T(8,128)S(1)} %get-tuple-element.72), channel_id=1, source_target_pairs={{1,2},{2,1},{3,4},{4,3},{5,6},{6,5},{7,8},{8,7},{9,10},{10,9},{11,... | collective-permute-start | bytes 196616 | tf_op jit(solution)/shard_map/ppermute | solution.py:546
  93.7 7.3 %collective-permute-start.15 = (f32[2,64,128]{2,1,0:T(8,128)S(1)}, f32[2,64,128]{2,1,0:T(8,128)S(1)}, u32[]{:S(2)}, u32[]{:S(2)}) collective-permute-start(f32[2,64,128]{2,1,0:T(8,128)S(1)} %get-tuple-element.73), channel_id=1, source_target_pairs={{0,1},{1,0},{2,3},{3,2},{4,5},{5,4},{6,7},{7,6},{8,9},{9,8},{10,11... | collective-permute-start | bytes 196616 | tf_op jit(solution)/shard_map/ppermute | solution.py:547

commit v7 on v6

--- a/solution.py
+++ b/solution.py
@@ -552,8 +552,21 @@
     return passed_along(high, "node", 1), passed_along(low, "node", -1)
 
 
-def exchanged(rows_out, axis):
-    came = lax.all_to_all(rows_out.reshape(-1, 1, 128), axis, 0, 0)
+Y_CHIPS = 4
+
+
+def plane_groups():
+    nodes, devs = lax.axis_size("node"), lax.axis_size("dev")
+    return [[n * devs + z + y for n in range(nodes) for y in range(Y_CHIPS)] for z in range(0, devs, Y_CHIPS)]
+
+
+def column_groups():
+    nodes, devs = lax.axis_size("node"), lax.axis_size("dev")
+    return [[n * devs + z + y for z in range(0, devs, Y_CHIPS)] for n in range(nodes) for y in range(Y_CHIPS)]
+
+
+def exchanged(rows_out, groups):
+    came = lax.all_to_all(rows_out.reshape(-1, 1, 128), ("node", "dev"), 0, 0, axis_index_groups=groups)
     return came.reshape(rows_out.shape)
 
 
@@ -599,7 +612,7 @@
         x_came = swap_x(low, high)
         joined, out, low, high, dot = call(
             functools.partial(cross_kernel, bool(earlier)),
-            [FIELD, FIELD, *FACES, pltpu.VMEM((8, 128), F32) if earlier else EIGHT],
+            [FIELD, FIELD, *FACES, pltpu.VMEM((32, 128), F32) if earlier else EIGHT],
             [pltpu.VMEM((256, 128), BF16)] * 2 + [pltpu.VMEM((256, 128), F32)] * 2,
             coef, local_table, joined, local, *x_came, *kinds, *earlier,
         )
@@ -610,8 +623,8 @@
     image, out, y_came, dot_d = solved(out, swap_y(*faces), ())
     second, out, (low, high), row = applied(out, y_came, (dot_a, dot_c, dot_d))
     before, after = swap_y(low, high)
-    row = call(sum_kernel, pltpu.VMEM((64, 128), F32), [], exchanged(row, "node"))
-    row = exchanged(row, "dev")
+    row = call(sum_kernel, pltpu.VMEM((16, 128), F32), [], exchanged(row, plane_groups()))
+    row = exchanged(row, column_groups())
     answer, rest = call(
         end_kernel,
         [FIELD, FIELD],

time: 108 us -> 113 us (1.046)
  blocking collectives: 10.3 us -> 43.1 us
  starting transfers between devices: 66.2 us -> 46.4 us
  waiting for transfers between devices: 21.2 us -> 13.9 us
    all_to_all x1 -> x2, blocking collectives: 10.3 us -> 43.1 us  [exchanged(): lax.all_to_all(rows_out.reshape(-1, 1, 128), ('node', 'dev'), 0, 0, axis_...]
    all_to_all x1 -> x0, starting transfers between devices: 21.5 us -> none  [exchanged(): came = lax.all_to_all(rows_out.reshape(-1, 1, 128), axis, 0, 0)]
    all_to_all x1 -> x0, waiting for transfers between devices: 5.39 us -> none  [exchanged(): came = lax.all_to_all(rows_out.reshape(-1, 1, 128), axis, 0, 0)]
    ppermute x5, waiting for transfers between devices: 8.46 us -> 6.52 us  [swap_y(): lax.ppermute(pair, 'dev', [(i, i + 1 if i % 2 == 0 else i - 1) for i in r...]
    ppermute x5, starting transfers between devices: 31.3 us -> 33 us  [swap_y(): lax.ppermute(pair, 'dev', [(i, i + 1 if i % 2 == 0 else i - 1) for i in r...]
  transfers between devices with their start and end apart: 17 -> 16, of which waited for: 12 -> 10; matrix products, arithmetic and copies ran while one was open for 0% -> 0% of each run, Pallas kernels for 0% -> 0%
where the time goes in v7:
time: 113 us
  starting transfers between devices  46.4 us (41%)
  blocking collectives  43.1 us (38%)
  waiting for transfers between devices  13.9 us (12%)
  Pallas kernels  7.91 us (7%)
  between operations  1.5 us (1%)
    all_to_all x2, blocking collectives, exchanged(): lax.all_to_all(rows_out.reshape(-1, 1, 128), ('node', 'dev'), 0, 0, axis_...  43.1 us
    ppermute x5, starting transfers between devices, swap_y(): lax.ppermute(pair, 'dev', [(i, i + 1 if i % 2 == 0 else i - 1) for i in r...  33 us
    ppermute x6, starting transfers between devices, passed_along(): return lax.ppermute(x, axis, [(i, (i + by) % peers) for i in range(peers)])  10 us
    pallas_call x10, Pallas kernels, call(): pl.pallas_call(kernel, out_shape=outs, in_specs=[pl.BlockSpec(memory_spac...  7.91 us
    ppermute x6, waiting for transfers between devices, passed_along(): return lax.ppermute(x, axis, [(i, (i + by) % peers) for i in range(peers)])  7.37 us
    ppermute x5, waiting for transfers between devices, swap_y(): lax.ppermute(pair, 'dev', [(i, i + 1 if i % 2 == 0 else i - 1) for i in r...  6.52 us
    ppermute x5, starting transfers between devices, swap_y(): lax.ppermute(other, 'dev', [(i, i - 1 if i % 2 == 0 else i + 1) for i in...  3.32 us
  transfers between devices with their start and end apart: 16, of which 10 were waited for; matrix products, arithmetic and copies ran while one was open for 0% of the time, Pallas kernels for 0%

profile of v7, /device:TPU:1, one launch (start us, length us, event | category | flops | bytes accessed | tf_op | source)
XLA Modules:
  0.0 112.8 jit_solution(4276946651479071103)
XLA Ops:
  0.6 0.0 copy-start.1
  1.3 1.3 %shard_map.86 = (f32[2,512,128]{2,1,0:T(8,128)S(1)}, f32[2,64,128]{2,1,0:T(8,128)S(1)}, f32[2,64,128]{2,1,0:T(8,128)S(1)}, f32[72,128]{1,0:T(8,128)S(1)}, f32[72...) custom-call(f32[2]{0:T(128)} %size_x_in.1, f32[1]{0:T(128)S(6)} %copy.15.size_y_in, ...), custom_call_target="tpu_custom_call" | custom-call | tf_op jit(solution)/shard_map/pallas_call | solution.py:524
  2.6 0.7 collective-permute-start
  3.3 6.6 %collective-permute-start.1 = (f32[2,64,128]{2,1,0:T(8,128)S(1)}, f32[2,64,128]{2,1,0:T(8,128)S(1)}, u32[]{:S(2)}, u32[]{:S(2)}) collective-permute-start(f32[2,64,128]{2,1,0:T(8,128)S(1)} %get-tuple-element.45), channel_id=1, source_target_pairs={{0,1},{1,0},{2,3},{3,2},{4,5},{5,4},{6,7},{7,6},{8,9},{9,8},{10,11... | collective-permute-start | bytes 196616 | tf_op jit(solution)/shard_map/ppermute | solution.py:547
  9.9 0.0 collective-permute-done.other.refs_3_
  9.9 1.6 %collective-permute-done.1.pair.refs_4_ = f32[2,64,128]{2,1,0:T(8,128)S(1)} collective-permute-done((f32[2,64,128]{2,1,0:T(8,128)S(1)}, f32[2,64,128]{2,1,0:T(8,128)S(1)}, u32[]{:S(2)}, u32[]{:S(2)}) %collective-permute-start.1) | collective-permute-done | bytes 65568 | tf_op jit(solution)/shard_map/ppermute | solution.py:547
  11.5 2.9 %collective-permute-start.2 = (f32[72,128]{1,0:T(8,128)S(1)}, f32[72,128]{1,0:T(8,128)S(1)}, u32[]{:S(2)}, u32[]{:S(2)}) collective-permute-start(f32[72,128]{1,0:T(8,128)S(1)} %get-tuple-element.48), channel_id=1, source_target_pairs={{0,64},{64,128},{128,192},{192,256},{256,320},{320,384},{384,448},... | collective-permute-start | bytes 110600 | tf_op jit(solution)/shard_map/ppermute | solution.py:19
  14.5 1.9 %collective-permute-start.3 = (f32[72,128]{1,0:T(8,128)S(1)}, f32[72,128]{1,0:T(8,128)S(1)}, u32[]{:S(2)}, u32[]{:S(2)}) collective-permute-start(f32[72,128]{1,0:T(8,128)S(1)} %get-tuple-element.49), channel_id=1, source_target_pairs={{0,448},{64,0},{128,64},{192,128},{256,192},{320,256},{384,320},{4... | collective-permute-start | bytes 110600 | tf_op jit(solution)/shard_map/ppermute | solution.py:19
  16.4 0.7 collective-permute-done.2.refs_5_.refs_6_
  17.1 0.8 collective-permute-done.3.refs_6_.refs_7_
  17.9 0.0 copy-done.1
  17.9 0.0 copy-start
  17.9 1.3 %shard_map.88 = (f32[2,512,128]{2,1,0:T(8,128)S(1)}, f32[2,512,128]{2,1,0:T(8,128)S(1)}, f32[2,64,128]{2,1,0:T(8,128)S(1)}, f32[2,64,128]{2,1,0:T(8,128)S(1)}, f32[8,128]{1,0:T(8,128)S(1)}) custom-call(f32[2,8,8,128]{3,2,1,0:T(8,128)S(1)} %get-tuple-element.41.coef.refs_0_, bf16[4,256,256]{2,1,0:T(8,128)(2,1)S(1)} %copy-done.1, ...), custom_call_target="tpu_custom_call" | custom-call | tf_op jit(solution)/shard_map/pallas_call | solution.py:524
  19.2 0.7 collective-permute-start.4
  19.9 5.5 %collective-permute-start.5 = (f32[2,64,128]{2,1,0:T(8,128)S(1)}, f32[2,64,128]{2,1,0:T(8,128)S(1)}, u32[]{:S(2)}, u32[]{:S(2)}) collective-permute-start(f32[2,64,128]{2,1,0:T(8,128)S(1)} %get-tuple-element.52), channel_id=1, source_target_pairs={{0,1},{1,0},{2,3},{3,2},{4,5},{5,4},{6,7},{7,6},{8,9},{9,8},{10,11... | collective-permute-start | bytes 196616 | tf_op jit(solution)/shard_map/ppermute | solution.py:547
  25.3 0.0 collective-permute-done.4.before
  25.3 1.6 %collective-permute-done.5.after = f32[2,64,128]{2,1,0:T(8,128)S(1)} collective-permute-done((f32[2,64,128]{2,1,0:T(8,128)S(1)}, f32[2,64,128]{2,1,0:T(8,128)S(1)}, u32[]{:S(2)}, u32[]{:S(2)}) %collective-permute-start.5) | collective-permute-done | bytes 65568 | tf_op jit(solution)/shard_map/ppermute | solution.py:547
  27.0 0.0 copy-done
  27.0 0.7 shard_map.89
  27.7 1.3 %collective-permute-start.6 = (f32[128,128]{1,0:T(8,128)S(1)}, f32[128,128]{1,0:T(8,128)S(1)}, u32[]{:S(2)}, u32[]{:S(2)}) collective-permute-start(f32[128,128]{1,0:T(8,128)S(1)} %get-tuple-element.55), channel_id=1, source_target_pairs={{0,64},{64,128},{128,192},{192,256},{256,320},{320,384},{384,448},... | collective-permute-start | bytes 196616 | tf_op jit(solution)/shard_map/ppermute | solution.py:19
  29.0 0.9 collective-permute-start.7
  29.9 0.7 collective-permute-done.6.refs_4_
  30.6 2.0 %collective-permute-done.7.refs_5_ = f32[128,128]{1,0:T(8,128)S(1)} collective-permute-done((f32[128,128]{1,0:T(8,128)S(1)}, f32[128,128]{1,0:T(8,128)S(1)}, u32[]{:S(2)}, u32[]{:S(2)}) %collective-permute-start.7) | collective-permute-done | bytes 65568 | tf_op jit(solution)/shard_map/ppermute | solution.py:19
  32.7 0.5 shard_map.90
  33.2 0.7 collective-permute-start.8
  33.9 7.5 %collective-permute-start.9 = (f32[2,64,128]{2,1,0:T(8,128)S(1)}, f32[2,64,128]{2,1,0:T(8,128)S(1)}, u32[]{:S(2)}, u32[]{:S(2)}) collective-permute-start(f32[2,64,128]{2,1,0:T(8,128)S(1)} %get-tuple-element.59), channel_id=1, source_target_pairs={{0,1},{1,0},{2,3},{3,2},{4,5},{5,4},{6,7},{7,6},{8,9},{9,8},{10,11... | collective-permute-start | bytes 196616 | tf_op jit(solution)/shard_map/ppermute | solution.py:547
  41.3 0.0 collective-permute-done.8.refs_3_
  41.4 1.6 %collective-permute-done.9.refs_4_ = f32[2,64,128]{2,1,0:T(8,128)S(1)} collective-permute-done((f32[2,64,128]{2,1,0:T(8,128)S(1)}, f32[2,64,128]{2,1,0:T(8,128)S(1)}, u32[]{:S(2)}, u32[]{:S(2)}) %collective-permute-start.9) | collective-permute-done | bytes 65568 | tf_op jit(solution)/shard_map/ppermute | solution.py:547
  43.0 1.3 %shard_map.91 = (f32[2,512,128]{2,1,0:T(8,128)S(1)}, f32[2,512,128]{2,1,0:T(8,128)S(1)}, f32[2,64,128]{2,1,0:T(8,128)S(1)}, f32[2,64,128]{2,1,0:T(8,128)S(1)}, f32[8,128]{1,0:T(8,128)S(1)}) custom-call(f32[2,8,8,128]{3,2,1,0:T(8,128)S(1)} %get-tuple-element.41.coef.refs_0_, bf16[4,256,256]{2,1,0:T(8,128)(2,1)S(1)} %copy-done.1, ...), custom_call_target="tpu_custom_call" | custom-call | tf_op jit(solution)/shard_map/pallas_call | solution.py:524
  44.3 0.7 collective-permute-start.10
  45.0 6.5 %collective-permute-start.11 = (f32[2,64,128]{2,1,0:T(8,128)S(1)}, f32[2,64,128]{2,1,0:T(8,128)S(1)}, u32[]{:S(2)}, u32[]{:S(2)}) collective-permute-start(f32[2,64,128]{2,1,0:T(8,128)S(1)} %get-tuple-element.62), channel_id=1, source_target_pairs={{0,1},{1,0},{2,3},{3,2},{4,5},{5,4},{6,7},{7,6},{8,9},{9,8},{10,11... | collective-permute-start | bytes 196616 | tf_op jit(solution)/shard_map/ppermute | solution.py:547
  51.5 0.0 collective-permute-done.10.before
  51.5 1.6 %collective-permute-done.11.after = f32[2,64,128]{2,1,0:T(8,128)S(1)} collective-permute-done((f32[2,64,128]{2,1,0:T(8,128)S(1)}, f32[2,64,128]{2,1,0:T(8,128)S(1)}, u32[]{:S(2)}, u32[]{:S(2)}) %collective-permute-start.11) | collective-permute-done | bytes 65568 | tf_op jit(solution)/shard_map/ppermute | solution.py:547
  53.1 0.7 shard_map.92
  53.8 2.4 %collective-permute-start.12 = (f32[128,128]{1,0:T(8,128)S(1)}, f32[128,128]{1,0:T(8,128)S(1)}, u32[]{:S(2)}, u32[]{:S(2)}) collective-permute-start(f32[128,128]{1,0:T(8,128)S(1)} %get-tuple-element.65), channel_id=1, source_target_pairs={{0,64},{64,128},{128,192},{192,256},{256,320},{320,384},{384,448},... | collective-permute-start | bytes 196616 | tf_op jit(solution)/shard_map/ppermute | solution.py:19
  56.2 0.6 collective-permute-start.13
  56.8 0.8 collective-permute-done.12.refs_4_
  57.6 2.4 %collective-permute-done.13.refs_5_ = f32[128,128]{1,0:T(8,128)S(1)} collective-permute-done((f32[128,128]{1,0:T(8,128)S(1)}, f32[128,128]{1,0:T(8,128)S(1)}, u32[]{:S(2)}, u32[]{:S(2)}) %collective-permute-start.13) | collective-permute-done | bytes 65568 | tf_op jit(solution)/shard_map/ppermute | solution.py:19
  59.9 0.6 shard_map.93
  60.6 0.7 collective-permute-start.14
  61.2 7.0 %collective-permute-start.15 = (f32[2,64,128]{2,1,0:T(8,128)S(1)}, f32[2,64,128]{2,1,0:T(8,128)S(1)}, u32[]{:S(2)}, u32[]{:S(2)}) collective-permute-start(f32[2,64,128]{2,1,0:T(8,128)S(1)} %get-tuple-element.73), channel_id=1, source_target_pairs={{0,1},{1,0},{2,3},{3,2},{4,5},{5,4},{6,7},{7,6},{8,9},{9,8},{10,11... | collective-permute-start | bytes 196616 | tf_op jit(solution)/shard_map/ppermute | solution.py:547
  68.3 16.1 %all_to_all.10 = f32[32,1,128]{2,1,0:T(1,128)S(1)} all-to-all(f32[32,1,128]{2,1,0:T(1,128)S(1)} %bitcast.20), channel_id=1, replica_groups={{0,1,2,3,64,65,66,67,128,129,130,131,192,193,194,195,256,257,258,259,32..., dimensions={0} | all-to-all | bytes 32768 | tf_op jit(solution)/shard_map/all_to_all | solution.py:569
  84.3 27.1 %all_to_all.11 = f32[16,1,128]{2,1,0:T(1,128)S(1)} all-to-all(f32[16,1,128]{2,1,0:T(1,128)S(1)} %bitcast.19), channel_id=1, replica_groups={{0,4,8,12,16,20,24,28,32,36,40,44,48,52,56,60},{1,5,9,13,17,21,25,29,33..., dimensions={0} | all-to-all | bytes 16384 | tf_op jit(solution)/shard_map/all_to_all | solution.py:569
  111.4 0.0 collective-permute-done.14.before
  111.4 0.0 collective-permute-done.15.after
  111.4 1.4 %shard_map.95 = (f32[2,512,128]{2,1,0:T(8,128)}, f32[2,512,128]{2,1,0:T(8,128)}) custom-call(f32[2,8,8,128]{3,2,1,0:T(8,128)S(1)} %get-tuple-element.41.coef.refs_0_, s32[2,128]{1,0:T(2,128)S(1)} %get-tuple-element.42.orient, f32[16,128]{1,0:T(8,128)S(1)} %bitcast.18, f32[2,512,128]{2,1,0:T(8,128)S(1)} %get-tuple-element.71.last, ...), custom_call_target="tpu_custom_call" | custom-call | tf_op jit(solution)/shard_map/pallas_call | solution.py:524
  (2 shorter events, 0.0 us)
Async XLA Ops:
  0.6 17.2 %copy-start.1 = (bf16[4,256,256]{2,1,0:T(8,128)(2,1)S(1)}, bf16[4,256,256]{2,1,0:T(8,128)(2,1)}, u32[]{:S(2)}) copy-start(bf16[4,256,256]{2,1,0:T(8,128)(2,1)} %constant.4.clone.refs_1_) | copy-start | bytes 1572868
  2.6 7.3 %collective-permute-start = (f32[2,64,128]{2,1,0:T(8,128)S(1)}, f32[2,64,128]{2,1,0:T(8,128)S(1)}, u32[]{:S(2)}, u32[]{:S(2)}) collective-permute-start(f32[2,64,128]{2,1,0:T(8,128)S(1)} %get-tuple-element.44), channel_id=1, source_target_pairs={{1,2},{2,1},{3,4},{4,3},{5,6},{6,5},{7,8},{8,7},{9,10},{10,9},{11,... | collective-permute-start | bytes 196616 | tf_op jit(solution)/shard_map/ppermute | solution.py:546
  3.3 8.2 %collective-permute-start.1 = (f32[2,64,128]{2,1,0:T(8,128)S(1)}, f32[2,64,128]{2,1,0:T(8,128)S(1)}, u32[]{:S(2)}, u32[]{:S(2)}) collective-permute-start(f32[2,64,128]{2,1,0:T(8,128)S(1)} %get-tuple-element.45), channel_id=1, source_target_pairs={{0,1},{1,0},{2,3},{3,2},{4,5},{5,4},{6,7},{7,6},{8,9},{9,8},{10,11... | collective-permute-start | bytes 196616 | tf_op jit(solution)/shard_map/ppermute | solution.py:547
  11.5 5.5 %collective-permute-start.2 = (f32[72,128]{1,0:T(8,128)S(1)}, f32[72,128]{1,0:T(8,128)S(1)}, u32[]{:S(2)}, u32[]{:S(2)}) collective-permute-start(f32[72,128]{1,0:T(8,128)S(1)} %get-tuple-element.48), channel_id=1, source_target_pairs={{0,64},{64,128},{128,192},{192,256},{256,320},{320,384},{384,448},... | collective-permute-start | bytes 110600 | tf_op jit(solution)/shard_map/ppermute | solution.py:19
  14.5 3.4 %collective-permute-start.3 = (f32[72,128]{1,0:T(8,128)S(1)}, f32[72,128]{1,0:T(8,128)S(1)}, u32[]{:S(2)}, u32[]{:S(2)}) collective-permute-start(f32[72,128]{1,0:T(8,128)S(1)} %get-tuple-element.49), channel_id=1, source_target_pairs={{0,448},{64,0},{128,64},{192,128},{256,192},{320,256},{384,320},{4... | collective-permute-start | bytes 110600 | tf_op jit(solution)/shard_map/ppermute | solution.py:19
  17.9 9.1 %copy-start = (bf16[4,256,256]{2,1,0:T(8,128)(2,1)S(1)}, bf16[4,256,256]{2,1,0:T(8,128)(2,1)}, u32[]{:S(2)}) copy-start(bf16[4,256,256]{2,1,0:T(8,128)(2,1)} %constant.5.clone.table.refs_1_) | copy-start | bytes 1572868
  19.2 6.1 %collective-permute-start.4 = (f32[2,64,128]{2,1,0:T(8,128)S(1)}, f32[2,64,128]{2,1,0:T(8,128)S(1)}, u32[]{:S(2)}, u32[]{:S(2)}) collective-permute-start(f32[2,64,128]{2,1,0:T(8,128)S(1)} %get-tuple-element.51), channel_id=1, source_target_pairs={{1,2},{2,1},{3,4},{4,3},{5,6},{6,5},{7,8},{8,7},{9,10},{10,9},{11,... | collective-permute-start | bytes 196616 | tf_op jit(solution)/shard_map/ppermute | solution.py:546
  19.9 7.1 %collective-permute-start.5 = (f32[2,64,128]{2,1,0:T(8,128)S(1)}, f32[2,64,128]{2,1,0:T(8,128)S(1)}, u32[]{:S(2)}, u32[]{:S(2)}) collective-permute-start(f32[2,64,128]{2,1,0:T(8,128)S(1)} %get-tuple-element.52), channel_id=1, source_target_pairs={{0,1},{1,0},{2,3},{3,2},{4,5},{5,4},{6,7},{7,6},{8,9},{9,8},{10,11... | collective-permute-start | bytes 196616 | tf_op jit(solution)/shard_map/ppermute | solution.py:547
  27.7 2.9 %collective-permute-start.6 = (f32[128,128]{1,0:T(8,128)S(1)}, f32[128,128]{1,0:T(8,128)S(1)}, u32[]{:S(2)}, u32[]{:S(2)}) collective-permute-start(f32[128,128]{1,0:T(8,128)S(1)} %get-tuple-element.55), channel_id=1, source_target_pairs={{0,64},{64,128},{128,192},{192,256},{256,320},{320,384},{384,448},... | collective-permute-start | bytes 196616 | tf_op jit(solution)/shard_map/ppermute | solution.py:19
  29.0 3.7 %collective-permute-start.7 = (f32[128,128]{1,0:T(8,128)S(1)}, f32[128,128]{1,0:T(8,128)S(1)}, u32[]{:S(2)}, u32[]{:S(2)}) collective-permute-start(f32[128,128]{1,0:T(8,128)S(1)} %get-tuple-element.56), channel_id=1, source_target_pairs={{0,448},{64,0},{128,64},{192,128},{256,192},{320,256},{384,320},{4... | collective-permute-start | bytes 196616 | tf_op jit(solution)/shard_map/ppermute | solution.py:19
  33.2 8.1 %collective-permute-start.8 = (f32[2,64,128]{2,1,0:T(8,128)S(1)}, f32[2,64,128]{2,1,0:T(8,128)S(1)}, u32[]{:S(2)}, u32[]{:S(2)}) collective-permute-start(f32[2,64,128]{2,1,0:T(8,128)S(1)} %get-tuple-element.58), channel_id=1, source_target_pairs={{1,2},{2,1},{3,4},{4,3},{5,6},{6,5},{7,8},{8,7},{9,10},{10,9},{11,... | collective-permute-start | bytes 196616 | tf_op jit(solution)/shard_map/ppermute | solution.py:546
  33.9 9.1 %collective-permute-start.9 = (f32[2,64,128]{2,1,0:T(8,128)S(1)}, f32[2,64,128]{2,1,0:T(8,128)S(1)}, u32[]{:S(2)}, u32[]{:S(2)}) collective-permute-start(f32[2,64,128]{2,1,0:T(8,128)S(1)} %get-tuple-element.59), channel_id=1, source_target_pairs={{0,1},{1,0},{2,3},{3,2},{4,5},{5,4},{6,7},{7,6},{8,9},{9,8},{10,11... | collective-permute-start | bytes 196616 | tf_op jit(solution)/shard_map/ppermute | solution.py:547
  44.3 7.2 %collective-permute-start.10 = (f32[2,64,128]{2,1,0:T(8,128)S(1)}, f32[2,64,128]{2,1,0:T(8,128)S(1)}, u32[]{:S(2)}, u32[]{:S(2)}) collective-permute-start(f32[2,64,128]{2,1,0:T(8,128)S(1)} %get-tuple-element.61), channel_id=1, source_target_pairs={{1,2},{2,1},{3,4},{4,3},{5,6},{6,5},{7,8},{8,7},{9,10},{10,9},{11,... | collective-permute-start | bytes 196616 | tf_op jit(solution)/shard_map/ppermute | solution.py:546
  45.0 8.1 %collective-permute-start.11 = (f32[2,64,128]{2,1,0:T(8,128)S(1)}, f32[2,64,128]{2,1,0:T(8,128)S(1)}, u32[]{:S(2)}, u32[]{:S(2)}) collective-permute-start(f32[2,64,128]{2,1,0:T(8,128)S(1)} %get-tuple-element.62), channel_id=1, source_target_pairs={{0,1},{1,0},{2,3},{3,2},{4,5},{5,4},{6,7},{7,6},{8,9},{9,8},{10,11... | collective-permute-start | bytes 196616 | tf_op jit(solution)/shard_map/ppermute | solution.py:547
  53.8 3.7 %collective-permute-start.12 = (f32[128,128]{1,0:T(8,128)S(1)}, f32[128,128]{1,0:T(8,128)S(1)}, u32[]{:S(2)}, u32[]{:S(2)}) collective-permute-start(f32[128,128]{1,0:T(8,128)S(1)} %get-tuple-element.65), channel_id=1, source_target_pairs={{0,64},{64,128},{128,192},{192,256},{256,320},{320,384},{384,448},... | collective-permute-start | bytes 196616 | tf_op jit(solution)/shard_map/ppermute | solution.py:19
  56.2 3.7 %collective-permute-start.13 = (f32[128,128]{1,0:T(8,128)S(1)}, f32[128,128]{1,0:T(8,128)S(1)}, u32[]{:S(2)}, u32[]{:S(2)}) collective-permute-start(f32[128,128]{1,0:T(8,128)S(1)} %get-tuple-element.66), channel_id=1, source_target_pairs={{0,448},{64,0},{128,64},{192,128},{256,192},{320,256},{384,320},{4... | collective-permute-start | bytes 196616 | tf_op jit(solution)/shard_map/ppermute | solution.py:19
  60.6 50.8 %collective-permute-start.14 = (f32[2,64,128]{2,1,0:T(8,128)S(1)}, f32[2,64,128]{2,1,0:T(8,128)S(1)}, u32[]{:S(2)}, u32[]{:S(2)}) collective-permute-start(f32[2,64,128]{2,1,0:T(8,128)S(1)} %get-tuple-element.72), channel_id=1, source_target_pairs={{1,2},{2,1},{3,4},{4,3},{5,6},{6,5},{7,8},{8,7},{9,10},{10,9},{11,... | collective-permute-start | bytes 196616 | tf_op jit(solution)/shard_map/ppermute | solution.py:546
  61.2 50.2 %collective-permute-start.15 = (f32[2,64,128]{2,1,0:T(8,128)S(1)}, f32[2,64,128]{2,1,0:T(8,128)S(1)}, u32[]{:S(2)}, u32[]{:S(2)}) collective-permute-start(f32[2,64,128]{2,1,0:T(8,128)S(1)} %get-tuple-element.73), channel_id=1, source_target_pairs={{0,1},{1,0},{2,3},{3,2},{4,5},{5,4},{6,7},{7,6},{8,9},{9,8},{10,11... | collective-permute-start | bytes 196616 | tf_op jit(solution)/shard_map/ppermute | solution.py:547
